TPU v7x, 32 devices: a whole 2x2x4 slice. The times are simulated.
32 devices in a mesh: ctx: 16 (over z, y, x), head: 2 (over core).
Axes of the slice: x: 2, y: 2, z: 4, core: 2. Of those that a mesh axis runs over, the one named last changes fastest.
Arguments:
- queries: bfloat16 [8192, 2048], P('ctx', 'head'), may hold values from -6 to 6
- key_vectors: bfloat16 [8192, 2048], P('ctx', 'head'), may hold values from -6 to 6
- values: bfloat16 [8192, 2048], P('ctx', 'head'), may hold values from -6 to 6
- level_table: float32 [64, 16, 7], P(None, 'head'), may hold values from 0.25 to 2
- weight_index: int32 [8192], P('ctx'), may hold values from 0 to 63
- norm_gain: float32 [2048], P('head'), may hold values from 0.25 to 1.75
- out_weight: bfloat16 [2048, 2048], P('head'), may hold values from -0.125 to 0.125
Outputs:
- mixed_out: bfloat16 [8192, 2048], P('ctx', 'head')
All inputs are finite; a program needn't handle non-finite values.
Results may differ from a plain program's by a relative error of at most 0.01.
Values may be sent and summed in bfloat16 or wider, within the bound.
No kernel may reach another device: no remote copies, remote signals or barrier semaphores. Data moves between devices by JAX's collectives and lax.ppermute only.
A program may use at most 128 MiB of HBM per device.

v0:
```python
import math

import jax
import jax.numpy as jnp
import numpy as np
from jax import lax
from jax.sharding import PartitionSpec as P

STRETCHES_DEV = 4


ROPE_BASE = 500000.0
NORM_EPS = 1e-06


def partner_2(block, axis, apart):
    count = lax.axis_size(axis)
    route = []
    for low in range(count):
        high = low | 1 << apart
        if high != low and high < count:
            route += [(low, high), (high, low)]
    return lax.ppermute(block, axis, route)


def rotate_flat(vectors, positions, head_dim):
    tok_rows, model_width = vectors.shape
    half_dim = head_dim // 2
    frequency = jnp.exp(
        jnp.arange(half_dim, dtype=jnp.float32) * (-2.0 * math.log(ROPE_BASE) / head_dim)
    )
    angles = positions[:, None] * frequency[None, :]
    cosine = jnp.cos(angles)
    sine_part = jnp.sin(angles)
    cosine_full = jnp.concatenate([cosine, cosine], axis=1)
    sine_full = jnp.concatenate([sine_part, sine_part], axis=1)
    rows = jnp.arange(head_dim, dtype=jnp.int32)[:, None]
    cols = jnp.arange(head_dim, dtype=jnp.int32)[None, :]
    upper = (cols < half_dim) & (rows == cols + half_dim)
    lower = (cols >= half_dim) & (rows == cols - half_dim)
    swapper = jnp.where(upper, -1.0, 0.0) + jnp.where(lower, 1.0, 0.0)
    widened = vectors.astype(jnp.float32).reshape(-1, head_dim)
    swapped = jnp.dot(widened, swapper.astype(jnp.float32), precision=lax.Precision.HIGHEST)
    heads_here = model_width // head_dim
    widened = widened.reshape(tok_rows, heads_here, head_dim)
    swapped = swapped.reshape(tok_rows, heads_here, head_dim)
    turned = widened * cosine_full[:, None, :] + swapped * sine_full[:, None, :]
    return turned.astype(jnp.bfloat16)


def level_scale(level_index, stretch_len):
    if level_index == 0:
        return stretch_len ** (-0.5)
    return (2 ** (level_index - 1) * stretch_len) ** (-0.5)


def rounded(matrix):
    return lax.optimization_barrier(matrix.astype(jnp.bfloat16)).astype(jnp.float32)


def local_buckets(states):
    stretch_count = states.shape[0]
    stretch_ids = np.arange(stretch_count)
    result = []
    for bit_index in range(stretch_count.bit_length() - 1):
        grouped = states.reshape(
            (stretch_count >> bit_index, 1 << bit_index) + states.shape[1:]
        ).sum(axis=1)
        source = np.maximum((stretch_ids >> bit_index) - 1, 0)
        present = stretch_ids >> bit_index & 1 == 1
        result.append(jnp.where(jnp.asarray(present)[:, None, None, None], grouped[source], 0.0))
    return result


def local(queries, key_vectors, values, level_table, weight_index, norm_gain, out_weight):
    tok_rows, model_width = queries.shape
    table_rows, heads_here, level_count = level_table.shape
    head_dim = model_width // heads_here
    stretch_len = tok_rows // STRETCHES_DEV
    shard_index = lax.axis_index("ctx")
    positions = (shard_index * tok_rows + jnp.arange(tok_rows, dtype=jnp.int32)).astype(jnp.float32)
    rotated_queries = rotate_flat(queries, positions, head_dim)
    rotated_keys = rotate_flat(key_vectors, positions, head_dim)
    query_stretches = rotated_queries.reshape(STRETCHES_DEV, stretch_len, heads_here, head_dim)
    key_stretches = rotated_keys.reshape(STRETCHES_DEV, stretch_len, heads_here, head_dim)
    value_stretches = values.reshape(STRETCHES_DEV, stretch_len, heads_here, head_dim)
    states = jnp.einsum(
        "cthd,cthe->chde", key_stretches, value_stretches, preferred_element_type=jnp.float32
    )
    shard_state = states.sum(axis=0)
    ctx_bits = lax.axis_size("ctx").bit_length() - 1
    cross_states = []
    running = shard_state
    for bit_index in range(ctx_bits):
        partner = partner_2(running, "ctx", bit_index)
        present = (shard_index >> bit_index & 1).astype(jnp.float32)
        cross_states.append(partner * present)
        running = running + partner
    widened_table = jnp.broadcast_to(
        jnp.transpose(level_table, (0, 2, 1))[:, :, :, None],
        (table_rows, level_count, heads_here, head_dim),
    ).reshape(table_rows, level_count * model_width)
    one_hot = (weight_index[:, None] == jnp.arange(table_rows, dtype=jnp.int32)[None, :]).astype(
        jnp.float32
    )

    def level_weight(level_index):
        block = widened_table[:, level_index * model_width : (level_index + 1) * model_width]
        return jnp.dot(one_hot, block, precision=lax.Precision.HIGHEST)

    scores = jnp.einsum(
        "cthd,cshd->chts", query_stretches, key_stretches, preferred_element_type=jnp.float32
    )
    causal_mask = jnp.tril(jnp.ones((stretch_len, stretch_len), dtype=bool))
    scores = jnp.where(causal_mask, scores, 0.0).astype(jnp.bfloat16)
    level_outs = [
        jnp.einsum(
            "chts,cshe->cthe", scores, value_stretches, preferred_element_type=jnp.float32
        ).reshape(tok_rows, model_width)
    ]
    for bucket in local_buckets(states):
        level_outs.append(
            jnp.einsum(
                "cthd,chde->cthe",
                query_stretches,
                bucket.astype(jnp.bfloat16),
                preferred_element_type=jnp.float32,
            ).reshape(tok_rows, model_width)
        )
    combined = jnp.zeros((tok_rows, model_width), jnp.float32)
    for level_index in range(len(level_outs)):
        combined = (
            combined
            + level_weight(level_index)
            * level_scale(level_index, stretch_len)
            * level_outs[level_index]
        )
    first_cross = len(level_outs)
    for bit_index in range(ctx_bits):
        level_index = first_cross + bit_index
        cross_out = jnp.einsum(
            "thd,hde->the",
            rotated_queries,
            cross_states[bit_index].astype(jnp.bfloat16),
            preferred_element_type=jnp.float32,
        ).reshape(tok_rows, model_width)
        combined = (
            combined + level_weight(level_index) * level_scale(level_index, stretch_len) * cross_out
        )
    per_head = combined.reshape(tok_rows, heads_here, head_dim)
    mean_square = jnp.mean(per_head * per_head, axis=-1, keepdims=True)
    normed = per_head * lax.rsqrt(mean_square + NORM_EPS) * norm_gain.reshape(heads_here, head_dim)
    hidden = normed.astype(jnp.bfloat16).reshape(tok_rows, model_width)
    partial_out = rounded(jnp.dot(hidden, out_weight, preferred_element_type=jnp.float32))
    mixed_out = lax.psum_scatter(
        partial_out.astype(jnp.bfloat16), "head", scatter_dimension=1, tiled=True
    )
    return mixed_out


def solution(mesh):
    return jax.shard_map(
        local,
        mesh=mesh,
        in_specs=(
            P("ctx", "head"),
            P("ctx", "head"),
            P("ctx", "head"),
            P(None, "head", None),
            P("ctx"),
            P("head"),
            P("head", None),
        ),
        out_specs=P("ctx", "head"),
        check_vma=False,
    )
```

profile of v0, /device:TPU:0, one launch (start us, length us, event | category | flops | bytes accessed | tf_op | source)
XLA Modules:
  0.0 176.1 jit_solution(13883548508172002786)
XLA Ops:
  12.6 2.5 %copy.145 = bf16[64,8,8,128]{3,2,1,0:T(8,128)(2,1)} copy(bf16[64,8,8,128]{3,1,2,0:T(8,128)(2,1)} %bitcast.135) | data formatting | bytes 2097152
  19.4 2.4 %convolution_bitcast_fusion = f32[4096,128]{0,1:T(8,128)} fusion(bf16[4096,128]{1,0:T(8,128)(2,1)S(1)} %reshape.151, s32[128]{0:T(128)S(1)} %get-tuple-element.15, s32[128]{0:T(128)S(1)} %get-tuple-element.16, pred[128]{0:T(512)(128)(4,1)S(1)} %get-tuple-element.17, pred[128]{0:T(512)(128)(4,1)S(1)} %get-tuple-element.18), kind=kOutput, calls=%fused_computation.2 | convolution fusion | flops 805421056 | bytes 3147008 | tf_op jit(solution)/shard_map/dot_general | solution.py:43
  21.8 2.9 %copy.110 = f32[4096,128]{1,0:T(8,128)} copy(f32[4096,128]{0,1:T(8,128)} %convolution_bitcast_fusion) | data formatting | bytes 4194304 | tf_op jit(solution)/shard_map/dot_general | solution.py:43
  31.1 2.4 %copy.115 = bf16[4,128,8,128]{1,3,2,0:T(8,128)(2,1)} copy(bf16[4,128,8,128]{3,2,1,0:T(8,128)(2,1)} %get-tuple-element.8) | data formatting | bytes 2097152 | tf_op jit(solution)/shard_map/convert_element_type | solution.py:48
  33.5 4.1 %fusion.92 = (f32[8,128,128]{2,1,0:T(8,128)}, f32[4,8,128,128]{3,2,1,0:T(8,128)}) fusion(bf16[4,128,8,128]{1,3,2,0:T(8,128)(2,1)} %copy.115, bf16[4,128,8,128]{3,2,1,0:T(8,128)(2,1)} %bitcast.114), kind=kOutput, calls=%fused_computation.136 | convolution fusion | flops 134610944 | bytes 4718592 | tf_op jit(solution)/shard_map/cthd,cthe->chde/dot_general | solution.py:87
  39.6 2.9 %collective-permute-start = (f32[8,128,128]{1,2,0:T(8,128)}, f32[8,128,128]{1,2,0:T(8,128)}, u32[]{:S(2)}, u32[]{:S(2)}) collective-permute-start(f32[8,128,128]{1,2,0:T(8,128)} %copy.123), channel_id=1, source_target_pairs={{0,2},{2,0},{4,6},{6,4},{8,10},{10,8},{12,14},{14,12},{16,18},{18,... | collective-permute-start | bytes 1572872 | tf_op jit(solution)/shard_map/ppermute | solution.py:23
  53.3 2.4 %fusion.45 = f32[512,1024]{1,0:T(8,128)} fusion(f32[64,7168]{1,0:T(8,128)S(1)} %bitcast.131, s32[512]{0:T(512)S(1)} %copy-done.11), kind=kOutput, calls=%fused_computation.75 | convolution fusion | flops 402685952 | bytes 2361344 | tf_op jit(solution)/shard_map/dot_general | solution.py:109
  55.7 2.4 %fusion.47 = f32[512,1024]{1,0:T(8,128)} fusion(f32[64,7168]{1,0:T(8,128)S(1)} %bitcast.132, s32[512]{0:T(512)S(1)} %copy-done.11), kind=kOutput, calls=%fused_computation.77 | convolution fusion | flops 402685952 | bytes 2361344 | tf_op jit(solution)/shard_map/dot_general | solution.py:109
  59.2 3.2 %gather_fusion = bf16[4,8,128,128]{3,2,1,0:T(8,128)(2,1)} fusion(f32[4,8,128,128]{3,2,1,0:T(8,128)} %get-tuple-element.14, s32[1024]{0:T(1024)S(1)} %pad_clamp_fusion.1), kind=kCustom, calls=%fused_computation | custom fusion | bytes 2097168 | tf_op jit(solution)/shard_map/gather | solution.py:71
  62.4 2.7 %gather_fusion.1 = bf16[4,8,128,128]{3,2,1,0:T(8,128)(2,1)} fusion(bf16[2,8,128,128]{3,2,1,0:T(8,128)(2,1)} %bitcast_reduce_fusion, s32[1024]{0:T(1024)S(1)} %pad_clamp_fusion), kind=kCustom, calls=%fused_computation.1 | custom fusion | bytes 2097168 | tf_op jit(solution)/shard_map/gather | solution.py:71
  65.1 3.6 %convolution_bitcast_fusion.2 = f32[4,128,8,128]{1,3,2,0:T(8,128)} fusion(bf16[4,8,128,128]{3,2,1,0:T(8,128)(2,1)} %gather_fusion.1, pred[4]{0:T(512)(128)(4,1)S(1)} %copy-done.14, bf16[4,128,8,128]{3,2,1,0:T(8,128)(2,1)S(1)} %get-tuple-element.7), kind=kOutput, calls=%fused_computation.35 | convolution fusion | flops 134742016 | bytes 4194308 | tf_op jit(solution)/shard_map/cthd,chde->cthe/dot_general | solution.py:123
  70.9 3.6 %convolution_bitcast_fusion.4 = f32[4,128,8,128]{3,1,2,0:T(8,128)} fusion(bf16[4,128,8,128]{1,3,2,0:T(8,128)(2,1)} %copy.115, pred[128,128]{1,0:T(8,128)(4,1)S(1)} %iota_compare_fusion.10, bf16[4,128,8,128]{3,2,1,0:T(8,128)(2,1)} %bitcast.115, bf16[4,128,8,128]{3,2,1,0:T(8,128)(2,1)S(1)} %get-tuple-element.7), kind=kOutput, calls=%fused_computation.37 | convolution fusion | flops 269484032 | bytes 5259264 | tf_op jit(solution)/shard_map/chts,cshe->cthe/dot_general | solution.py:117
  79.1 4.1 %copy.114 = f32[4,128,8,128]{3,2,1,0:T(8,128)} copy(f32[4,128,8,128]{3,1,2,0:T(8,128)} %convolution_bitcast_fusion.4) | data formatting | bytes 4194304 | tf_op jit(solution)/shard_map/chts,cshe->cthe/transpose | solution.py:117
  83.2 2.9 %copy.119 = f32[4,128,8,128]{3,2,1,0:T(8,128)} copy(f32[4,128,8,128]{1,3,2,0:T(8,128)} %convolution_bitcast_fusion.3) | data formatting | bytes 4194304 | tf_op jit(solution)/shard_map/cthd,chde->cthe/transpose | solution.py:123
  86.1 2.9 %copy.122 = f32[4,128,8,128]{3,2,1,0:T(8,128)} copy(f32[4,128,8,128]{1,3,2,0:T(8,128)} %convolution_bitcast_fusion.2) | data formatting | bytes 4194304 | tf_op jit(solution)/shard_map/cthd,chde->cthe/transpose | solution.py:123
  94.9 3.3 %fusion.49 = f32[512,1024]{1,0:T(8,128)} fusion(f32[64,7168]{1,0:T(8,128)} %bitcast.133, s32[512]{0:T(512)S(1)} %copy-done.11), kind=kOutput, calls=%fused_computation.79 | convolution fusion | flops 402685952 | bytes 2361344 | tf_op jit(solution)/shard_map/dot_general | solution.py:109
  101.5 5.2 %collective-permute-done.2 = f32[8,128,128]{1,2,0:T(8,128)} collective-permute-done((f32[8,128,128]{1,2,0:T(8,128)}, f32[8,128,128]{1,2,0:T(8,128)}, u32[]{:S(2)}, u32[]{:S(2)}) %collective-permute-start.2) | collective-permute-done | bytes 524320 | tf_op jit(solution)/shard_map/ppermute | solution.py:23
  108.8 2.6 %collective-permute-start.3 = (f32[8,128,128]{1,2,0:T(8,128)}, f32[8,128,128]{1,2,0:T(8,128)}, u32[]{:S(2)}, u32[]{:S(2)}) collective-permute-start(f32[8,128,128]{1,2,0:T(8,128)} %add.113), channel_id=1, source_target_pairs={{0,16},{16,0},{2,18},{18,2},{4,20},{20,4},{6,22},{22,6},{8,24},{24... | collective-permute-start | bytes 1572872 | tf_op jit(solution)/shard_map/ppermute | solution.py:23
  118.1 15.2 %collective-permute-done.3 = f32[8,128,128]{1,2,0:T(8,128)} collective-permute-done((f32[8,128,128]{1,2,0:T(8,128)}, f32[8,128,128]{1,2,0:T(8,128)}, u32[]{:S(2)}, u32[]{:S(2)}) %collective-permute-start.3) | collective-permute-done | bytes 524320 | tf_op jit(solution)/shard_map/ppermute | solution.py:23
  133.4 2.8 %fusion.29 = f32[8,128,512]{2,1,0:T(8,128)} fusion(bf16[512,8,128]{2,1,0:T(8,128)(2,1)S(1)} %fusion.3, f32[8,128,128]{1,2,0:T(8,128)} %collective-permute-done.3, f32[]{:T(128)S(6)} %convert_element_type.82), kind=kOutput, calls=%fused_computation.51 | convolution fusion | flops 134479872 | bytes 3670020 | tf_op jit(solution)/shard_map/thd,hde->the/dot_general | solution.py:141
  136.2 3.1 %copy.141 = f32[512,1024]{1,0:T(8,128)} copy(f32[512,1024]{0,1:T(8,128)} %bitcast.120) | data formatting | bytes 4194304 | tf_op jit(solution)/shard_map/reshape | solution.py:146
  139.3 12.4 %multiply_bitcast_fusion = (f32[64,8,8,128]{3,1,2,0:T(8,128)S(1)}, f32[512,1024]{1,0:T(8,128)}) fusion(f32[512,1024]{1,0:T(8,128)} %copy.141, f32[512,1024]{1,0:T(8,128)S(1)} %copy-done.2, f32[512,1024]{1,0:T(8,128)} %copy.140, f32[512,1024]{1,0:T(8,128)} %fusion.39, f32[512,1024]{1,0:T(8,128)} %copy.139, f32[512,1024]{1,0:T(8,128)} %fusion.41, ...), kind=kLoop, calls=%fused_computation.29 | loop fusion | flops 11010048 | bytes 33554432
  154.4 5.9 %convolution_convert_fusion = bf16[512,2048]{1,0:T(8,128)(2,1)} fusion(bf16[1024,2048]{1,0:T(8,128)(2,1)} %param.19, f32[512,1024]{1,0:T(8,128)S(1)} %copy-done.10, f32[64,8,8,128]{3,2,1,0:T(8,128)S(1)} %bitcast.134, f32[1024]{0:T(1024)S(1)} %copy-done.16), kind=kOutput, calls=%fused_computation.4 | convolution fusion | flops 2150105088 | bytes 10489856 | tf_op jit(solution)/shard_map/dot_general | solution.py:154
  160.3 9.0 %reduce-scatter.2.cloned.1.call-done = bf16[512,1024]{1,0:T(8,128)(2,1)} async-done(((bf16[512,2048]{1,0:T(8,128)(2,1)}), bf16[512,1024]{1,0:T(8,128)(2,1)}) %reduce-scatter.2.cloned.1.call-update) | async-done | bytes 1048592 | tf_op jit(solution)/shard_map/reduce_scatter | solution.py:155
  (88 shorter events, 57.9 us)
Async XLA Ops:
  6.5 2.4 %copy-start.7 = (bf16[512,1024]{1,0:T(8,128)(2,1)S(1)}, bf16[512,1024]{1,0:T(8,128)(2,1)}, u32[]{:S(2)}) copy-start(bf16[512,1024]{1,0:T(8,128)(2,1)} %param.13) | copy-start | bytes 3145732
  6.5 162.7 %reduce-scatter.2.cloned.1.call-start = ((), (), s32[]{:S(2)}) async-start(), calls=%async_computation.1 | async-start | bytes 3145728 | tf_op jit(solution)/shard_map/reduce_scatter | solution.py:155
  9.0 1.6 copy-start.8
  11.0 4.1 %copy-start.9 = (bf16[4096,128]{1,0:T(8,128)(2,1)S(1)}, bf16[4096,128]{1,0:T(8,128)(2,1)}, u32[]{:S(2)}) copy-start(bf16[4096,128]{1,0:T(8,128)(2,1)} %reshape.149) | copy-start | bytes 3145732
  24.7 2.2 %copy-start.3 = (f32[64,8,8,128]{3,1,2,0:T(8,128)S(1)}, f32[64,8,8,128]{3,1,2,0:T(8,128)}, u32[]{:S(2)}) copy-start(f32[64,8,8,128]{3,1,2,0:T(8,128)} %convert_bitcast_fusion) | copy-start | bytes 6291460
  27.0 1.7 copy-start
  27.0 2.3 %copy-start.4 = (f32[4096,128]{1,0:T(8,128)S(1)}, f32[4096,128]{1,0:T(8,128)}, u32[]{:S(2)}) copy-start(f32[4096,128]{1,0:T(8,128)} %copy.110) | copy-start | bytes 6291460
  33.4 9.1 %copy-start.12 = (f32[64,8,7]{0,1,2:T(8,128)S(1)}, f32[64,8,7]{0,1,2:T(8,128)}, u32[]{:S(2)}) copy-start(f32[64,8,7]{0,1,2:T(8,128)} %param.16) | copy-start | bytes 43012
  39.6 34.9 %collective-permute-start = (f32[8,128,128]{1,2,0:T(8,128)}, f32[8,128,128]{1,2,0:T(8,128)}, u32[]{:S(2)}, u32[]{:S(2)}) collective-permute-start(f32[8,128,128]{1,2,0:T(8,128)} %copy.123), channel_id=1, source_target_pairs={{0,2},{2,0},{4,6},{6,4},{8,10},{10,8},{12,14},{14,12},{16,18},{18,... | collective-permute-start | bytes 1572872 | tf_op jit(solution)/shard_map/ppermute | solution.py:23
  43.2 0.7 copy-start.11
  43.6 12.2 %copy-start.5 = (f32[8,8,56,128]{3,1,2,0:T(8,128)}, f32[8,8,56,128]{3,1,2,0:T(8,128)S(1)}, u32[]{:S(2)}) copy-start(f32[8,8,56,128]{3,1,2,0:T(8,128)S(1)} %copy.182) | copy-start | bytes 5505028
  53.3 4.8 %copy-start.15 = (s32[4]{0:T(128)S(1)}, s32[4]{0:T(128)}, u32[]{:S(2)}) copy-start(s32[4]{0:T(128)} %constant.69) | copy-start | bytes 52
  53.3 4.8 %copy-start.1 = (f32[4,8,128,128]{3,2,1,0:T(8,128)S(1)}, f32[4,8,128,128]{3,2,1,0:T(8,128)}, u32[]{:S(2)}) copy-start(f32[4,8,128,128]{3,2,1,0:T(8,128)} %get-tuple-element.14) | copy-start | bytes 6291460
  59.2 5.9 %copy-start.14 = (pred[4]{0:T(512)(128)(4,1)S(1)}, pred[4]{0:T(512)(128)(4,1)}, u32[]{:S(2)}) copy-start(pred[4]{0:T(512)(128)(4,1)} %constant.66.clone) | copy-start | bytes 16
  65.1 3.6 %copy-start.6 = (bf16[4,8,128,128]{3,2,1,0:T(8,128)(2,1)S(1)}, bf16[4,8,128,128]{3,2,1,0:T(8,128)(2,1)}, u32[]{:S(2)}) copy-start(bf16[4,8,128,128]{3,2,1,0:T(8,128)(2,1)} %gather_fusion) | copy-start | bytes 3145732
  65.1 3.6 %copy-start.13 = (pred[4]{0:T(512)(128)(4,1)S(1)}, pred[4]{0:T(512)(128)(4,1)}, u32[]{:S(2)}) copy-start(pred[4]{0:T(512)(128)(4,1)} %constant.63.clone) | copy-start | bytes 16
  76.6 14.6 %collective-permute-start.1 = (f32[8,128,128]{1,2,0:T(8,128)}, f32[8,128,128]{1,2,0:T(8,128)}, u32[]{:S(2)}, u32[]{:S(2)}) collective-permute-start(f32[8,128,128]{1,2,0:T(8,128)} %add.109), channel_id=1, source_target_pairs={{0,4},{4,0},{2,6},{6,2},{8,12},{12,8},{10,14},{14,10},{16,20},{20,... | collective-permute-start | bytes 1572872 | tf_op jit(solution)/shard_map/ppermute | solution.py:23
  93.3 13.4 %collective-permute-start.2 = (f32[8,128,128]{1,2,0:T(8,128)}, f32[8,128,128]{1,2,0:T(8,128)}, u32[]{:S(2)}, u32[]{:S(2)}) collective-permute-start(f32[8,128,128]{1,2,0:T(8,128)} %add.111), channel_id=1, source_target_pairs={{0,8},{8,0},{2,10},{10,2},{4,12},{12,4},{6,14},{14,6},{16,24},{24,... | collective-permute-start | bytes 1572872 | tf_op jit(solution)/shard_map/ppermute | solution.py:23
  108.8 24.6 %collective-permute-start.3 = (f32[8,128,128]{1,2,0:T(8,128)}, f32[8,128,128]{1,2,0:T(8,128)}, u32[]{:S(2)}, u32[]{:S(2)}) collective-permute-start(f32[8,128,128]{1,2,0:T(8,128)} %add.113), channel_id=1, source_target_pairs={{0,16},{16,0},{2,18},{18,2},{4,20},{20,4},{6,22},{22,6},{8,24},{24... | collective-permute-start | bytes 1572872 | tf_op jit(solution)/shard_map/ppermute | solution.py:23
  136.2 3.1 %copy-start.2 = (f32[512,1024]{1,0:T(8,128)S(1)}, f32[512,1024]{1,0:T(8,128)}, u32[]{:S(2)}) copy-start(f32[512,1024]{1,0:T(8,128)} %fusion.37) | copy-start | bytes 6291460
  152.1 1.5 copy-start.16
  152.8 1.6 copy-start.10
Sparse Core Ops, SparseCore 0:
  160.4 8.8 reduce-scatter.1
where the time goes:
time: 177 us; the launch traced here: 176 us
  matrix products  49 us (28%)
  local copies, waits for them, and re-layouts  45.9 us (26%)
  waiting for transfers between devices  29.5 us (17%)
  other arithmetic  29.4 us (17%)
  between operations  13.7 us (8%)
  starting transfers between devices  8.63 us (5%)
    ppermute x4, waiting for transfers between devices, partner_2(): return lax.ppermute(block, axis, route)  20.4 us
    dot_general x7, matrix products, level_weight(): return jnp.dot(one_hot, block, precision=lax.Precision.HIGHEST)  17.5 us
    unnamed x3, other arithmetic  15.5 us
    reduce_scatter x1, waiting for transfers between devices, local(): lax.psum_scatter(partial_out.astype(jnp.bfloat16), 'head', scatter_dimens...  9.01 us
    reshape x4, local copies, waits for them, and re-layouts, local(): cross_out = jnp.einsum('thd,hde->the', rotated_queries, cross_states[bit_...  8.68 us
    ppermute x4, starting transfers between devices, partner_2(): return lax.ppermute(block, axis, route)  8.62 us
    unnamed x39, local copies, waits for them, and re-layouts  7.78 us
    dot_general x4, matrix products, local(): jnp.einsum('thd,hde->the', rotated_queries, cross_states[bit_index].astyp...  7.33 us
  transfers between devices with their start and end apart: 5, of which 3 were waited for; matrix products, arithmetic and copies ran while one was open for 33% of the time, Pallas kernels for 0%

commit v1 on v0

v1 whole, which is shorter than its diff:
```python
import functools
import math

import jax
import jax.numpy as jnp
import numpy as np
from jax import lax
from jax.experimental import pallas as pl
from jax.experimental.pallas import tpu as pltpu
from jax.sharding import PartitionSpec as P

STRETCHES_DEV = 4
ROPE_BASE = 500000.0
NORM_EPS = 1e-06
MIB = 1 << 20

F32 = jnp.float32
BF16 = jnp.bfloat16


def angle_tables(positions, head_dim):
    half_dim = head_dim // 2
    frequency = np.exp(np.arange(half_dim) * (-2.0 * math.log(ROPE_BASE) / head_dim))
    angles = np.asarray(positions, np.float64)[:, None] * frequency[None, :]
    cosine, sine = np.cos(angles), np.sin(angles)
    return (
        np.concatenate([cosine, cosine], axis=1).astype(np.float32),
        np.concatenate([-sine, sine], axis=1).astype(np.float32),
    )


def level_scale(level_index, stretch_len):
    if level_index == 0:
        return stretch_len ** (-0.5)
    return (2 ** (level_index - 1) * stretch_len) ** (-0.5)


def fill_angles(row_cos_ref, row_sin_ref, base_ref, cos_ref, sin_ref):
    base_cos = base_ref[0:1, :]
    base_sin = base_ref[1:2, :]
    row_cos = row_cos_ref[...]
    row_sin = row_sin_ref[...]
    cos_ref[...] = base_cos * row_cos - base_sin * row_sin
    sin_ref[...] = base_sin * row_cos + base_cos * row_sin


def rotated(vectors, cosine, sine):
    wide = vectors.astype(F32)
    half = wide.shape[-1] // 2
    return (wide * cosine + pltpu.roll(wide, half, 1) * sine).astype(BF16)


def dot_tn(a, b):
    return lax.dot_general(a, b, (((0,), (0,)), ((), ())), preferred_element_type=F32)


def dot_nt(a, b):
    return lax.dot_general(a, b, (((1,), (1,)), ((), ())), preferred_element_type=F32)


def dot_nn(a, b):
    return jnp.dot(a, b, preferred_element_type=F32)


def local_plan(stretches):
    plan = []
    for stretch in range(stretches):
        row = []
        for bit in range(stretches.bit_length() - 1):
            if stretch >> bit & 1:
                end = stretch >> bit << bit
                row.append((bit, tuple(range(end - (1 << bit), end))))
        plan.append(row)
    return plan


def state_kernel(
    heads_step,
    head_dim,
    row_cos_ref,
    row_sin_ref,
    base_ref,
    key_ref,
    value_ref,
    key_out,
    total_out,
    bucket_out,
    cos_ref,
    sin_ref,
):
    @pl.when(pl.program_id(0) == 0)
    def _():
        fill_angles(row_cos_ref, row_sin_ref, base_ref, cos_ref, sin_ref)

    tok_rows = key_ref.shape[0]
    stretch_len = tok_rows // STRETCHES_DEV
    groups = bucket_groups()
    for head in range(heads_step):
        cols = slice(head * head_dim, (head + 1) * head_dim)
        states = []
        for stretch in range(STRETCHES_DEV):
            rows = slice(stretch * stretch_len, (stretch + 1) * stretch_len)
            turned = rotated(key_ref[rows, cols], cos_ref[rows, :], sin_ref[rows, :])
            key_out[rows, cols] = turned
            states.append(dot_tn(turned, value_ref[rows, cols]))
        for spot, members in enumerate(groups):
            bucket_out[head, spot] = sum(states[m] for m in members).astype(BF16)
        total_out[head] = sum(states).astype(BF16)


def bucket_groups():
    groups = []
    for row in local_plan(STRETCHES_DEV):
        for _, members in row:
            if members not in groups:
                groups.append(members)
    return groups


def fill_one_hot(index_ref, one_hot_ref):
    table_rows = one_hot_ref.shape[0] // 3
    rows = lax.broadcasted_iota(jnp.int32, one_hot_ref.shape, 0)
    rows = lax.rem(rows, table_rows)
    one_hot_ref[...] = jnp.where(rows == index_ref[...], 1.0, 0.0).astype(BF16)


def level_weights(one_hot_ref, table):
    high = table.astype(BF16)
    rest = table - high.astype(F32)
    middle = rest.astype(BF16)
    low = (rest - middle.astype(F32)).astype(BF16)
    return dot_tn(one_hot_ref[...], jnp.concatenate([high, middle, low], axis=0))


def local_kernel(
    heads_step,
    head_dim,
    row_cos_ref,
    row_sin_ref,
    base_ref,
    index_ref,
    table_ref,
    query_ref,
    key_ref,
    value_ref,
    bucket_ref,
    query_out,
    combined_out,
    weight_out,
    cos_ref,
    sin_ref,
    one_hot_ref,
):
    @pl.when(pl.program_id(0) == 0)
    def _():
        fill_angles(row_cos_ref, row_sin_ref, base_ref, cos_ref, sin_ref)
        fill_one_hot(index_ref, one_hot_ref)

    tok_rows = key_ref.shape[0]
    stretch_len = tok_rows // STRETCHES_DEV
    groups = bucket_groups()
    shape = (stretch_len, stretch_len)
    causal = lax.broadcasted_iota(jnp.int32, shape, 0) >= lax.broadcasted_iota(jnp.int32, shape, 1)
    for head in range(heads_step):
        cols = slice(head * head_dim, (head + 1) * head_dim)
        weights = level_weights(one_hot_ref, table_ref[head])
        weight_out[head] = weights
        for stretch, row in enumerate(local_plan(STRETCHES_DEV)):
            rows = slice(stretch * stretch_len, (stretch + 1) * stretch_len)
            turned = rotated(query_ref[rows, cols], cos_ref[rows, :], sin_ref[rows, :])
            query_out[rows, cols] = turned
            scores = jnp.where(causal, dot_nt(turned, key_ref[rows, cols]), 0.0).astype(BF16)
            total = weights[rows, 0:1] * dot_nn(scores, value_ref[rows, cols])
            for bit, members in row:
                read = dot_nn(turned, bucket_ref[head, groups.index(members)])
                total = total + weights[rows, bit + 1 : bit + 2] * read
            combined_out[rows, cols] = total


def cross_kernel(
    heads_step,
    head_dim,
    first_level,
    levels,
    present_ref,
    combined_ref,
    query_ref,
    weight_ref,
    gain_ref,
    *refs,
):
    bucket_refs = refs[:levels]
    hidden_out = refs[levels]
    for head in range(heads_step):
        cols = slice(head * head_dim, (head + 1) * head_dim)
        total = combined_ref[:, cols]
        queries = query_ref[:, cols]
        for level in range(levels):
            spot = first_level + level
            weight = weight_ref[head, :, spot : spot + 1] * present_ref[level]
            total = total + weight * dot_nn(queries, bucket_refs[level][head])
        mean_square = jnp.mean(total * total, axis=-1, keepdims=True)
        normed = total * lax.rsqrt(mean_square + NORM_EPS) * gain_ref[:, cols]
        hidden_out[:, cols] = normed.astype(BF16)


def project_kernel(place_ref, hidden_ref, weight_ref, out_ref):
    out_ref[...] = dot_nn(hidden_ref[...], weight_ref[...])


def project_add_kernel(place_ref, hidden_ref, weight_ref, part_ref, out_ref):
    out_ref[...] = (part_ref[...] + dot_nn(hidden_ref[...], weight_ref[...])).astype(BF16)


def cost(flops, size):
    return pl.CostEstimate(flops=int(flops), bytes_accessed=int(size), transcendentals=0)


def local(queries, key_vectors, values, level_table, weight_index, norm_gain, out_weight):
    tok_rows, model_width = queries.shape
    table_rows, heads_here, level_count = level_table.shape
    head_dim = model_width // heads_here
    stretch_len = tok_rows // STRETCHES_DEV
    n_ctx = lax.axis_size("ctx")
    n_head = lax.axis_size("head")
    ctx_bits = n_ctx.bit_length() - 1
    shard_index = lax.axis_index("ctx")
    head_index = lax.axis_index("head")
    group_count = len(bucket_groups())

    other_weight = lax.ppermute(out_weight, "head", [(i, i ^ 1) for i in range(n_head)])

    row_cos, row_sin = angle_tables(np.arange(tok_rows), head_dim)
    base_cos, base_sin = angle_tables(np.arange(n_ctx) * tok_rows, head_dim)
    base_all = jnp.asarray(np.stack([base_cos, base_sin], axis=1))
    base = lax.dynamic_index_in_dim(base_all, shard_index, 0, keepdims=False)

    step = 2
    steps = heads_here // step
    width = step * head_dim
    wide = pl.BlockSpec((tok_rows, width), lambda h: (0, h))
    table_spec = pl.BlockSpec((tok_rows, head_dim), lambda h: (0, 0))
    base_spec = pl.BlockSpec((2, head_dim), lambda h: (0, 0))
    state_spec = pl.BlockSpec((step, head_dim, head_dim), lambda h: (h, 0, 0))
    bucket_spec = pl.BlockSpec((step, group_count, head_dim, head_dim), lambda h: (h, 0, 0, 0))
    angle_scratch = [pltpu.VMEM((tok_rows, head_dim), F32)] * 2
    params = pltpu.CompilerParams(
        dimension_semantics=("arbitrary",), vmem_limit_bytes=32 * MIB
    )
    head_macs = tok_rows * head_dim * head_dim * heads_here
    block_bytes = tok_rows * model_width * 2

    keys, shard_state, local_states = pl.pallas_call(
        functools.partial(state_kernel, step, head_dim),
        grid=(steps,),
        in_specs=[table_spec, table_spec, base_spec, wide, wide],
        out_specs=[wide, state_spec, bucket_spec],
        out_shape=[
            jax.ShapeDtypeStruct((tok_rows, model_width), BF16),
            jax.ShapeDtypeStruct((heads_here, head_dim, head_dim), BF16),
            jax.ShapeDtypeStruct((heads_here, group_count, head_dim, head_dim), BF16),
        ],
        scratch_shapes=angle_scratch,
        compiler_params=params,
        cost_estimate=cost(2 * head_macs, 4 * block_bytes),
        name="states",
    )(row_cos, row_sin, base, key_vectors, values)

    scales = np.array([level_scale(i, stretch_len) for i in range(level_count)], np.float32)
    table = jnp.transpose(level_table, (1, 0, 2)) * scales

    rotated_queries, combined, weights = pl.pallas_call(
        functools.partial(local_kernel, step, head_dim),
        grid=(steps,),
        in_specs=[
            table_spec,
            table_spec,
            base_spec,
            pl.BlockSpec((1, tok_rows), lambda h: (0, 0)),
            pl.BlockSpec((step, table_rows, level_count), lambda h: (h, 0, 0)),
            wide,
            wide,
            wide,
            bucket_spec,
        ],
        out_specs=[
            wide,
            wide,
            pl.BlockSpec((step, tok_rows, level_count), lambda h: (h, 0, 0)),
        ],
        out_shape=[
            jax.ShapeDtypeStruct((tok_rows, model_width), BF16),
            jax.ShapeDtypeStruct((tok_rows, model_width), F32),
            jax.ShapeDtypeStruct((heads_here, tok_rows, level_count), F32),
        ],
        scratch_shapes=angle_scratch + [pltpu.VMEM((3 * table_rows, tok_rows), BF16)],
        compiler_params=params,
        cost_estimate=cost(8 * head_macs, 8 * block_bytes),
        name="local_levels",
    )(
        row_cos,
        row_sin,
        base,
        weight_index.reshape(1, tok_rows),
        table,
        queries,
        keys,
        values,
        local_states,
    )

    buckets = []
    running = shard_state
    for bit in range(ctx_bits):
        partner = lax.ppermute(running, "ctx", [(i, i ^ (1 << bit)) for i in range(n_ctx)])
        buckets.append(partner)
        running = (running.astype(F32) + partner.astype(F32)).astype(BF16)
    present = (shard_index >> jnp.arange(ctx_bits, dtype=jnp.int32) & 1).astype(F32)

    first_cross = level_count - ctx_bits

    hidden = pl.pallas_call(
        functools.partial(cross_kernel, step, head_dim, first_cross, ctx_bits),
        grid=(steps,),
        in_specs=[
            pl.BlockSpec(memory_space=pltpu.SMEM),
            wide,
            wide,
            pl.BlockSpec((step, tok_rows, level_count), lambda h: (h, 0, 0)),
            pl.BlockSpec((1, width), lambda h: (0, h)),
        ]
        + [state_spec] * ctx_bits,
        out_specs=wide,
        out_shape=jax.ShapeDtypeStruct((tok_rows, model_width), BF16),
        compiler_params=params,
        cost_estimate=cost(2 * ctx_bits * head_macs, 6 * block_bytes),
        name="cross_levels",
    )(present, combined, rotated_queries, weights, norm_gain.reshape(1, model_width), *buckets)

    other_hidden = lax.ppermute(hidden, "head", [(i, i ^ 1) for i in range(n_head)])

    out_cols = out_weight.shape[1] // n_head
    tile = min(512, out_cols)
    tiles = out_cols // tile
    place = (head_index * tiles).astype(jnp.int32).reshape(1)
    hidden_spec = pl.BlockSpec((tok_rows, model_width), lambda n, place: (0, 0))
    weight_spec = pl.BlockSpec((model_width, tile), lambda n, place: (0, place[0] + n))
    out_spec = pl.BlockSpec((tok_rows, tile), lambda n, place: (0, n))
    matmul_flops = 2 * tok_rows * model_width * out_cols

    own_part = pl.pallas_call(
        project_kernel,
        grid_spec=pltpu.PrefetchScalarGridSpec(
            num_scalar_prefetch=1,
            grid=(tiles,),
            in_specs=[hidden_spec, weight_spec],
            out_specs=out_spec,
        ),
        out_shape=jax.ShapeDtypeStruct((tok_rows, out_cols), F32),
        compiler_params=params,
        cost_estimate=cost(matmul_flops, 8 * MIB),
        name="own_group",
    )(place, hidden, out_weight)

    return pl.pallas_call(
        project_add_kernel,
        grid_spec=pltpu.PrefetchScalarGridSpec(
            num_scalar_prefetch=1,
            grid=(tiles,),
            in_specs=[hidden_spec, weight_spec, out_spec],
            out_specs=out_spec,
        ),
        out_shape=jax.ShapeDtypeStruct((tok_rows, out_cols), BF16),
        compiler_params=params,
        cost_estimate=cost(matmul_flops, 8 * MIB),
        name="other_group",
    )(place, other_hidden, other_weight, own_part)


def solution(mesh):
    return jax.shard_map(
        local,
        mesh=mesh,
        in_specs=(
            P("ctx", "head"),
            P("ctx", "head"),
            P("ctx", "head"),
            P(None, "head", None),
            P("ctx"),
            P("head"),
            P("head", None),
        ),
        out_specs=P("ctx", "head"),
        check_vma=False,
    )
```

time: 177 us -> 61.8 us (0.35)
  matrix products: 49 us -> 0 us
  local copies, waits for them, and re-layouts: 45.9 us -> 13.3 us
  other arithmetic: 29.4 us -> 1 us
  Pallas kernels: 0 us -> 18.8 us
  between operations: 13.7 us -> 0.17 us
  waiting for transfers between devices: 29.5 us -> 19.2 us
    dot_general x18 -> x0, matrix products: 49 us -> none  [the longest x7 17.5 us: level_weight(): return jnp.dot(one_hot, block, precision=lax.Precision.HIGHEST)]
    pallas_call x0 -> x5, Pallas kernels: none -> 18.8 us  [the longest x1 6.59 us: local(): pl.pallas_call(functools.partial(local_kernel, step, head_dim), grid=(ste...]
    unnamed x3 -> x0, other arithmetic: 15.5 us -> none
    reshape x6 -> x0, local copies, waits for them, and re-layouts: 11.5 us -> none  [the longest x4 8.68 us: local(): cross_out = jnp.einsum('thd,hde->the', rotated_queries, cross_states[bit_...]
    transpose x4 -> x0, local copies, waits for them, and re-layouts: 10.1 us -> none  [the longest x2 5.79 us: local(): jnp.einsum('cthd,chde->cthe', query_stretches, bucket.astype(jnp.bfloat16...]
    reduce_scatter x1 -> x0, waiting for transfers between devices: 9.01 us -> none  [local(): lax.psum_scatter(partial_out.astype(jnp.bfloat16), 'head', scatter_dimens...]
    add x3 -> x0, other arithmetic: 6.15 us -> none  [local(): running = running + partner]
    gather x2 -> x0, local copies, waits for them, and re-layouts: 5.92 us -> none  [local_buckets(): grouped[source]]
  transfers between devices with their start and end apart: 5 -> 6, of which waited for: 3 -> 4; matrix products, arithmetic and copies ran while one was open for 33% -> 4% of each run, Pallas kernels for 0% -> 25%
where the time goes in v1:
time: 61.8 us; the launch traced here: 61.2 us
  waiting for transfers between devices  19.2 us (31%)
  Pallas kernels  18.8 us (30%)
  local copies, waits for them, and re-layouts  13.3 us (22%)
  starting transfers between devices  8.87 us (14%)
  other arithmetic  1 us (2%)
    ppermute x4, waiting for transfers between devices, local(): lax.ppermute(running, 'ctx', [(i, i ^ 1 << bit) for i in range(n_ctx)])  19.1 us
    unnamed x44, local copies, waits for them, and re-layouts  11.7 us
    ppermute x4, starting transfers between devices, local(): lax.ppermute(running, 'ctx', [(i, i ^ 1 << bit) for i in range(n_ctx)])  8.35 us
    pallas_call x1, Pallas kernels, local(): pl.pallas_call(functools.partial(local_kernel, step, head_dim), grid=(ste...  6.59 us
    pallas_call x1, Pallas kernels, local(): pl.pallas_call(functools.partial(cross_kernel, step, head_dim, first_cros...  4.73 us
    pallas_call x1, Pallas kernels, local(): pl.pallas_call(project_add_kernel, grid_spec=pltpu.PrefetchScalarGridSpec...  3.48 us
    pallas_call x1, Pallas kernels, local(): pl.pallas_call(functools.partial(state_kernel, step, head_dim), grid=(ste...  2.23 us
    pallas_call x1, Pallas kernels, local(): pl.pallas_call(project_kernel, grid_spec=pltpu.PrefetchScalarGridSpec(num...  1.74 us
  transfers between devices with their start and end apart: 6, of which 4 were waited for; matrix products, arithmetic and copies ran while one was open for 4% of the time, Pallas kernels for 25%

profile of v1, /device:TPU:0, one launch (start us, length us, event | category | flops | bytes accessed | tf_op | source)
XLA Modules:
  0.0 61.2 jit_solution(302500211029207869)
XLA Ops:
  1.1 1.2 %copy-done = bf16[512,1024]{1,0:T(8,128)(2,1)S(1)} copy-done((bf16[512,1024]{1,0:T(8,128)(2,1)S(1)}, bf16[512,1024]{1,0:T(8,128)(2,1)}, u32[]{:S(2)}) %copy-start) | copy-done | bytes 1048600
  2.4 1.2 %copy-done.3 = bf16[512,1024]{1,0:T(8,128)(2,1)S(1)} copy-done((bf16[512,1024]{1,0:T(8,128)(2,1)S(1)}, bf16[512,1024]{1,0:T(8,128)(2,1)}, u32[]{:S(2)}) %copy-start.3) | copy-done | bytes 1048600
  3.6 0.9 %copy-done.5 = f32[512,128]{1,0:T(8,128)S(1)} copy-done((f32[512,128]{1,0:T(8,128)S(1)}, f32[512,128]{1,0:T(8,128)}, u32[]{:S(2)}) %copy-start.5) | copy-done | bytes 262168
  4.5 0.9 %copy-done.7 = f32[512,128]{1,0:T(8,128)S(1)} copy-done((f32[512,128]{1,0:T(8,128)S(1)}, f32[512,128]{1,0:T(8,128)}, u32[]{:S(2)}) %copy-start.7) | copy-done | bytes 262168
  5.5 2.2 %states.1 = (bf16[512,1024]{1,0:T(8,128)(2,1)S(1)}, bf16[8,128,128]{2,1,0:T(8,128)(2,1)S(1)}, bf16[8,3,128,128]{3,2,1,0:T(8,128)(2,1)S(1)}) custom-call(f32[512,128]{1,0:T(8,128)S(1)} %copy-done.5, f32[512,128]{1,0:T(8,128)S(1)} %copy-done.7, f32[2,128]{1,0:T(2,128)S(1)} %dynamic-slice_bitcast_fusion.base_ref, bf16[512,1024]{1,0:T(8,128)(2,1)S(1)} %copy-done.3, ...), custom_call_target="tpu_custom_call" | custom-call | flops 134217728 | bytes 4194304 | tf_op jit(solution)/shard_map/states/pallas_call | solution.py:253
  7.8 2.6 %collective-permute-start = (bf16[8,128,128]{2,1,0:T(8,128)(2,1)S(1)}, bf16[8,128,128]{2,1,0:T(8,128)(2,1)S(1)}, u32[]{:S(2)}, u32[]{:S(2)}) collective-permute-start(bf16[8,128,128]{2,1,0:T(8,128)(2,1)S(1)} %get-tuple-element.16), channel_id=1, source_target_pairs={{0,2},{2,0},{4,6},{6,4},{8,10},{10,8},{12,14},{14,12},{16,18},{18,... | collective-permute-start | bytes 786440 | tf_op jit(solution)/shard_map/ppermute | solution.py:315
  10.3 7.0 %collective-permute-done.refs_0_ = bf16[8,128,128]{2,1,0:T(8,128)(2,1)S(1)} collective-permute-done((bf16[8,128,128]{2,1,0:T(8,128)(2,1)S(1)}, bf16[8,128,128]{2,1,0:T(8,128)(2,1)S(1)}, u32[]{:S(2)}, u32[]{:S(2)}) %collective-permute-start) | collective-permute-done | bytes 262176 | tf_op jit(solution)/shard_map/ppermute | solution.py:315
  18.1 1.8 %collective-permute-start.1 = (bf16[8,128,128]{2,1,0:T(8,128)(2,1)S(1)}, bf16[8,128,128]{2,1,0:T(8,128)(2,1)S(1)}, u32[]{:S(2)}, u32[]{:S(2)}) collective-permute-start(bf16[8,128,128]{2,1,0:T(8,128)(2,1)S(1)} %add_convert_fusion.2), channel_id=1, source_target_pairs={{0,4},{2,6},{4,0},{6,2},{8,12},{10,14},{12,8},{14,10},{16,20},{18,... | collective-permute-start | bytes 786440 | tf_op jit(solution)/shard_map/ppermute | solution.py:315
  19.8 6.4 %collective-permute-done.1.refs_1_ = bf16[8,128,128]{2,1,0:T(8,128)(2,1)S(1)} collective-permute-done((bf16[8,128,128]{2,1,0:T(8,128)(2,1)S(1)}, bf16[8,128,128]{2,1,0:T(8,128)(2,1)S(1)}, u32[]{:S(2)}, u32[]{:S(2)}) %collective-permute-start.1) | collective-permute-done | bytes 262176 | tf_op jit(solution)/shard_map/ppermute | solution.py:315
  26.3 0.7 %copy-done.11 = bf16[8,128,128]{2,1,0:T(8,128)(2,1)} copy-done((bf16[8,128,128]{2,1,0:T(8,128)(2,1)}, bf16[8,128,128]{2,1,0:T(8,128)(2,1)S(1)}, u32[]{:S(2)}) %copy-start.11) | copy-done | bytes 262168
  27.0 1.6 %collective-permute-start.2 = (bf16[8,128,128]{2,1,0:T(8,128)(2,1)S(1)}, bf16[8,128,128]{2,1,0:T(8,128)(2,1)S(1)}, u32[]{:S(2)}, u32[]{:S(2)}) collective-permute-start(bf16[8,128,128]{2,1,0:T(8,128)(2,1)S(1)} %add_convert_fusion.1), channel_id=1, source_target_pairs={{0,8},{2,10},{4,12},{6,14},{8,0},{10,2},{12,4},{14,6},{16,24},{18,... | collective-permute-start | bytes 786440 | tf_op jit(solution)/shard_map/ppermute | solution.py:315
  28.6 5.7 %collective-permute-done.2.refs_2_ = bf16[8,128,128]{2,1,0:T(8,128)(2,1)S(1)} collective-permute-done((bf16[8,128,128]{2,1,0:T(8,128)(2,1)S(1)}, bf16[8,128,128]{2,1,0:T(8,128)(2,1)S(1)}, u32[]{:S(2)}, u32[]{:S(2)}) %collective-permute-start.2) | collective-permute-done | bytes 262176 | tf_op jit(solution)/shard_map/ppermute | solution.py:315
  34.3 0.8 %add_convert_fusion = bf16[8,128,128]{2,1,0:T(8,128)(2,1)} fusion(bf16[8,128,128]{2,1,0:T(8,128)(2,1)S(1)} %collective-permute-done.2.refs_2_, bf16[8,128,128]{2,1,0:T(8,128)(2,1)S(1)} %add_convert_fusion.1), kind=kLoop, calls=%fused_computation | loop fusion | flops 524288 | bytes 786432 | tf_op jit(solution)/shard_map/convert_element_type | solution.py:317
  35.1 0.7 %copy-done.13 = bf16[8,128,128]{2,1,0:T(8,128)(2,1)} copy-done((bf16[8,128,128]{2,1,0:T(8,128)(2,1)}, bf16[8,128,128]{2,1,0:T(8,128)(2,1)S(1)}, u32[]{:S(2)}) %copy-start.13) | copy-done | bytes 262168
  35.8 2.4 %collective-permute-start.3 = (bf16[8,128,128]{2,1,0:T(8,128)(2,1)}, bf16[8,128,128]{2,1,0:T(8,128)(2,1)}, u32[]{:S(2)}, u32[]{:S(2)}) collective-permute-start(bf16[8,128,128]{2,1,0:T(8,128)(2,1)} %add_convert_fusion), channel_id=1, source_target_pairs={{0,16},{2,18},{4,20},{6,22},{8,24},{10,26},{12,28},{14,30},{16,0},... | collective-permute-start | bytes 786440 | tf_op jit(solution)/shard_map/ppermute | solution.py:315
  38.3 0.9 %copy.14 = f32[64,8,7]{2,0,1:T(8,128)} copy(f32[64,8,7]{0,1,2:T(8,128)S(1)} %broadcast_multiply_fusion) | data formatting | bytes 28672 | tf_op jit(solution)/shard_map/mul | solution.py:270
  39.2 0.9 %copy-done.8 = f32[512,128]{1,0:T(8,128)S(1)} copy-done((f32[512,128]{1,0:T(8,128)S(1)}, f32[512,128]{1,0:T(8,128)}, u32[]{:S(2)}) %copy-start.8) | copy-done | bytes 262168
  40.1 0.9 %copy-done.15 = f32[64,8,7]{2,0,1:T(8,128)S(1)} copy-done((f32[64,8,7]{2,0,1:T(8,128)S(1)}, f32[64,8,7]{2,0,1:T(8,128)}, u32[]{:S(2)}) %copy-start.15) | copy-done | bytes 14360
  41.1 1.1 %copy-done.17 = bf16[8,3,128,128]{3,2,1,0:T(8,128)(2,1)S(1)} copy-done((bf16[8,3,128,128]{3,2,1,0:T(8,128)(2,1)S(1)}, bf16[8,3,128,128]{3,2,1,0:T(8,128)(2,1)}, u32[]{:S(2)}) %copy-start.17) | copy-done | bytes 786456
  42.2 6.6 %local_levels.1 = (bf16[512,1024]{1,0:T(8,128)(2,1)S(1)}, f32[512,1024]{1,0:T(8,128)S(1)}, f32[8,512,7]{2,1,0:T(8,128)S(1)}) custom-call(f32[512,128]{1,0:T(8,128)S(1)} %copy-done.6, f32[512,128]{1,0:T(8,128)S(1)} %copy-done.8, f32[2,128]{1,0:T(2,128)S(1)} %dynamic-slice_bitcast_fusion.base_ref, s32[1,512]{1,0:T(1,128)S(1)} %bitcast.8, ...), custom_call_target="tpu_custom_call" | custom-call | flops 536870912 | bytes 8388608 | tf_op jit(solution)/shard_map/local_levels/pallas_call | solution.py:272
  49.0 4.7 %cross_levels.1.hidden_ref = bf16[512,1024]{1,0:T(8,128)(2,1)S(1)} custom-call(f32[4]{0:T(128)S(1)} %and_convert_fusion.present_ref, f32[512,1024]{1,0:T(8,128)S(1)} %get-tuple-element.13.combined_ref, bf16[512,1024]{1,0:T(8,128)(2,1)S(1)} %get-tuple-element.14.query_ref, f32[8,512,7]{2,1,0:T(8,128)S(1)} %get-tuple-element.15.weight_ref, ...), custom_call_target="tpu_custom_call" | custom-call | flops 536870912 | bytes 6291456 | tf_op jit(solution)/shard_map/cross_levels/pallas_call | solution.py:322
  53.8 2.2 %copy-done.2 = bf16[1024,2048]{1,0:T(8,128)(2,1)S(1)} copy-done((bf16[1024,2048]{1,0:T(8,128)(2,1)S(1)}, bf16[1024,2048]{1,0:T(8,128)(2,1)}, u32[]{:S(2)}) %copy-start.2) | copy-done | bytes 4194328
  56.0 1.7 %own_group.1.part_ref = f32[512,1024]{1,0:T(8,128)S(1)} custom-call(s32[1]{0:T(128)} %bitcast.place_ref, bf16[512,1024]{1,0:T(8,128)(2,1)S(1)} %cross_levels.1.hidden_ref, bf16[1024,2048]{1,0:T(8,128)(2,1)S(1)} %copy-done.2), custom_call_target="tpu_custom_call" | custom-call | flops 1073741824 | bytes 8388608 | tf_op jit(solution)/shard_map/own_group/pallas_call | solution.py:351
  57.8 3.5 %other_group.1 = bf16[512,1024]{1,0:T(8,128)(2,1)} custom-call(s32[1]{0:T(128)} %bitcast.place_ref, bf16[512,1024]{1,0:T(8,128)(2,1)S(1)} %collective-permute-done.4.hidden_ref, bf16[1024,2048]{1,0:T(8,128)(2,1)} %collective-permute-done.5.weight_ref, f32[512,1024]{1,0:T(8,128)S(1)} %own_group.1.part_ref), custom_call_target="tpu_custom_call" | custom-call | flops 1073741824 | bytes 8388608 | tf_op jit(solution)/shard_map/other_group/pallas_call | solution.py:365
  (44 shorter events, 2.3 us)
Async XLA Ops:
  0.0 57.8 %collective-permute-start.5 = (bf16[1024,2048]{1,0:T(8,128)(2,1)}, bf16[1024,2048]{1,0:T(8,128)(2,1)}, u32[]{:S(2)}, u32[]{:S(2)}) collective-permute-start(bf16[1024,2048]{1,0:T(8,128)(2,1)} %weight_ref.1), channel_id=1, source_target_pairs={{0,1},{1,0},{2,3},{3,2},{4,5},{5,4},{6,7},{7,6},{8,9},{9,8},{10,11... | collective-permute-start | bytes 12582920 | tf_op jit(solution)/shard_map/ppermute | solution.py:231
  1.1 1.2 %copy-start = (bf16[512,1024]{1,0:T(8,128)(2,1)S(1)}, bf16[512,1024]{1,0:T(8,128)(2,1)}, u32[]{:S(2)}) copy-start(bf16[512,1024]{1,0:T(8,128)(2,1)} %value_ref.3) | copy-start | bytes 3145732
  2.4 1.2 %copy-start.3 = (bf16[512,1024]{1,0:T(8,128)(2,1)S(1)}, bf16[512,1024]{1,0:T(8,128)(2,1)}, u32[]{:S(2)}) copy-start(bf16[512,1024]{1,0:T(8,128)(2,1)} %key_ref.1) | copy-start | bytes 3145732
  3.6 0.9 %copy-start.5 = (f32[512,128]{1,0:T(8,128)S(1)}, f32[512,128]{1,0:T(8,128)}, u32[]{:S(2)}) copy-start(f32[512,128]{1,0:T(8,128)} %constant.27.clone.row_cos_ref) | copy-start | bytes 786436
  4.5 0.9 %copy-start.7 = (f32[512,128]{1,0:T(8,128)S(1)}, f32[512,128]{1,0:T(8,128)}, u32[]{:S(2)}) copy-start(f32[512,128]{1,0:T(8,128)} %constant.28.clone.row_sin_ref) | copy-start | bytes 786436
  5.5 32.7 %copy-start.20 = (f32[64,8,7]{0,1,2:T(8,128)S(1)}, f32[64,8,7]{0,1,2:T(8,128)}, u32[]{:S(2)}) copy-start(f32[64,8,7]{0,1,2:T(8,128)} %param.14) | copy-start | bytes 43012
  5.5 32.7 %copy-start.21 = (f32[7]{0:T(128)S(1)}, f32[7]{0:T(128)}, u32[]{:S(2)}) copy-start(f32[7]{0:T(128)} %constant.29.clone) | copy-start | bytes 88
  5.5 33.7 %copy-start.1 = (bf16[512,1024]{1,0:T(8,128)(2,1)S(1)}, bf16[512,1024]{1,0:T(8,128)(2,1)}, u32[]{:S(2)}) copy-start(bf16[512,1024]{1,0:T(8,128)(2,1)} %value_ref.3) | copy-start | bytes 3145732
  5.5 33.7 %copy-start.4 = (bf16[512,1024]{1,0:T(8,128)(2,1)S(1)}, bf16[512,1024]{1,0:T(8,128)(2,1)}, u32[]{:S(2)}) copy-start(bf16[512,1024]{1,0:T(8,128)(2,1)} %query_ref.1) | copy-start | bytes 3145732
  5.5 33.7 %copy-start.6 = (f32[512,128]{1,0:T(8,128)S(1)}, f32[512,128]{1,0:T(8,128)}, u32[]{:S(2)}) copy-start(f32[512,128]{1,0:T(8,128)} %constant.27.clone.row_cos_ref) | copy-start | bytes 786436
  5.5 33.6 %copy-start.19 = (s32[512]{0:T(512)S(1)}, s32[512]{0:T(512)}, u32[]{:S(2)}) copy-start(s32[512]{0:T(512)} %param.15) | copy-start | bytes 6148
  7.8 27.3 %copy-start.16 = (bf16[8,3,128,128]{3,2,1,0:T(8,128)(2,1)}, bf16[8,3,128,128]{3,2,1,0:T(8,128)(2,1)S(1)}, u32[]{:S(2)}) copy-start(bf16[8,3,128,128]{3,2,1,0:T(8,128)(2,1)S(1)} %get-tuple-element.12.bucket_ref) | copy-start | bytes 2359300
  7.8 9.5 %collective-permute-start = (bf16[8,128,128]{2,1,0:T(8,128)(2,1)S(1)}, bf16[8,128,128]{2,1,0:T(8,128)(2,1)S(1)}, u32[]{:S(2)}, u32[]{:S(2)}) collective-permute-start(bf16[8,128,128]{2,1,0:T(8,128)(2,1)S(1)} %get-tuple-element.16), channel_id=1, source_target_pairs={{0,2},{2,0},{4,6},{6,4},{8,10},{10,8},{12,14},{14,12},{16,18},{18,... | collective-permute-start | bytes 786440 | tf_op jit(solution)/shard_map/ppermute | solution.py:315
  18.1 8.1 %collective-permute-start.1 = (bf16[8,128,128]{2,1,0:T(8,128)(2,1)S(1)}, bf16[8,128,128]{2,1,0:T(8,128)(2,1)S(1)}, u32[]{:S(2)}, u32[]{:S(2)}) collective-permute-start(bf16[8,128,128]{2,1,0:T(8,128)(2,1)S(1)} %add_convert_fusion.2), channel_id=1, source_target_pairs={{0,4},{2,6},{4,0},{6,2},{8,12},{10,14},{12,8},{14,10},{16,20},{18,... | collective-permute-start | bytes 786440 | tf_op jit(solution)/shard_map/ppermute | solution.py:315
  27.0 7.3 %collective-permute-start.2 = (bf16[8,128,128]{2,1,0:T(8,128)(2,1)S(1)}, bf16[8,128,128]{2,1,0:T(8,128)(2,1)S(1)}, u32[]{:S(2)}, u32[]{:S(2)}) collective-permute-start(bf16[8,128,128]{2,1,0:T(8,128)(2,1)S(1)} %add_convert_fusion.1), channel_id=1, source_target_pairs={{0,8},{2,10},{4,12},{6,14},{8,0},{10,2},{12,4},{14,6},{16,24},{18,... | collective-permute-start | bytes 786440 | tf_op jit(solution)/shard_map/ppermute | solution.py:315
  35.8 13.2 %collective-permute-start.3 = (bf16[8,128,128]{2,1,0:T(8,128)(2,1)}, bf16[8,128,128]{2,1,0:T(8,128)(2,1)}, u32[]{:S(2)}, u32[]{:S(2)}) collective-permute-start(bf16[8,128,128]{2,1,0:T(8,128)(2,1)} %add_convert_fusion), channel_id=1, source_target_pairs={{0,16},{2,18},{4,20},{6,22},{8,24},{10,26},{12,28},{14,30},{16,0},... | collective-permute-start | bytes 786440 | tf_op jit(solution)/shard_map/ppermute | solution.py:315
  39.2 1.0 %copy-start.8 = (f32[512,128]{1,0:T(8,128)S(1)}, f32[512,128]{1,0:T(8,128)}, u32[]{:S(2)}) copy-start(f32[512,128]{1,0:T(8,128)} %constant.28.clone.row_sin_ref) | copy-start | bytes 786436
  41.1 1.1 %copy-start.17 = (bf16[8,3,128,128]{3,2,1,0:T(8,128)(2,1)S(1)}, bf16[8,3,128,128]{3,2,1,0:T(8,128)(2,1)}, u32[]{:S(2)}) copy-start(bf16[8,3,128,128]{3,2,1,0:T(8,128)(2,1)} %copy-done.16) | copy-start | bytes 2359300
  42.2 6.8 %copy-start.10 = (bf16[8,128,128]{2,1,0:T(8,128)(2,1)S(1)}, bf16[8,128,128]{2,1,0:T(8,128)(2,1)}, u32[]{:S(2)}) copy-start(bf16[8,128,128]{2,1,0:T(8,128)(2,1)} %copy-done.9) | copy-start | bytes 786436
  42.2 6.8 %copy-start.12 = (bf16[8,128,128]{2,1,0:T(8,128)(2,1)S(1)}, bf16[8,128,128]{2,1,0:T(8,128)(2,1)}, u32[]{:S(2)}) copy-start(bf16[8,128,128]{2,1,0:T(8,128)(2,1)} %copy-done.11) | copy-start | bytes 786436
  42.2 6.8 %copy-start.14 = (bf16[8,128,128]{2,1,0:T(8,128)(2,1)S(1)}, bf16[8,128,128]{2,1,0:T(8,128)(2,1)}, u32[]{:S(2)}) copy-start(bf16[8,128,128]{2,1,0:T(8,128)(2,1)} %copy-done.13) | copy-start | bytes 786436
  42.2 6.8 %copy-start.18 = (f32[1024]{0:T(1024)S(1)}, f32[1024]{0:T(1024)}, u32[]{:S(2)}) copy-start(f32[1024]{0:T(1024)} %param.16) | copy-start | bytes 12292
  53.7 4.0 %collective-permute-start.4 = (bf16[512,1024]{1,0:T(8,128)(2,1)S(1)}, bf16[512,1024]{1,0:T(8,128)(2,1)S(1)}, u32[]{:S(2)}, u32[]{:S(2)}) collective-permute-start(bf16[512,1024]{1,0:T(8,128)(2,1)S(1)} %cross_levels.1.hidden_ref), channel_id=1, source_target_pairs={{0,1},{1,0},{2,3},{3,2},{4,5},{5,4},{6,7},{7,6},{8,9},{9,8},{10,11... | collective-permute-start | bytes 3145736 | tf_op jit(solution)/shard_map/ppermute | solution.py:340
  53.8 2.2 %copy-start.2 = (bf16[1024,2048]{1,0:T(8,128)(2,1)S(1)}, bf16[1024,2048]{1,0:T(8,128)(2,1)}, u32[]{:S(2)}) copy-start(bf16[1024,2048]{1,0:T(8,128)(2,1)} %weight_ref.1) | copy-start | bytes 12582916
  (4 other events, 3.1 us)

commit v2 on v1

v2 whole, which is shorter than its diff:
```python
import functools
import math

import jax
import jax.numpy as jnp
import numpy as np
from jax import lax
from jax.experimental import pallas as pl
from jax.experimental.pallas import tpu as pltpu
from jax.sharding import PartitionSpec as P

STRETCHES_DEV = 4
ROPE_BASE = 500000.0
NORM_EPS = 1e-06
VMEM_LIMIT = 56 << 20

F32 = jnp.float32
BF16 = jnp.bfloat16


def angle_tables(positions, head_dim):
    half_dim = head_dim // 2
    frequency = np.exp(np.arange(half_dim) * (-2.0 * math.log(ROPE_BASE) / head_dim))
    angles = np.asarray(positions, np.float64)[:, None] * frequency[None, :]
    cosine, sine = np.cos(angles), np.sin(angles)
    return (
        np.concatenate([cosine, cosine], axis=1).astype(np.float32),
        np.concatenate([-sine, sine], axis=1).astype(np.float32),
    )


def level_scale(level_index, stretch_len):
    if level_index == 0:
        return stretch_len ** (-0.5)
    return (2 ** (level_index - 1) * stretch_len) ** (-0.5)


def fill_angles(row_cos_ref, row_sin_ref, base_ref, cos_ref, sin_ref):
    base_cos = base_ref[0:1, :]
    base_sin = base_ref[1:2, :]
    row_cos = row_cos_ref[...]
    row_sin = row_sin_ref[...]
    cos_ref[...] = base_cos * row_cos - base_sin * row_sin
    sin_ref[...] = base_sin * row_cos + base_cos * row_sin


def rotated(vectors, cosine, sine):
    wide = vectors.astype(F32)
    half = wide.shape[-1] // 2
    return (wide * cosine + pltpu.roll(wide, half, 1) * sine).astype(BF16)


def dot_tn(a, b):
    return lax.dot_general(a, b, (((0,), (0,)), ((), ())), preferred_element_type=F32)


def dot_nt(a, b):
    return lax.dot_general(a, b, (((1,), (1,)), ((), ())), preferred_element_type=F32)


def dot_nn(a, b):
    return jnp.dot(a, b, preferred_element_type=F32)


def local_plan(stretches):
    plan = []
    for stretch in range(stretches):
        row = []
        for bit in range(stretches.bit_length() - 1):
            if stretch >> bit & 1:
                end = stretch >> bit << bit
                row.append((bit, tuple(range(end - (1 << bit), end))))
        plan.append(row)
    return plan


def state_kernel(
    slots,
    quarter_heads,
    head_dim,
    place_ref,
    row_cos_ref,
    row_sin_ref,
    base_ref,
    key_ref,
    value_ref,
    key_out,
    bucket_out,
    *refs,
):
    total_outs = refs[:slots]
    cos_ref, sin_ref = refs[slots:]
    slot = pl.program_id(0)

    @pl.when(slot == 0)
    def _():
        fill_angles(row_cos_ref, row_sin_ref, base_ref, cos_ref, sin_ref)

    tok_rows = key_ref.shape[0]
    stretch_len = tok_rows // STRETCHES_DEV
    groups = bucket_groups()
    for head in range(quarter_heads):
        cols = slice(head * head_dim, (head + 1) * head_dim)
        states = []
        for stretch in range(STRETCHES_DEV):
            rows = slice(stretch * stretch_len, (stretch + 1) * stretch_len)
            turned = rotated(key_ref[rows, cols], cos_ref[rows, :], sin_ref[rows, :])
            key_out[rows, cols] = turned
            states.append(dot_tn(turned, value_ref[rows, cols]))
        for spot, members in enumerate(groups):
            bucket_out[head, spot] = sum(states[m] for m in members).astype(BF16)
        total = sum(states).astype(BF16)
        for index in range(slots):

            @pl.when(slot == index)
            def _():
                total_outs[index][head] = total


def bucket_groups():
    groups = []
    for row in local_plan(STRETCHES_DEV):
        for _, members in row:
            if members not in groups:
                groups.append(members)
    return groups


def fill_one_hot(index_ref, one_hot_ref):
    table_rows = one_hot_ref.shape[0] // 3
    rows = lax.broadcasted_iota(jnp.int32, one_hot_ref.shape, 0)
    rows = lax.rem(rows, table_rows)
    one_hot_ref[...] = jnp.where(rows == index_ref[...], 1.0, 0.0).astype(BF16)


def level_weights(one_hot_ref, table):
    high = table.astype(BF16)
    rest = table - high.astype(F32)
    middle = rest.astype(BF16)
    low = (rest - middle.astype(F32)).astype(BF16)
    return dot_tn(one_hot_ref[...], jnp.concatenate([high, middle, low], axis=0))


def local_kernel(
    quarter_heads,
    head_dim,
    first_slot,
    place_ref,
    row_cos_ref,
    row_sin_ref,
    base_ref,
    index_ref,
    table_ref,
    scale_ref,
    query_ref,
    key_ref,
    value_ref,
    bucket_ref,
    query_out,
    combined_out,
    weight_out,
    cos_ref,
    sin_ref,
    one_hot_ref,
):
    @pl.when(pl.program_id(0) == 0)
    def _():
        fill_angles(row_cos_ref, row_sin_ref, base_ref, cos_ref, sin_ref)
        fill_one_hot(index_ref, one_hot_ref)

    tok_rows = key_ref.shape[0]
    levels = scale_ref.shape[1]
    stretch_len = tok_rows // STRETCHES_DEV
    groups = bucket_groups()
    shape = (stretch_len, stretch_len)
    causal = lax.broadcasted_iota(jnp.int32, shape, 0) >= lax.broadcasted_iota(jnp.int32, shape, 1)
    quarter = place_ref[first_slot + pl.program_id(0)]
    for head in range(quarter_heads):
        cols = slice(head * head_dim, (head + 1) * head_dim)
        table = table_ref[:, pl.ds(quarter * quarter_heads + head, 1), :]
        table = table.reshape(table.shape[0], levels) * scale_ref[...]
        weights = level_weights(one_hot_ref, table)
        weight_out[0, :, head * levels : (head + 1) * levels] = weights
        for stretch, row in enumerate(local_plan(STRETCHES_DEV)):
            rows = slice(stretch * stretch_len, (stretch + 1) * stretch_len)
            turned = rotated(query_ref[rows, cols], cos_ref[rows, :], sin_ref[rows, :])
            query_out[rows, cols] = turned
            scores = jnp.where(causal, dot_nt(turned, key_ref[rows, cols]), 0.0).astype(BF16)
            total = weights[rows, 0:1] * dot_nn(scores, value_ref[rows, cols])
            for bit, members in row:
                read = dot_nn(turned, bucket_ref[head, groups.index(members)])
                total = total + weights[rows, bit + 1 : bit + 2] * read
            combined_out[rows, cols] = total


def cross_kernel(
    slots,
    quarter_heads,
    head_dim,
    levels,
    low_levels,
    high_levels,
    place_ref,
    combined_ref,
    query_ref,
    weight_ref,
    gain_ref,
    *refs,
):
    low_refs = refs[:slots]
    high_refs = refs[slots : 2 * slots]
    hidden_out = refs[2 * slots]
    shard_index = place_ref[place_ref.shape[0] - 2]
    cross_levels = low_levels + high_levels
    present = [(shard_index >> bit & 1).astype(F32) for bit in range(cross_levels)]
    for slot in range(slots):

        @pl.when(pl.program_id(0) == slot)
        def _():
            for head in range(quarter_heads):
                cols = slice(head * head_dim, (head + 1) * head_dim)
                total = combined_ref[:, cols]
                queries = query_ref[:, cols]
                for level in range(cross_levels):
                    if level < low_levels:
                        bucket = low_refs[slot][level * quarter_heads + head]
                    else:
                        bucket = high_refs[slot][(level - low_levels) * quarter_heads + head]
                    spot = head * levels + levels - cross_levels + level
                    weight = weight_ref[0, :, spot : spot + 1] * present[level]
                    total = total + weight * dot_nn(queries, bucket)
                mean_square = jnp.mean(total * total, axis=-1, keepdims=True)
                normed = total * lax.rsqrt(mean_square + NORM_EPS) * gain_ref[:, cols]
                hidden_out[:, cols] = normed.astype(BF16)


def project(slots, place_ref, hidden_refs, weight_ref):
    width = weight_ref.shape[0] // slots
    here = slots // len(hidden_refs)
    total = None
    for slot in range(slots):
        start = pl.multiple_of(place_ref[slot] * width, width)
        spot = slot % here * width
        part = dot_nn(
            hidden_refs[slot // here][:, spot : spot + width], weight_ref[pl.ds(start, width), :]
        )
        total = part if total is None else total + part
    return total


def own_kernel(slots, place_ref, *refs):
    *hidden_refs, weight_ref, out_ref = refs
    out_ref[...] = project(slots, place_ref, hidden_refs, weight_ref).astype(BF16)


def other_kernel(slots, place_ref, *refs):
    *hidden_refs, weight_ref, part_ref, out_ref = refs
    total = project(slots, place_ref, hidden_refs, weight_ref).astype(BF16).astype(F32)
    out_ref[...] = (part_ref[...].astype(F32) + total).astype(BF16)


def cost(flops, size):
    return pl.CostEstimate(flops=int(flops), bytes_accessed=int(size), transcendentals=0)


def bfloat_sum(*blocks):
    return sum(block.astype(F32) for block in blocks).astype(BF16)


def high_buckets(total, shard_index, first_bit, ctx_bits, n_ctx):
    buckets = []
    for low in range(first_bit, ctx_bits, 2):
        bits = min(2, ctx_bits - low)
        radix = 1 << bits
        mask = (radix - 1) << low
        digit = shard_index >> low & (radix - 1)

        def turned(index, by):
            return index & ~mask | (((index >> low) + by) & (radix - 1)) << low

        back = [
            lax.ppermute(total, "ctx", [(i, turned(i, by)) for i in range(n_ctx)])
            for by in range(1, radix)
        ]
        buckets.append(back[0])
        if bits == 2:
            wide = [block.astype(F32) for block in back]
            buckets.append(
                jnp.where(digit == 2, wide[0] + wide[1], wide[1] + wide[2]).astype(BF16)
            )
        if low + bits < ctx_bits:
            total = bfloat_sum(total, *back)
    return buckets


def local(queries, key_vectors, values, level_table, weight_index, norm_gain, out_weight):
    tok_rows, model_width = queries.shape
    table_rows, heads_here, level_count = level_table.shape
    head_dim = model_width // heads_here
    stretch_len = tok_rows // STRETCHES_DEV
    n_ctx = lax.axis_size("ctx")
    n_head = lax.axis_size("head")
    ctx_bits = n_ctx.bit_length() - 1
    shard_index = lax.axis_index("ctx")
    head_index = lax.axis_index("head")
    group_count = len(bucket_groups())

    low_bits = min(2, ctx_bits)
    slots = 1 << low_bits
    quarter_heads = heads_here // slots
    width = quarter_heads * head_dim
    chunk = slots // 2

    def swap_heads(block):
        return lax.ppermute(block, "head", [(i, i ^ 1) for i in range(n_head)])

    def swap_low(block, by):
        return lax.ppermute(block, "ctx", [(i, i ^ by) for i in range(n_ctx)])

    other_weight = swap_heads(out_weight)
    order = jnp.arange(slots, dtype=jnp.int32) ^ (shard_index & (slots - 1)).astype(jnp.int32)
    place = jnp.concatenate(
        [order, jnp.stack([shard_index, head_index]).astype(jnp.int32)]
    )

    row_cos, row_sin = angle_tables(np.arange(tok_rows), head_dim)
    base = np.stack(angle_tables(np.arange(n_ctx) * tok_rows, head_dim), axis=1)
    scales = np.array([[level_scale(i, stretch_len) for i in range(level_count)]], np.float32)

    def fixed(*shape):
        return pl.BlockSpec(shape, lambda s, place: (0,) * len(shape))

    def ordered(first):
        return pl.BlockSpec((tok_rows, width), lambda s, place: (0, place[first + s]))

    def by_slot(first):
        return pl.BlockSpec((tok_rows, width), lambda s, place: (0, first + s))

    def bucket_by_slot(first):
        return pl.BlockSpec(
            (quarter_heads, group_count, head_dim, head_dim), lambda s, place: (first + s, 0, 0, 0)
        )

    angle_specs = [
        fixed(tok_rows, head_dim),
        fixed(tok_rows, head_dim),
        pl.BlockSpec((None, 2, head_dim), lambda s, place: (place[slots], 0, 0)),
    ]
    angle_scratch = [pltpu.VMEM((tok_rows, head_dim), F32)] * 2
    params = pltpu.CompilerParams(
        dimension_semantics=("arbitrary",), vmem_limit_bytes=VMEM_LIMIT
    )
    head_macs = tok_rows * head_dim * head_dim * heads_here
    block_bytes = tok_rows * model_width * 2

    keys, local_states, *shares = pl.pallas_call(
        functools.partial(state_kernel, slots, quarter_heads, head_dim),
        grid_spec=pltpu.PrefetchScalarGridSpec(
            num_scalar_prefetch=1,
            grid=(slots,),
            in_specs=angle_specs + [ordered(0), ordered(0)],
            out_specs=[by_slot(0), bucket_by_slot(0)]
            + [fixed(quarter_heads, head_dim, head_dim)] * slots,
            scratch_shapes=angle_scratch,
        ),
        out_shape=[
            jax.ShapeDtypeStruct((tok_rows, model_width), BF16),
            jax.ShapeDtypeStruct((heads_here, group_count, head_dim, head_dim), BF16),
        ]
        + [jax.ShapeDtypeStruct((quarter_heads, head_dim, head_dim), BF16)] * slots,
        compiler_params=params,
        cost_estimate=cost(2 * head_macs, 4 * block_bytes),
        name="states",
    )(place, row_cos, row_sin, base, key_vectors, values)

    def local_levels(first):
        return pl.pallas_call(
            functools.partial(local_kernel, quarter_heads, head_dim, first),
            grid_spec=pltpu.PrefetchScalarGridSpec(
                num_scalar_prefetch=1,
                grid=(chunk,),
                in_specs=angle_specs
                + [
                    fixed(1, tok_rows),
                    fixed(table_rows, heads_here, level_count),
                    fixed(1, level_count),
                    ordered(first),
                    by_slot(first),
                    ordered(first),
                    bucket_by_slot(first),
                ],
                out_specs=[
                    by_slot(0),
                    by_slot(0),
                    pl.BlockSpec(
                        (1, tok_rows, quarter_heads * level_count), lambda s, place: (s, 0, 0)
                    ),
                ],
                scratch_shapes=angle_scratch + [pltpu.VMEM((3 * table_rows, tok_rows), BF16)],
            ),
            out_shape=[
                jax.ShapeDtypeStruct((tok_rows, chunk * width), BF16),
                jax.ShapeDtypeStruct((tok_rows, chunk * width), F32),
                jax.ShapeDtypeStruct((chunk, tok_rows, quarter_heads * level_count), F32),
            ],
            compiler_params=params,
            cost_estimate=cost(4 * head_macs, 4 * block_bytes),
            name="local_levels",
        )(
            place,
            row_cos,
            row_sin,
            base,
            weight_index.reshape(1, tok_rows),
            level_table,
            scales,
            queries,
            keys,
            values,
            local_states,
        )

    parts = [shares[0]] + [swap_low(shares[by], by) for by in range(1, slots)]
    total = bfloat_sum(*parts)

    def low_payload(by):
        levels = []
        for bit in range(low_bits):
            members = [m for m in range(slots) if m >> bit == 1]
            levels.append(bfloat_sum(*[parts[m ^ by] for m in members]))
        return jnp.concatenate(levels, axis=0)

    high = jnp.concatenate(high_buckets(total, shard_index, low_bits, ctx_bits, n_ctx), axis=0)
    low_slots = [low_payload(0)] + [swap_low(low_payload(by), by) for by in range(1, slots)]
    high_slots = [high] + [swap_low(high, by) for by in range(1, slots)]
    gain = norm_gain.reshape(1, model_width)
    high_bits = ctx_bits - low_bits

    hidden, other_hidden = [], []
    for first in range(0, slots, chunk):
        rotated_queries, combined, weights = local_levels(first)
        piece = pl.pallas_call(
            functools.partial(
                cross_kernel, chunk, quarter_heads, head_dim, level_count, low_bits, high_bits
            ),
            grid_spec=pltpu.PrefetchScalarGridSpec(
                num_scalar_prefetch=1,
                grid=(chunk,),
                in_specs=[
                    by_slot(0),
                    by_slot(0),
                    pl.BlockSpec(
                        (1, tok_rows, quarter_heads * level_count), lambda s, place: (s, 0, 0)
                    ),
                    pl.BlockSpec((1, width), lambda s, place, first=first: (0, place[first + s])),
                ]
                + [fixed(low_bits * quarter_heads, head_dim, head_dim)] * chunk
                + [fixed(high_bits * quarter_heads, head_dim, head_dim)] * chunk,
                out_specs=by_slot(0),
            ),
            out_shape=jax.ShapeDtypeStruct((tok_rows, chunk * width), BF16),
            compiler_params=params,
            cost_estimate=cost(ctx_bits * head_macs, 3 * block_bytes),
            name="cross_levels",
        )(
            place,
            combined,
            rotated_queries,
            weights,
            gain,
            *low_slots[first : first + chunk],
            *high_slots[first : first + chunk],
        )
        hidden.append(piece)
        other_hidden.append(swap_heads(piece))

    out_cols = out_weight.shape[1] // n_head
    tile = min(256, out_cols)
    tiles = out_cols // tile
    hidden_specs = [fixed(tok_rows, chunk * width)] * len(hidden)
    weight_spec = pl.BlockSpec(
        (model_width, tile), lambda n, place: (0, place[slots + 1] * tiles + n)
    )
    out_spec = pl.BlockSpec((tok_rows, tile), lambda n, place: (0, n))
    matmul_flops = 2 * tok_rows * model_width * out_cols

    def projection(kernel, name, in_specs, *operands):
        return pl.pallas_call(
            functools.partial(kernel, slots),
            grid_spec=pltpu.PrefetchScalarGridSpec(
                num_scalar_prefetch=1, grid=(tiles,), in_specs=in_specs, out_specs=out_spec
            ),
            out_shape=jax.ShapeDtypeStruct((tok_rows, out_cols), BF16),
            compiler_params=params,
            cost_estimate=cost(matmul_flops, 8 * block_bytes),
            name=name,
        )(place, *operands)

    own_part = projection(
        own_kernel, "own_group", hidden_specs + [weight_spec], *hidden, out_weight
    )
    return projection(
        other_kernel,
        "other_group",
        hidden_specs + [weight_spec, out_spec],
        *other_hidden,
        other_weight,
        own_part,
    )


def solution(mesh):
    return jax.shard_map(
        local,
        mesh=mesh,
        in_specs=(
            P("ctx", "head"),
            P("ctx", "head"),
            P("ctx", "head"),
            P(None, "head", None),
            P("ctx"),
            P("head"),
            P("head", None),
        ),
        out_specs=P("ctx", "head"),
        check_vma=False,
    )
```

time: 61.8 us -> 71.1 us (1.15)
  Pallas kernels: 18.8 us -> 39 us
  local copies, waits for them, and re-layouts: 13.3 us -> 2.53 us
  waiting for transfers between devices: 19.2 us -> 10.8 us
  starting transfers between devices: 8.87 us -> 14.9 us
  other arithmetic: 1 us -> 3.13 us
    pallas_call x5 -> x7, Pallas kernels: 18.8 us -> 39 us  [the longest x2 12.6 us: local_levels(): pl.pallas_call(functools.partial(local_kernel, quarter_heads, head_dim, f...]
    unnamed x44 -> x21, local copies, waits for them, and re-layouts: 11.7 us -> 2.53 us
    ppermute x6 -> x15, waiting for transfers between devices: 19.2 us -> 10.8 us  [the longest x9 7.75 us: swap_low(): return lax.ppermute(block, 'ctx', [(i, i ^ by) for i in range(n_ctx)])]
    ppermute x6 -> x15, starting transfers between devices: 8.87 us -> 14.9 us  [the longest x9 9.23 us: swap_low(): return lax.ppermute(block, 'ctx', [(i, i ^ by) for i in range(n_ctx)])]
    concatenate x0 -> x4, other arithmetic: none -> 2.2 us  [the longest x2 1.53 us: low_payload(): return jnp.concatenate(levels, axis=0)]
    mul x1 -> x0, local copies, waits for them, and re-layouts: 0.89 us -> none  [local(): table = jnp.transpose(level_table, (1, 0, 2)) * scales]
  transfers between devices with their start and end apart: 6 -> 15, of which waited for: 4 -> 6; matrix products, arithmetic and copies ran while one was open for 4% -> 6% of each run, Pallas kernels for 25% -> 47%
where the time goes in v2:
time: 71.1 us; the launch traced here: 70.5 us
  Pallas kernels  39 us (55%)
  starting transfers between devices  14.9 us (21%)
  waiting for transfers between devices  10.8 us (15%)
  other arithmetic  3.13 us (4%)
  local copies, waits for them, and re-layouts  2.53 us (4%)
    pallas_call x2, Pallas kernels, local_levels(): pl.pallas_call(functools.partial(local_kernel, quarter_heads, head_dim, f...  12.6 us
    pallas_call x2, Pallas kernels, projection(): pl.pallas_call(functools.partial(kernel, slots), grid_spec=pltpu.Prefetch...  11.1 us
    pallas_call x2, Pallas kernels, local(): pl.pallas_call(functools.partial(cross_kernel, chunk, quarter_heads, head...  9.36 us
    ppermute x9, starting transfers between devices, swap_low(): return lax.ppermute(block, 'ctx', [(i, i ^ by) for i in range(n_ctx)])  9.23 us
    ppermute x9, waiting for transfers between devices, swap_low(): return lax.ppermute(block, 'ctx', [(i, i ^ by) for i in range(n_ctx)])  7.75 us
    pallas_call x1, Pallas kernels, local(): pl.pallas_call(functools.partial(state_kernel, slots, quarter_heads, head...  5.97 us
    ppermute x3, starting transfers between devices, high_buckets(): lax.ppermute(total, 'ctx', [(i, turned(i, by)) for i in range(n_ctx)])  4.67 us
    ppermute x3, waiting for transfers between devices, high_buckets(): lax.ppermute(total, 'ctx', [(i, turned(i, by)) for i in range(n_ctx)])  3.01 us
  transfers between devices with their start and end apart: 15, of which 6 were waited for; matrix products, arithmetic and copies ran while one was open for 6% of the time, Pallas kernels for 47%

profile of v2, /device:TPU:0, one launch (start us, length us, event | category | flops | bytes accessed | tf_op | source)
XLA Modules:
  0.0 70.5 jit_solution(511886098334702244)
XLA Ops:
  0.5 0.7 pad_add_fusion.place_ref
  1.1 6.0 %states.1 = (bf16[512,1024]{1,0:T(8,128)(2,1)}, bf16[8,3,128,128]{3,2,1,0:T(8,128)(2,1)}, bf16[2,128,128]{2,1,0:T(8,128)(2,1)}, bf16[2,128,128]{2,1,0:T(8,128)(2...) custom-call(s32[6]{0:T(128)} %pad_add_fusion.place_ref, f32[512,128]{1,0:T(8,128)} %constant.20.clone.row_cos_ref, ...), custom_call_target="tpu_custom_call" | custom-call | flops 134217728 | bytes 4194304 | tf_op jit(solution)/shard_map/states/pallas_call | solution.py:356
  7.1 2.6 %collective-permute-start = (bf16[2,128,128]{2,1,0:T(8,128)(2,1)}, bf16[2,128,128]{2,1,0:T(8,128)(2,1)S(1)}, u32[]{:S(2)}, u32[]{:S(2)}) collective-permute-start(bf16[2,128,128]{2,1,0:T(8,128)(2,1)} %get-tuple-element.22), channel_id=1, source_target_pairs={{0,2},{2,0},{4,6},{6,4},{8,10},{10,8},{12,14},{14,12},{16,18},{18,... | collective-permute-start | bytes 196616 | tf_op jit(solution)/shard_map/ppermute | solution.py:318
  9.6 1.5 %collective-permute-start.1 = (bf16[2,128,128]{2,1,0:T(8,128)(2,1)}, bf16[2,128,128]{2,1,0:T(8,128)(2,1)S(1)}, u32[]{:S(2)}, u32[]{:S(2)}) collective-permute-start(bf16[2,128,128]{2,1,0:T(8,128)(2,1)} %get-tuple-element.23), channel_id=1, source_target_pairs={{0,4},{2,6},{4,0},{6,2},{8,12},{10,14},{12,8},{14,10},{16,20},{18,... | collective-permute-start | bytes 196616 | tf_op jit(solution)/shard_map/ppermute | solution.py:318
  11.2 1.4 %collective-permute-done = bf16[2,128,128]{2,1,0:T(8,128)(2,1)S(1)} collective-permute-done((bf16[2,128,128]{2,1,0:T(8,128)(2,1)}, bf16[2,128,128]{2,1,0:T(8,128)(2,1)S(1)}, u32[]{:S(2)}, u32[]{:S(2)}) %collective-permute-start) | collective-permute-done | bytes 65568 | tf_op jit(solution)/shard_map/ppermute | solution.py:318
  12.6 1.5 %collective-permute-done.1 = bf16[2,128,128]{2,1,0:T(8,128)(2,1)S(1)} collective-permute-done((bf16[2,128,128]{2,1,0:T(8,128)(2,1)}, bf16[2,128,128]{2,1,0:T(8,128)(2,1)S(1)}, u32[]{:S(2)}, u32[]{:S(2)}) %collective-permute-start.1) | collective-permute-done | bytes 65568 | tf_op jit(solution)/shard_map/ppermute | solution.py:318
  14.1 2.4 %collective-permute-done.2 = bf16[2,128,128]{2,1,0:T(8,128)(2,1)S(1)} collective-permute-done((bf16[2,128,128]{2,1,0:T(8,128)(2,1)}, bf16[2,128,128]{2,1,0:T(8,128)(2,1)S(1)}, u32[]{:S(2)}, u32[]{:S(2)}) %collective-permute-start.2) | collective-permute-done | bytes 65568 | tf_op jit(solution)/shard_map/ppermute | solution.py:318
  16.5 0.9 %fusion.4 = (bf16[2,128,128]{2,1,0:T(8,128)(2,1)S(1)}, bf16[2,128,128]{2,1,0:T(8,128)(2,1)S(1)}, bf16[2,128,128]{2,1,0:T(8,128)(2,1)S(1)}) fusion(bf16[2,128,128]{2,1,0:T(8,128)(2,1)S(1)} %collective-permute-done, bf16[2,128,128]{2,1,0:T(8,128)(2,1)} %get-tuple-element.25, bf16[2,128,128]{2,1,0:T(8,128)(2,1)S(1)} %collective-permute-done.2, ...), kind=kLoop, calls=%fused_computation.15 | loop fusion | flops 360448 | bytes 458752 | tf_op jit(solution)/shard_map/convert_element_type | solution.py:267
  17.4 3.7 %collective-permute-start.6 = (bf16[2,128,128]{2,1,0:T(8,128)(2,1)S(1)}, bf16[2,128,128]{2,1,0:T(8,128)(2,1)S(1)}, u32[]{:S(2)}, u32[]{:S(2)}) collective-permute-start(bf16[2,128,128]{2,1,0:T(8,128)(2,1)S(1)} %get-tuple-element.30), channel_id=1, source_target_pairs={{0,24},{2,26},{4,28},{6,30},{8,0},{10,2},{12,4},{14,6},{16,8},{18,... | collective-permute-start | bytes 196616 | tf_op jit(solution)/shard_map/ppermute | solution.py:282
  21.1 1.0 %collective-permute-start.4 = (bf16[2,128,128]{2,1,0:T(8,128)(2,1)S(1)}, bf16[2,128,128]{2,1,0:T(8,128)(2,1)S(1)}, u32[]{:S(2)}, u32[]{:S(2)}) collective-permute-start(bf16[2,128,128]{2,1,0:T(8,128)(2,1)S(1)} %get-tuple-element.30), channel_id=1, source_target_pairs={{0,8},{2,10},{4,12},{6,14},{8,16},{10,18},{12,20},{14,22},{16,24},... | collective-permute-start | bytes 196616 | tf_op jit(solution)/shard_map/ppermute | solution.py:282
  22.1 1.5 %pad_maximum_fusion = (bf16[4,128,128]{2,1,0:T(8,128)(2,1)S(1)}, bf16[4,128,128]{2,1,0:T(8,128)(2,1)}) fusion(bf16[2,128,128]{2,1,0:T(8,128)(2,1)S(1)} %get-tuple-element.31, bf16[2,128,128]{2,1,0:T(8,128)(2,1)} %get-tuple-element.25, bf16[2,128,128]{2,1,0:T(8,128)(2,1)S(1)} %collective-permute-done), kind=kLoop, calls=%fused_computation.5 | loop fusion | flops 131072 | bytes 458752 | tf_op jit(solution)/shard_map/concatenate | solution.py:431
  24.2 2.1 %collective-permute-done.5 = bf16[2,128,128]{2,1,0:T(8,128)(2,1)S(1)} collective-permute-done((bf16[2,128,128]{2,1,0:T(8,128)(2,1)S(1)}, bf16[2,128,128]{2,1,0:T(8,128)(2,1)S(1)}, u32[]{:S(2)}, u32[]{:S(2)}) %collective-permute-start.5) | collective-permute-done | bytes 65568 | tf_op jit(solution)/shard_map/ppermute | solution.py:282
  26.3 0.9 %collective-permute-done.4 = bf16[2,128,128]{2,1,0:T(8,128)(2,1)S(1)} collective-permute-done((bf16[2,128,128]{2,1,0:T(8,128)(2,1)S(1)}, bf16[2,128,128]{2,1,0:T(8,128)(2,1)S(1)}, u32[]{:S(2)}, u32[]{:S(2)}) %collective-permute-start.4) | collective-permute-done | bytes 65568 | tf_op jit(solution)/shard_map/ppermute | solution.py:282
  27.9 1.5 %collective-permute-start.10 = (bf16[4,128,128]{2,1,0:T(8,128)(2,1)S(1)}, bf16[4,128,128]{2,1,0:T(8,128)(2,1)S(1)}, u32[]{:S(2)}, u32[]{:S(2)}) collective-permute-start(bf16[4,128,128]{2,1,0:T(8,128)(2,1)S(1)} %get-tuple-element.32), channel_id=1, source_target_pairs={{0,6},{2,4},{4,2},{6,0},{8,14},{10,12},{12,10},{14,8},{16,22},{18,... | collective-permute-start | bytes 393224 | tf_op jit(solution)/shard_map/ppermute | solution.py:318
  29.4 1.5 %collective-permute-start.9 = (bf16[4,128,128]{2,1,0:T(8,128)(2,1)S(1)}, bf16[4,128,128]{2,1,0:T(8,128)(2,1)S(1)}, u32[]{:S(2)}, u32[]{:S(2)}) collective-permute-start(bf16[4,128,128]{2,1,0:T(8,128)(2,1)S(1)} %get-tuple-element.33), channel_id=1, source_target_pairs={{0,4},{2,6},{4,0},{6,2},{8,12},{10,14},{12,8},{14,10},{16,20},{18,... | collective-permute-start | bytes 393224 | tf_op jit(solution)/shard_map/ppermute | solution.py:318
  31.4 2.4 %collective-permute-done.7.refs_3_ = bf16[4,128,128]{2,1,0:T(8,128)(2,1)S(1)} collective-permute-done((bf16[4,128,128]{2,1,0:T(8,128)(2,1)S(1)}, bf16[4,128,128]{2,1,0:T(8,128)(2,1)S(1)}, u32[]{:S(2)}, u32[]{:S(2)}) %collective-permute-start.7) | collective-permute-done | bytes 131104 | tf_op jit(solution)/shard_map/ppermute | solution.py:318
  34.3 0.9 %copy.12.table_ref = f32[64,8,7]{2,1,0:T(8,128)} copy(f32[64,8,7]{0,1,2:T(8,128)S(1)} %copy-done.9) | data formatting | bytes 28672 | tf_op args[3]
  35.1 6.3 %local_levels.3 = (bf16[512,512]{1,0:T(8,128)(2,1)}, f32[512,512]{1,0:T(8,128)}, f32[2,512,14]{2,1,0:T(8,128)}) custom-call(s32[6]{0:T(128)} %pad_add_fusion.place_ref, f32[512,128]{1,0:T(8,128)} %constant.20.clone.row_cos_ref, f32[512,128]{1,0:T(8,128)} %constant.21.clone.row_sin_ref, f32[16,2,128]{2,1,0:T(2,128)} %constant.22.clone.base_ref, ...), custom_call_target="tpu_custom_call" | custom-call | flops 268435456 | bytes 4194304 | tf_op jit(solution)/shard_map/local_levels/pallas_call | solution.py:377
  41.4 6.3 %local_levels.2 = (bf16[512,512]{1,0:T(8,128)(2,1)}, f32[512,512]{1,0:T(8,128)}, f32[2,512,14]{2,1,0:T(8,128)}) custom-call(s32[6]{0:T(128)} %pad_add_fusion.place_ref, f32[512,128]{1,0:T(8,128)} %constant.20.clone.row_cos_ref, f32[512,128]{1,0:T(8,128)} %constant.21.clone.row_sin_ref, f32[16,2,128]{2,1,0:T(2,128)} %constant.22.clone.base_ref, ...), custom_call_target="tpu_custom_call" | custom-call | flops 268435456 | bytes 4194304 | tf_op jit(solution)/shard_map/local_levels/pallas_call | solution.py:377
  47.7 4.7 %cross_levels.2.refs_0_ = bf16[512,512]{1,0:T(8,128)(2,1)} custom-call(s32[6]{0:T(128)} %pad_add_fusion.place_ref, f32[512,512]{1,0:T(8,128)} %get-tuple-element.19.combined_ref, bf16[512,512]{1,0:T(8,128)(2,1)} %get-tuple-element.20.query_ref, f32[2,512,14]{2,1,0:T(8,128)} %get-tuple-element.21.weight_ref, f32[1,1024]{1,0:T(1,128)} %bitcast.4, ...), custom_call_target="tpu_custom_call" | custom-call | flops 268435456 | bytes 3145728 | tf_op jit(solution)/shard_map/cross_levels/pallas_call | solution.py:442
  53.2 4.7 %cross_levels.3.refs_1_ = bf16[512,512]{1,0:T(8,128)(2,1)} custom-call(s32[6]{0:T(128)} %pad_add_fusion.place_ref, f32[512,512]{1,0:T(8,128)} %get-tuple-element.26.combined_ref, bf16[512,512]{1,0:T(8,128)(2,1)} %get-tuple-element.27.query_ref, f32[2,512,14]{2,1,0:T(8,128)} %get-tuple-element.28.weight_ref, f32[1,1024]{1,0:T(1,128)} %bitcast.5, ...), custom_call_target="tpu_custom_call" | custom-call | flops 268435456 | bytes 3145728 | tf_op jit(solution)/shard_map/cross_levels/pallas_call | solution.py:442
  58.4 5.5 %own_group.1.refs_3_ = bf16[512,1024]{1,0:T(8,128)(2,1)} custom-call(s32[6]{0:T(128)} %pad_add_fusion.place_ref, bf16[512,512]{1,0:T(8,128)(2,1)} %cross_levels.2.refs_0_, bf16[512,512]{1,0:T(8,128)(2,1)} %cross_levels.3.refs_1_, bf16[1024,2048]{1,0:T(8,128)(2,1)} %refs_2_.1), custom_call_target="tpu_custom_call" | custom-call | flops 1073741824 | bytes 8388608 | tf_op jit(solution)/shard_map/own_group/pallas_call | solution.py:488
  64.0 0.8 %copy-done = bf16[512,512]{1,0:T(8,128)(2,1)} copy-done((bf16[512,512]{1,0:T(8,128)(2,1)}, bf16[512,512]{1,0:T(8,128)(2,1)S(1)}, u32[]{:S(2)}) %copy-start) | copy-done | bytes 524312
  64.9 5.6 %other_group.1 = bf16[512,1024]{1,0:T(8,128)(2,1)} custom-call(s32[6]{0:T(128)} %pad_add_fusion.place_ref, bf16[512,512]{1,0:T(8,128)(2,1)} %copy-done, bf16[512,512]{1,0:T(8,128)(2,1)} %copy-done.1, bf16[1024,2048]{1,0:T(8,128)(2,1)} %collective-permute-done.14.refs_2_, bf16[512,1024]{1,0:T(8,128)(2,1)} %own_group.1.refs_3_), custom_call_target="tpu_custom_call" | custom-call | flops 1073741824 | bytes 8388608 | tf_op jit(solution)/shard_map/other_group/pallas_call | solution.py:488
  (41 shorter events, 4.1 us)
Async XLA Ops:
  0.0 34.3 %copy-start.9 = (f32[64,8,7]{0,1,2:T(8,128)S(1)}, f32[64,8,7]{0,1,2:T(8,128)}, u32[]{:S(2)}) copy-start(f32[64,8,7]{0,1,2:T(8,128)} %param.14) | copy-start | bytes 43012
  0.0 64.0 %collective-permute-start.14 = (bf16[1024,2048]{1,0:T(8,128)(2,1)}, bf16[1024,2048]{1,0:T(8,128)(2,1)}, u32[]{:S(2)}, u32[]{:S(2)}) collective-permute-start(bf16[1024,2048]{1,0:T(8,128)(2,1)} %refs_2_.1), channel_id=1, source_target_pairs={{0,1},{1,0},{2,3},{3,2},{4,5},{5,4},{6,7},{7,6},{8,9},{9,8},{10,11... | collective-permute-start | bytes 12582920 | tf_op jit(solution)/shard_map/ppermute | solution.py:315
  7.1 5.5 %collective-permute-start = (bf16[2,128,128]{2,1,0:T(8,128)(2,1)}, bf16[2,128,128]{2,1,0:T(8,128)(2,1)S(1)}, u32[]{:S(2)}, u32[]{:S(2)}) collective-permute-start(bf16[2,128,128]{2,1,0:T(8,128)(2,1)} %get-tuple-element.22), channel_id=1, source_target_pairs={{0,2},{2,0},{4,6},{6,4},{8,10},{10,8},{12,14},{14,12},{16,18},{18,... | collective-permute-start | bytes 196616 | tf_op jit(solution)/shard_map/ppermute | solution.py:318
  9.6 4.5 %collective-permute-start.1 = (bf16[2,128,128]{2,1,0:T(8,128)(2,1)}, bf16[2,128,128]{2,1,0:T(8,128)(2,1)S(1)}, u32[]{:S(2)}, u32[]{:S(2)}) collective-permute-start(bf16[2,128,128]{2,1,0:T(8,128)(2,1)} %get-tuple-element.23), channel_id=1, source_target_pairs={{0,4},{2,6},{4,0},{6,2},{8,12},{10,14},{12,8},{14,10},{16,20},{18,... | collective-permute-start | bytes 196616 | tf_op jit(solution)/shard_map/ppermute | solution.py:318
  11.2 5.4 %collective-permute-start.2 = (bf16[2,128,128]{2,1,0:T(8,128)(2,1)}, bf16[2,128,128]{2,1,0:T(8,128)(2,1)S(1)}, u32[]{:S(2)}, u32[]{:S(2)}) collective-permute-start(bf16[2,128,128]{2,1,0:T(8,128)(2,1)} %get-tuple-element.24), channel_id=1, source_target_pairs={{0,6},{2,4},{4,2},{6,0},{8,14},{10,12},{12,10},{14,8},{16,22},{18,... | collective-permute-start | bytes 196616 | tf_op jit(solution)/shard_map/ppermute | solution.py:318
  17.4 6.7 %collective-permute-start.6 = (bf16[2,128,128]{2,1,0:T(8,128)(2,1)S(1)}, bf16[2,128,128]{2,1,0:T(8,128)(2,1)S(1)}, u32[]{:S(2)}, u32[]{:S(2)}) collective-permute-start(bf16[2,128,128]{2,1,0:T(8,128)(2,1)S(1)} %get-tuple-element.30), channel_id=1, source_target_pairs={{0,24},{2,26},{4,28},{6,30},{8,0},{10,2},{12,4},{14,6},{16,8},{18,... | collective-permute-start | bytes 196616 | tf_op jit(solution)/shard_map/ppermute | solution.py:282
  21.1 5.2 %collective-permute-start.5 = (bf16[2,128,128]{2,1,0:T(8,128)(2,1)S(1)}, bf16[2,128,128]{2,1,0:T(8,128)(2,1)S(1)}, u32[]{:S(2)}, u32[]{:S(2)}) collective-permute-start(bf16[2,128,128]{2,1,0:T(8,128)(2,1)S(1)} %get-tuple-element.30), channel_id=1, source_target_pairs={{0,16},{2,18},{4,20},{6,22},{8,24},{10,26},{12,28},{14,30},{16,0},... | collective-permute-start | bytes 196616 | tf_op jit(solution)/shard_map/ppermute | solution.py:282
  21.1 6.1 %collective-permute-start.4 = (bf16[2,128,128]{2,1,0:T(8,128)(2,1)S(1)}, bf16[2,128,128]{2,1,0:T(8,128)(2,1)S(1)}, u32[]{:S(2)}, u32[]{:S(2)}) collective-permute-start(bf16[2,128,128]{2,1,0:T(8,128)(2,1)S(1)} %get-tuple-element.30), channel_id=1, source_target_pairs={{0,8},{2,10},{4,12},{6,14},{8,16},{10,18},{12,20},{14,22},{16,24},... | collective-permute-start | bytes 196616 | tf_op jit(solution)/shard_map/ppermute | solution.py:282
  23.6 7.3 %collective-permute-start.3 = (bf16[4,128,128]{2,1,0:T(8,128)(2,1)S(1)}, bf16[4,128,128]{2,1,0:T(8,128)(2,1)S(1)}, u32[]{:S(2)}, u32[]{:S(2)}) collective-permute-start(bf16[4,128,128]{2,1,0:T(8,128)(2,1)S(1)} %get-tuple-element.34), channel_id=1, source_target_pairs={{0,2},{2,0},{4,6},{6,4},{8,10},{10,8},{12,14},{14,12},{16,18},{18,... | collective-permute-start | bytes 393224 | tf_op jit(solution)/shard_map/ppermute | solution.py:318
  27.2 20.5 %copy-start.2 = (bf16[4,128,128]{2,1,0:T(8,128)(2,1)}, bf16[4,128,128]{2,1,0:T(8,128)(2,1)S(1)}, u32[]{:S(2)}) copy-start(bf16[4,128,128]{2,1,0:T(8,128)(2,1)S(1)} %pad_maximum_fusion.4.refs_2_) | copy-start | bytes 393220
  27.2 6.5 %collective-permute-start.7 = (bf16[4,128,128]{2,1,0:T(8,128)(2,1)S(1)}, bf16[4,128,128]{2,1,0:T(8,128)(2,1)S(1)}, u32[]{:S(2)}, u32[]{:S(2)}) collective-permute-start(bf16[4,128,128]{2,1,0:T(8,128)(2,1)S(1)} %pad_maximum_fusion.4.refs_2_), channel_id=1, source_target_pairs={{0,2},{2,0},{4,6},{6,4},{8,10},{10,8},{12,14},{14,12},{16,18},{18,... | collective-permute-start | bytes 393224 | tf_op jit(solution)/shard_map/ppermute | solution.py:318
  27.9 24.6 %collective-permute-start.10 = (bf16[4,128,128]{2,1,0:T(8,128)(2,1)S(1)}, bf16[4,128,128]{2,1,0:T(8,128)(2,1)S(1)}, u32[]{:S(2)}, u32[]{:S(2)}) collective-permute-start(bf16[4,128,128]{2,1,0:T(8,128)(2,1)S(1)} %get-tuple-element.32), channel_id=1, source_target_pairs={{0,6},{2,4},{4,2},{6,0},{8,14},{10,12},{12,10},{14,8},{16,22},{18,... | collective-permute-start | bytes 393224 | tf_op jit(solution)/shard_map/ppermute | solution.py:318
  29.4 23.1 %collective-permute-start.9 = (bf16[4,128,128]{2,1,0:T(8,128)(2,1)S(1)}, bf16[4,128,128]{2,1,0:T(8,128)(2,1)S(1)}, u32[]{:S(2)}, u32[]{:S(2)}) collective-permute-start(bf16[4,128,128]{2,1,0:T(8,128)(2,1)S(1)} %get-tuple-element.33), channel_id=1, source_target_pairs={{0,4},{2,6},{4,0},{6,2},{8,12},{10,14},{12,8},{14,10},{16,20},{18,... | collective-permute-start | bytes 393224 | tf_op jit(solution)/shard_map/ppermute | solution.py:318
  30.9 16.9 %copy-start.3 = (bf16[4,128,128]{2,1,0:T(8,128)(2,1)}, bf16[4,128,128]{2,1,0:T(8,128)(2,1)S(1)}, u32[]{:S(2)}) copy-start(bf16[4,128,128]{2,1,0:T(8,128)(2,1)S(1)} %collective-permute-done.3.refs_1_) | copy-start | bytes 393220
  30.9 21.6 %collective-permute-start.12 = (bf16[4,128,128]{2,1,0:T(8,128)(2,1)S(1)}, bf16[4,128,128]{2,1,0:T(8,128)(2,1)S(1)}, u32[]{:S(2)}, u32[]{:S(2)}) collective-permute-start(bf16[4,128,128]{2,1,0:T(8,128)(2,1)S(1)} %pad_maximum_fusion.4.refs_2_), channel_id=1, source_target_pairs={{0,6},{2,4},{4,2},{6,0},{8,14},{10,12},{12,10},{14,8},{16,22},{18,... | collective-permute-start | bytes 393224 | tf_op jit(solution)/shard_map/ppermute | solution.py:318
  33.7 14.0 %copy-start.7 = (bf16[4,128,128]{2,1,0:T(8,128)(2,1)}, bf16[4,128,128]{2,1,0:T(8,128)(2,1)S(1)}, u32[]{:S(2)}) copy-start(bf16[4,128,128]{2,1,0:T(8,128)(2,1)S(1)} %collective-permute-done.7.refs_3_) | copy-start | bytes 393220
  33.7 18.8 %collective-permute-start.11 = (bf16[4,128,128]{2,1,0:T(8,128)(2,1)S(1)}, bf16[4,128,128]{2,1,0:T(8,128)(2,1)S(1)}, u32[]{:S(2)}, u32[]{:S(2)}) collective-permute-start(bf16[4,128,128]{2,1,0:T(8,128)(2,1)S(1)} %pad_maximum_fusion.4.refs_2_), channel_id=1, source_target_pairs={{0,4},{2,6},{4,0},{6,2},{8,12},{10,14},{12,8},{14,10},{16,20},{18,... | collective-permute-start | bytes 393224 | tf_op jit(solution)/shard_map/ppermute | solution.py:318
  52.4 0.7 copy-start.4
  52.4 11.5 %collective-permute-start.8 = (bf16[512,512]{1,0:T(8,128)(2,1)}, bf16[512,512]{1,0:T(8,128)(2,1)S(1)}, u32[]{:S(2)}, u32[]{:S(2)}) collective-permute-start(bf16[512,512]{1,0:T(8,128)(2,1)} %cross_levels.2.refs_0_), channel_id=1, source_target_pairs={{0,1},{1,0},{2,3},{3,2},{4,5},{5,4},{6,7},{7,6},{8,9},{9,8},{10,11... | collective-permute-start | bytes 1572872 | tf_op jit(solution)/shard_map/ppermute | solution.py:315
  52.5 0.7 copy-start.6
  52.5 0.7 copy-start.8
  57.9 6.0 %collective-permute-start.13 = (bf16[512,512]{1,0:T(8,128)(2,1)}, bf16[512,512]{1,0:T(8,128)(2,1)S(1)}, u32[]{:S(2)}, u32[]{:S(2)}) collective-permute-start(bf16[512,512]{1,0:T(8,128)(2,1)} %cross_levels.3.refs_1_), channel_id=1, source_target_pairs={{0,1},{1,0},{2,3},{3,2},{4,5},{5,4},{6,7},{7,6},{8,9},{9,8},{10,11... | collective-permute-start | bytes 1572872 | tf_op jit(solution)/shard_map/ppermute | solution.py:315
  63.9 0.8 %copy-start = (bf16[512,512]{1,0:T(8,128)(2,1)}, bf16[512,512]{1,0:T(8,128)(2,1)S(1)}, u32[]{:S(2)}) copy-start(bf16[512,512]{1,0:T(8,128)(2,1)S(1)} %collective-permute-done.8.refs_0_) | copy-start | bytes 1572868
  63.9 1.0 %copy-start.1 = (bf16[512,512]{1,0:T(8,128)(2,1)}, bf16[512,512]{1,0:T(8,128)(2,1)S(1)}, u32[]{:S(2)}) copy-start(bf16[512,512]{1,0:T(8,128)(2,1)S(1)} %collective-permute-done.13.refs_1_) | copy-start | bytes 1572868
  (1 other events, 0.6 us)

commit v3 on v0

v3 whole, which is shorter than its diff:
```python
import functools
import math

import jax
import jax.numpy as jnp
import numpy as np
from jax import lax
from jax.experimental import pallas as pl
from jax.experimental.pallas import tpu as pltpu
from jax.sharding import PartitionSpec as P

STRETCHES_DEV = 4
ROPE_BASE = 500000.0
NORM_EPS = 1e-06
FETCH_LIMIT = 59 << 20
LOCAL_LIMIT = 40 << 20
SMALL_LIMIT = 20 << 20
FINE = 16

F32 = jnp.float32
BF16 = jnp.bfloat16


def angle_rows(positions, head_dim):
    half_dim = head_dim // 2
    frequency = np.exp(np.arange(half_dim) * (-2.0 * math.log(ROPE_BASE) / head_dim))
    angles = np.asarray(positions, np.float64)[:, None] * frequency[None, :]
    cosine, sine = np.cos(angles), np.sin(angles)
    return [
        np.concatenate([cosine, cosine], axis=1).astype(np.float32),
        np.concatenate([-sine, sine], axis=1).astype(np.float32),
    ]


def level_scale(level_index, stretch_len):
    if level_index == 0:
        return stretch_len ** (-0.5)
    return (2 ** (level_index - 1) * stretch_len) ** (-0.5)


def quarter_of(slot, slots):
    return slot ^ (lax.axis_index("ctx") & (slots - 1))


def turn_sum(cos_a, sin_a, cos_b, sin_b):
    return cos_a * cos_b - sin_a * sin_b, sin_a * cos_b + cos_a * sin_b


def fill_angles(angle_ref, shard_index, n_ctx, cos_ref, sin_ref):
    coarse = cos_ref.shape[0] // FINE
    fine_cos, fine_sin = angle_ref[0:FINE, :], angle_ref[FINE : 2 * FINE, :]
    first = 2 * FINE
    coarse_cos = angle_ref[first : first + coarse, :]
    coarse_sin = angle_ref[first + coarse : first + 2 * coarse, :]
    first += 2 * coarse
    base_cos = angle_ref[pl.ds(first + shard_index, 1), :]
    base_sin = angle_ref[pl.ds(first + n_ctx + shard_index, 1), :]
    coarse_cos, coarse_sin = turn_sum(coarse_cos, coarse_sin, base_cos, base_sin)
    for index in range(coarse):
        rows = slice(index * FINE, (index + 1) * FINE)
        cos_ref[rows, :], sin_ref[rows, :] = turn_sum(
            coarse_cos[index : index + 1, :], coarse_sin[index : index + 1, :], fine_cos, fine_sin
        )


def rotated(vectors, cosine, sine):
    wide = vectors.astype(F32)
    half = wide.shape[-1] // 2
    return (wide * cosine + pltpu.roll(wide, half, 1) * sine).astype(BF16)


def dot_tn(a, b):
    return lax.dot_general(a, b, (((0,), (0,)), ((), ())), preferred_element_type=F32)


def dot_nt(a, b):
    return lax.dot_general(a, b, (((1,), (1,)), ((), ())), preferred_element_type=F32)


def dot_nn(a, b):
    return jnp.dot(a, b, preferred_element_type=F32)


def local_plan(stretches):
    plan = []
    for stretch in range(stretches):
        row = []
        for bit in range(stretches.bit_length() - 1):
            if stretch >> bit & 1:
                end = stretch >> bit << bit
                row.append((bit, tuple(range(end - (1 << bit), end))))
        plan.append(row)
    return plan


def state_kernel(
    slots,
    head_dim,
    n_ctx,
    angle_hbm,
    query_hbm,
    key_hbm,
    value_hbm,
    query_out,
    value_out,
    key_out,
    cos_out,
    sin_out,
    bucket_out,
    *refs,
):
    total_outs = refs[:slots]
    key_raw, angle_ref, sems = refs[slots:]
    tok_rows, model_width = key_raw.shape
    width = model_width // slots

    def fetch(source, target, slot, sem):
        start = pl.multiple_of(quarter_of(slot, slots) * width, width)
        return pltpu.make_async_copy(
            source.at[:, pl.ds(start, width)], target.at[:, pl.ds(slot * width, width)], sem
        )

    angles_in = pltpu.make_async_copy(angle_hbm, angle_ref, sems.at[3, 0])
    angles_in.start()
    order = list(range(slots - 1, -1, -1))
    copies = {}
    for kind, (source, target) in enumerate(
        ((key_hbm, key_raw), (value_hbm, value_out), (query_hbm, query_out))
    ):
        for slot in order:
            copies[kind, slot] = fetch(source, target, slot, sems.at[kind, slot])
    for slot in order:
        copies[0, slot].start()
        copies[1, slot].start()
    for slot in range(slots):
        copies[2, slot].start()
    angles_in.wait()
    fill_angles(angle_ref, lax.axis_index("ctx"), n_ctx, cos_out, sin_out)

    stretch_len = tok_rows // STRETCHES_DEV
    groups = bucket_groups()
    quarter_heads = width // head_dim
    for slot in order:
        copies[0, slot].wait()
        copies[1, slot].wait()
        heads = range(slot * quarter_heads, (slot + 1) * quarter_heads)
        turned, states = {}, {}
        for head in heads:
            cols = slice(head * head_dim, (head + 1) * head_dim)
            for stretch in range(STRETCHES_DEV):
                rows = slice(stretch * stretch_len, (stretch + 1) * stretch_len)
                block = rotated(key_raw[rows, cols], cos_out[rows, :], sin_out[rows, :])
                turned[head, stretch] = block
                states[head, stretch] = dot_tn(block, value_out[rows, cols])
        for head in heads:
            cols = slice(head * head_dim, (head + 1) * head_dim)
            for stretch in range(STRETCHES_DEV):
                rows = slice(stretch * stretch_len, (stretch + 1) * stretch_len)
                key_out[rows, cols] = turned[head, stretch]
            sums = {}
            for group, members in enumerate(groups):
                sums[members] = sum(states[head, m] for m in members)
                bucket_out[head, group] = sums[members].astype(BF16)
            total = sum(states[head, m] for m in range(STRETCHES_DEV))
            total_outs[slot][head - heads[0]] = total.astype(BF16)
    for slot in range(slots):
        copies[2, slot].wait()


def bucket_groups():
    groups = []
    for row in local_plan(STRETCHES_DEV):
        for _, members in row:
            if members not in groups:
                groups.append(members)
    return groups


def fill_one_hot(index_ref, one_hot_ref):
    table_rows = one_hot_ref.shape[0] // 3
    rows = lax.broadcasted_iota(jnp.int32, one_hot_ref.shape, 0)
    rows = lax.rem(rows, table_rows)
    one_hot_ref[...] = jnp.where(rows == index_ref[...], 1.0, 0.0).astype(BF16)


def exact_parts(table):
    high = table.astype(BF16)
    rest = table - high.astype(F32)
    middle = rest.astype(BF16)
    low = (rest - middle.astype(F32)).astype(BF16)
    return jnp.concatenate([high, middle, low], axis=1)


def fetch_weight(slots, weight_hbm, weight_out, sems):
    rows = weight_out.shape[0] // slots
    out_cols = weight_out.shape[1]
    column = pl.multiple_of(lax.axis_index("head") * out_cols, out_cols)
    copies = []
    for slot in range(slots):
        start = pl.multiple_of(quarter_of(slot, slots) * rows, rows)
        copies.append(
            pltpu.make_async_copy(
                weight_hbm.at[pl.ds(start, rows), pl.ds(column, out_cols)],
                weight_out.at[pl.ds(slot * rows, rows), :],
                sems.at[slot],
            )
        )
        copies[-1].start()
    return copies


def local_levels(
    head_dim, first_head, query_ref, key_ref, value_ref, cos_ref, sin_ref, bucket_ref,
    weight_ref, query_out, combined_out
):
    tok_rows, width = query_out.shape
    stretch_len = tok_rows // STRETCHES_DEV
    groups = bucket_groups()
    shape = (stretch_len, stretch_len)
    causal = lax.broadcasted_iota(jnp.int32, shape, 0) >= lax.broadcasted_iota(jnp.int32, shape, 1)
    stride = weight_ref.shape[1] // bucket_ref.shape[0]
    spans = [
        slice(stretch * stretch_len, (stretch + 1) * stretch_len)
        for stretch in range(STRETCHES_DEV)
    ]
    plan = local_plan(STRETCHES_DEV)
    for spot in range(width // head_dim):
        head = first_head + spot
        cols = slice(head * head_dim, (head + 1) * head_dim)
        outs = slice(spot * head_dim, (spot + 1) * head_dim)
        weights = weight_ref[:, head * stride : head * stride + len(plan)]
        turned = [
            rotated(query_ref[rows, cols], cos_ref[rows, :], sin_ref[rows, :]) for rows in spans
        ]
        scores = [dot_nt(turned[i], key_ref[rows, cols]) for i, rows in enumerate(spans)]
        reads = [
            [
                (bit, dot_nn(turned[i], bucket_ref[head, groups.index(members)]))
                for bit, members in plan[i]
            ]
            for i in range(STRETCHES_DEV)
        ]
        scores = [jnp.where(causal, block, 0.0).astype(BF16) for block in scores]
        totals = [dot_nn(scores[i], value_ref[rows, cols]) for i, rows in enumerate(spans)]
        for i, rows in enumerate(spans):
            totals[i] = weights[rows, 0:1] * totals[i]
            for bit, read in reads[i]:
                totals[i] = totals[i] + weights[rows, bit + 1 : bit + 2] * read
        for i, rows in enumerate(spans):
            query_out[rows, outs] = turned[i]
            combined_out[rows, outs] = totals[i]


def first_local_kernel(
    slots,
    head_dim,
    levels,
    index_ref,
    table_ref,
    out_weight_hbm,
    query_ref,
    key_ref,
    value_ref,
    cos_ref,
    sin_ref,
    bucket_ref,
    weight_out,
    out_weight_out,
    query_out,
    combined_out,
    one_hot_ref,
    sems,
):
    copies = fetch_weight(slots, out_weight_hbm, out_weight_out, sems)
    fill_one_hot(index_ref, one_hot_ref)
    quarter_heads = table_ref.shape[1] // slots
    table_rows = table_ref.shape[2]
    stride = weight_out.shape[1] // table_ref.shape[1]
    stretch_len = weight_out.shape[0] // STRETCHES_DEV
    level = lax.broadcasted_iota(jnp.int32, (levels, table_rows), 0)
    scale = jnp.zeros((levels, table_rows), F32)
    for index in range(levels):
        scale = jnp.where(level == index, level_scale(index, stretch_len), scale)
    tables = []
    for slot in range(slots):
        for spot in range(quarter_heads):
            head = quarter_of(slot, slots) * quarter_heads + spot
            tables.append(table_ref[:, pl.ds(head, 1), :].reshape(levels, table_rows) * scale)
            if stride > levels:
                tables.append(jnp.zeros((stride - levels, table_rows), F32))
    parts = exact_parts(jnp.concatenate(tables, axis=0))
    weight_out[...] = dot_nn(parts, one_hot_ref[...]).T
    local_levels(
        head_dim, 0, query_ref, key_ref, value_ref, cos_ref, sin_ref, bucket_ref,
        weight_out, query_out, combined_out
    )
    for copy in copies:
        copy.wait()


def second_local_kernel(
    slots,
    head_dim,
    out_weight_hbm,
    query_ref,
    key_ref,
    value_ref,
    cos_ref,
    sin_ref,
    bucket_ref,
    weight_ref,
    out_weight_out,
    query_out,
    combined_out,
    sems,
):
    copies = fetch_weight(slots, out_weight_hbm, out_weight_out, sems)
    local_levels(
        head_dim, bucket_ref.shape[0] // 2, query_ref, key_ref, value_ref, cos_ref,
        sin_ref, bucket_ref, weight_ref, query_out, combined_out
    )
    for copy in copies:
        copy.wait()


def low_kernel(slots, low_bits, *refs):
    parts = [ref[...].astype(F32) for ref in refs[:slots]]
    total_out, *low_outs = refs[slots:]
    quarter_heads = parts[0].shape[0]
    total_out[...] = sum(parts).astype(BF16)
    for by in range(slots):
        for bit in range(low_bits):
            members = [m ^ by for m in range(slots) if m >> bit == 1]
            rows = slice(bit * quarter_heads, (bit + 1) * quarter_heads)
            low_outs[by][rows] = sum(parts[m] for m in members).astype(BF16)


def high_kernel(first_bit, bit_counts, *refs):
    *back_refs, out_ref = refs
    shard_index = lax.axis_index("ctx")
    quarter_heads = back_refs[0].shape[0]
    spot = 0
    level = 0
    for bits in bit_counts:
        radix = 1 << bits
        back = [ref[...].astype(F32) for ref in back_refs[spot : spot + radix - 1]]
        spot += radix - 1
        digit = shard_index >> (first_bit + level) & (radix - 1)
        out_ref[level * quarter_heads : (level + 1) * quarter_heads] = back[0].astype(BF16)
        level += 1
        if bits == 2:
            both = jnp.where(digit == 2, back[0] + back[1], back[1] + back[2])
            out_ref[level * quarter_heads : (level + 1) * quarter_heads] = both.astype(BF16)
            level += 1


def cross_kernel(
    first_slot,
    slots,
    all_slots,
    head_dim,
    levels,
    low_levels,
    high_levels,
    combined_ref,
    query_ref,
    weight_ref,
    gain_ref,
    *refs,
):
    low_refs = refs[:slots]
    high_refs = refs[slots : 2 * slots]
    hidden_out = refs[2 * slots]
    quarter_heads = hidden_out.shape[1] // head_dim // slots
    stride = weight_ref.shape[1] // (all_slots * quarter_heads)
    shard_index = lax.axis_index("ctx")
    cross_levels = low_levels + high_levels
    present = [(shard_index >> bit & 1).astype(F32) for bit in range(cross_levels)]
    for slot in range(slots):
        for spot in range(quarter_heads):
            here = slot * quarter_heads + spot
            head = first_slot * quarter_heads + here
            cols = slice(here * head_dim, (here + 1) * head_dim)
            total = combined_ref[:, cols]
            queries = query_ref[:, cols]
            for level in range(cross_levels):
                if level < low_levels:
                    bucket = low_refs[slot][level * quarter_heads + spot]
                else:
                    bucket = high_refs[slot][(level - low_levels) * quarter_heads + spot]
                column = head * stride + levels - cross_levels + level
                weight = weight_ref[:, column : column + 1] * present[level]
                total = total + weight * dot_nn(queries, bucket)
            mean_square = jnp.mean(total * total, axis=-1, keepdims=True)
            source = quarter_of(first_slot + slot, all_slots) * quarter_heads + spot
            gain = gain_ref[pl.ds(source, 1), :]
            normed = total * lax.rsqrt(mean_square + NORM_EPS) * gain
            hidden_out[:, cols] = normed.astype(BF16)


def early_kernel(tile, own_first, own_second, other_first, own_weight, other_weight, out_ref):
    depth = own_first.shape[1]
    for start in range(0, out_ref.shape[1], tile):
        cols = slice(start, start + tile)
        out_ref[:, cols] = (
            dot_nn(own_first[...], own_weight[0:depth, cols])
            + dot_nn(own_second[...], own_weight[depth:, cols])
            + dot_nn(other_first[...], other_weight[0:depth, cols])
        )


def late_kernel(tile, other_second, other_weight, part_ref, out_hbm, out_ref, sems):
    depth = other_second.shape[1]
    copies = []
    for index, start in enumerate(range(0, out_ref.shape[1], tile)):
        cols = slice(start, start + tile)
        total = part_ref[:, cols] + dot_nn(other_second[...], other_weight[depth:, cols])
        out_ref[:, cols] = total.astype(BF16)
        copies.append(
            pltpu.make_async_copy(out_ref.at[:, cols], out_hbm.at[:, cols], sems.at[index])
        )
        copies[-1].start()
    for copy in copies:
        copy.wait()


def call(kernel, name, operands, in_spaces, out_shapes, out_spaces, scratch, limit, flops, size):
    return pl.pallas_call(
        kernel,
        in_specs=[pl.BlockSpec(memory_space=space) for space in in_spaces],
        out_specs=[pl.BlockSpec(memory_space=space) for space in out_spaces],
        out_shape=out_shapes,
        scratch_shapes=scratch,
        compiler_params=pltpu.CompilerParams(vmem_limit_bytes=limit),
        cost_estimate=pl.CostEstimate(
            flops=int(flops), bytes_accessed=int(size), transcendentals=0
        ),
        name=name,
    )(*operands)


def local(queries, key_vectors, values, level_table, weight_index, norm_gain, out_weight):
    tok_rows, model_width = queries.shape
    table_rows, heads_here, levels = level_table.shape
    head_dim = model_width // heads_here
    stretch_len = tok_rows // STRETCHES_DEV
    n_ctx = lax.axis_size("ctx")
    n_head = lax.axis_size("head")
    ctx_bits = n_ctx.bit_length() - 1
    group_count = len(bucket_groups())
    low_bits = min(2, ctx_bits)
    high_bits = ctx_bits - low_bits
    slots = 1 << low_bits
    quarter_heads = heads_here // slots
    chunk = slots // 2
    half_width = model_width // 2
    out_cols = out_weight.shape[1] // n_head
    ANY, VMEM = pl.ANY, pltpu.VMEM

    def swap_heads(block):
        return lax.ppermute(block, "head", [(i, i ^ 1) for i in range(n_head)])

    def swap_low(block, by):
        return lax.ppermute(block, "ctx", [(i, i ^ by) for i in range(n_ctx)])

    coarse = tok_rows // FINE
    angles = np.concatenate(
        angle_rows(np.arange(FINE), head_dim)
        + angle_rows(np.arange(coarse) * FINE, head_dim)
        + angle_rows(np.arange(n_ctx) * tok_rows, head_dim)
    )
    head_macs = tok_rows * head_dim * head_dim
    block_bytes = tok_rows * model_width * 2

    def share(count=quarter_heads):
        return VMEM((count, head_dim, head_dim), BF16)

    block = VMEM((tok_rows, model_width), BF16)
    angle_block = VMEM((tok_rows, head_dim), F32)
    moved, moved_values, keys, cosine, sine, local_states, *shares = call(
        functools.partial(state_kernel, slots, head_dim, n_ctx),
        "states",
        (angles, queries, key_vectors, values),
        [ANY] * 4,
        [
            block,
            block,
            block,
            angle_block,
            angle_block,
            VMEM((heads_here, group_count, head_dim, head_dim), BF16),
        ]
        + [share()] * slots,
        [VMEM] * (6 + slots),
        [block, VMEM(angles.shape, F32), pltpu.SemaphoreType.DMA((4, slots))],
        FETCH_LIMIT,
        4 * head_macs * heads_here,
        4 * block_bytes,
    )

    out_weight, shares = lax.optimization_barrier((out_weight, shares))
    parts = [shares[0]] + [swap_low(shares[by], by) for by in range(1, slots)]
    other_weight = swap_heads(out_weight)

    half = VMEM((tok_rows, half_width), BF16)
    half_wide = VMEM((tok_rows, half_width), F32)
    weight_block = VMEM((model_width, out_cols), BF16)
    stride = -(-levels // 8) * 8
    level_block = VMEM((tok_rows, heads_here * stride), F32)
    inputs = (moved, keys, moved_values, cosine, sine, local_states)
    level_weights, own_weight, first_queries, first_combined = call(
        functools.partial(first_local_kernel, slots, head_dim, levels),
        "local_levels_first",
        (weight_index.reshape(1, tok_rows), level_table.transpose(2, 1, 0), out_weight) + inputs,
        [VMEM, VMEM, ANY] + [VMEM] * len(inputs),
        [level_block, weight_block, half, half_wide],
        [VMEM] * 4,
        [VMEM((3 * table_rows, tok_rows), BF16), pltpu.SemaphoreType.DMA((slots,))],
        LOCAL_LIMIT,
        3 * head_macs * heads_here,
        2 * block_bytes,
    )
    parts, inputs, level_weights = lax.optimization_barrier((parts, inputs, level_weights))

    low_count = low_bits * quarter_heads
    high_count = high_bits * quarter_heads
    total, *low_payloads = call(
        functools.partial(low_kernel, slots, low_bits),
        "low_buckets",
        parts,
        [VMEM] * slots,
        [share()] + [share(low_count)] * slots,
        [VMEM] * (1 + slots),
        [],
        SMALL_LIMIT,
        0,
        block_bytes,
    )

    back, bit_counts = [], []
    running = total
    for low in range(low_bits, ctx_bits, 2):
        bits = min(2, ctx_bits - low)
        radix = 1 << bits
        mask = (radix - 1) << low

        def turned(index, by):
            return index & ~mask | (((index >> low) + by) & (radix - 1)) << low

        arrived = [
            lax.ppermute(running, "ctx", [(i, turned(i, by)) for i in range(n_ctx)])
            for by in range(1, radix)
        ]
        back += arrived
        bit_counts.append(bits)
        if low + bits < ctx_bits:
            running = sum(a.astype(F32) for a in [running] + arrived).astype(BF16)

    low_slots = [low_payloads[0]] + [swap_low(low_payloads[by], by) for by in range(1, slots)]
    (high,) = call(
        functools.partial(high_kernel, low_bits, tuple(bit_counts)),
        "high_buckets",
        back,
        [VMEM] * len(back),
        [share(high_count)],
        [VMEM],
        [],
        SMALL_LIMIT,
        0,
        block_bytes,
    )
    high_slots = [high] + [swap_low(high, by) for by in range(1, slots)]

    other_block, second_queries, second_combined = call(
        functools.partial(second_local_kernel, slots, head_dim),
        "local_levels_second",
        (other_weight,) + inputs + (level_weights,),
        [ANY] + [VMEM] * (len(inputs) + 1),
        [weight_block, half, half_wide],
        [VMEM] * 3,
        [pltpu.SemaphoreType.DMA((slots,))],
        LOCAL_LIMIT,
        3 * head_macs * heads_here,
        2 * block_bytes,
    )

    gain, second_combined = lax.optimization_barrier((norm_gain, second_combined))
    gain = gain.reshape(heads_here, head_dim)
    hidden = []
    for first, combined, rotated_queries in (
        (0, first_combined, first_queries),
        (chunk, second_combined, second_queries),
    ):
        operands = (
            combined,
            rotated_queries,
            level_weights,
            gain,
            *low_slots[first : first + chunk],
            *high_slots[first : first + chunk],
        )
        (piece,) = call(
            functools.partial(
                cross_kernel, first, chunk, slots, head_dim, levels, low_bits, high_bits
            ),
            "cross_levels",
            operands,
            [VMEM] * len(operands),
            [half],
            [VMEM],
            [],
            SMALL_LIMIT,
            ctx_bits * head_macs * heads_here,
            block_bytes,
        )
        hidden.append(piece)
    other_hidden = [swap_heads(piece) for piece in hidden]

    tile = min(256, out_cols)
    (part,) = call(
        functools.partial(early_kernel, tile),
        "early_projection",
        (hidden[0], hidden[1], other_hidden[0], own_weight, other_block),
        [VMEM] * 5,
        [VMEM((tok_rows, out_cols), F32)],
        [VMEM],
        [],
        SMALL_LIMIT,
        3 * tok_rows * model_width * out_cols,
        2 * block_bytes,
    )
    (mixed_out,) = call(
        functools.partial(late_kernel, tile),
        "late_projection",
        (other_hidden[1], other_block, part),
        [VMEM] * 3,
        [jax.ShapeDtypeStruct((tok_rows, out_cols), BF16)],
        [ANY],
        [VMEM((tok_rows, out_cols), BF16), pltpu.SemaphoreType.DMA((out_cols // tile,))],
        SMALL_LIMIT,
        tok_rows * model_width * out_cols,
        2 * block_bytes,
    )
    return mixed_out


def solution(mesh):
    return jax.shard_map(
        local,
        mesh=mesh,
        in_specs=(
            P("ctx", "head"),
            P("ctx", "head"),
            P("ctx", "head"),
            P(None, "head", None),
            P("ctx"),
            P("head"),
            P("head", None),
        ),
        out_specs=P("ctx", "head"),
        check_vma=False,
    )
```

time: 177 us -> 39.9 us (0.23)
  matrix products: 49 us -> 0 us
  local copies, waits for them, and re-layouts: 45.9 us -> 2.2 us
  other arithmetic: 29.4 us -> 0 us
  waiting for transfers between devices: 29.5 us -> 7.61 us
  between operations: 13.7 us -> 0.11 us
  Pallas kernels: 0 us -> 12.9 us
  starting transfers between devices: 8.63 us -> 16.9 us
    dot_general x18 -> x0, matrix products: 49 us -> none  [the longest x7 17.5 us: level_weight(): return jnp.dot(one_hot, block, precision=lax.Precision.HIGHEST)]
    unnamed x3 -> x0, other arithmetic: 15.5 us -> none
    pallas_call x0 -> x9, Pallas kernels: none -> 12.9 us  [call(): pl.pallas_call(kernel, in_specs=[pl.BlockSpec(memory_space=space) for spa...]
    ppermute x4 -> x15, waiting for transfers between devices: 20.4 us -> 7.61 us  [the longest x9 4.89 us: swap_low(): return lax.ppermute(block, 'ctx', [(i, i ^ by) for i in range(n_ctx)])]
    reshape x6 -> x0, local copies, waits for them, and re-layouts: 11.5 us -> none  [the longest x4 8.68 us: local(): cross_out = jnp.einsum('thd,hde->the', rotated_queries, cross_states[bit_...]
    transpose x4 -> x0, local copies, waits for them, and re-layouts: 10.1 us -> none  [the longest x2 5.79 us: local(): jnp.einsum('cthd,chde->cthe', query_stretches, bucket.astype(jnp.bfloat16...]
    reduce_scatter x1 -> x0, waiting for transfers between devices: 9.01 us -> none  [local(): lax.psum_scatter(partial_out.astype(jnp.bfloat16), 'head', scatter_dimens...]
    ppermute x4 -> x15, starting transfers between devices: 8.62 us -> 16.9 us  [the longest x9 10.7 us: swap_low(): return lax.ppermute(block, 'ctx', [(i, i ^ by) for i in range(n_ctx)])]
  transfers between devices with their start and end apart: 5 -> 15, of which waited for: 3 -> 7; matrix products, arithmetic and copies ran while one was open for 33% -> 0% of each run, Pallas kernels for 0% -> 21%
where the time goes in v3:
time: 39.9 us; the launch traced here: 39.8 us
  starting transfers between devices  16.9 us (42%)
  Pallas kernels  12.9 us (32%)
  waiting for transfers between devices  7.61 us (19%)
  local copies, waits for them, and re-layouts  2.2 us (6%)
    pallas_call x9, Pallas kernels, call(): pl.pallas_call(kernel, in_specs=[pl.BlockSpec(memory_space=space) for spa...  12.9 us
    ppermute x9, starting transfers between devices, swap_low(): return lax.ppermute(block, 'ctx', [(i, i ^ by) for i in range(n_ctx)])  10.7 us
    ppermute x3, starting transfers between devices, local(): lax.ppermute(running, 'ctx', [(i, turned(i, by)) for i in range(n_ctx)])  5.57 us
    ppermute x9, waiting for transfers between devices, swap_low(): return lax.ppermute(block, 'ctx', [(i, i ^ by) for i in range(n_ctx)])  4.89 us
    ppermute x3, waiting for transfers between devices, local(): lax.ppermute(running, 'ctx', [(i, turned(i, by)) for i in range(n_ctx)])  2.61 us
    unnamed x8, local copies, waits for them, and re-layouts  2.2 us
  transfers between devices with their start and end apart: 15, of which 7 were waited for; matrix products, arithmetic and copies ran while one was open for 0% of the time, Pallas kernels for 21%

profile of v3, /device:TPU:0, one launch (start us, length us, event | category | flops | bytes accessed | tf_op | source)
XLA Modules:
  0.0 39.8 jit_solution(5073535157824158769)
XLA Ops:
  0.0 3.0 %states.1 = (bf16[512,1024]{1,0:T(8,128)(2,1)S(1)}, bf16[512,1024]{1,0:T(8,128)(2,1)S(1)}, bf16[512,1024]{1,0:T(8,128)(2,1)S(1)}, f32[512,128]{1,0:T(8,128)S(1)}...) custom-call(f32[128,128]{1,0:T(8,128)} %constant.2.clone.angle_hbm, ...), custom_call_target="tpu_custom_call" | custom-call | flops 268435456 | bytes 4194304 | tf_op jit(solution)/shard_map/states/pallas_call | solution.py:428
  3.5 2.6 %collective-permute-start.1 = (bf16[2,128,128]{2,1,0:T(8,128)(2,1)S(1)}, bf16[2,128,128]{2,1,0:T(8,128)(2,1)S(1)}, u32[]{:S(2)}, u32[]{:S(2)}) collective-permute-start(bf16[2,128,128]{2,1,0:T(8,128)(2,1)S(1)} %get-tuple-element.51), channel_id=1, source_target_pairs={{0,2},{2,0},{4,6},{6,4},{8,10},{10,8},{12,14},{14,12},{16,18},{18,... | collective-permute-start | bytes 196616 | tf_op jit(solution)/shard_map/ppermute | solution.py:464
  6.1 1.5 %collective-permute-start.2 = (bf16[2,128,128]{2,1,0:T(8,128)(2,1)S(1)}, bf16[2,128,128]{2,1,0:T(8,128)(2,1)S(1)}, u32[]{:S(2)}, u32[]{:S(2)}) collective-permute-start(bf16[2,128,128]{2,1,0:T(8,128)(2,1)S(1)} %get-tuple-element.52), channel_id=1, source_target_pairs={{0,4},{2,6},{4,0},{6,2},{8,12},{10,14},{12,8},{14,10},{16,20},{18,... | collective-permute-start | bytes 196616 | tf_op jit(solution)/shard_map/ppermute | solution.py:464
  7.6 2.2 %copy-done = bf16[1024,2048]{1,0:T(8,128)(2,1)S(1)} copy-done((bf16[1024,2048]{1,0:T(8,128)(2,1)S(1)}, bf16[1024,2048]{1,0:T(8,128)(2,1)}, u32[]{:S(2)}) %copy-start) | copy-done | bytes 4194328
  9.8 1.6 %local_levels_first.1 = (f32[512,64]{1,0:T(8,128)S(1)}, bf16[1024,1024]{1,0:T(8,128)(2,1)S(1)}, bf16[512,512]{1,0:T(8,128)(2,1)S(1)}, f32[512,512]{1,0:T(8,128)S(1)}) custom-call(s32[1,512]{1,0:T(1,128)S(1)} %bitcast.6, f32[7,8,64]{2,1,0:T(8,128)S(1)} %bitcast.3, bf16[1024,2048]{1,0:T(8,128)(2,1)S(1)} %copy-done, ...), custom_call_target="tpu_custom_call" | custom-call | flops 201326592 | bytes 2097152 | tf_op jit(solution)/shard_map/local_levels_first/pallas_call | solution.py:428
  11.5 1.3 %collective-permute-done.3.refs_3_ = bf16[2,128,128]{2,1,0:T(8,128)(2,1)S(1)} collective-permute-done((bf16[2,128,128]{2,1,0:T(8,128)(2,1)S(1)}, bf16[2,128,128]{2,1,0:T(8,128)(2,1)S(1)}, u32[]{:S(2)}, u32[]{:S(2)}) %collective-permute-start.3) | collective-permute-done | bytes 65568 | tf_op jit(solution)/shard_map/ppermute | solution.py:464
  12.9 1.6 %collective-permute-start.6 = (bf16[2,128,128]{2,1,0:T(8,128)(2,1)S(1)}, bf16[2,128,128]{2,1,0:T(8,128)(2,1)S(1)}, u32[]{:S(2)}, u32[]{:S(2)}) collective-permute-start(bf16[2,128,128]{2,1,0:T(8,128)(2,1)S(1)} %get-tuple-element.78), channel_id=1, source_target_pairs={{0,8},{2,10},{4,12},{6,14},{8,16},{10,18},{12,20},{14,22},{16,24},... | collective-permute-start | bytes 196616 | tf_op jit(solution)/shard_map/ppermute | solution.py:551
  14.5 2.6 %collective-permute-start.7 = (bf16[2,128,128]{2,1,0:T(8,128)(2,1)S(1)}, bf16[2,128,128]{2,1,0:T(8,128)(2,1)S(1)}, u32[]{:S(2)}, u32[]{:S(2)}) collective-permute-start(bf16[2,128,128]{2,1,0:T(8,128)(2,1)S(1)} %get-tuple-element.78), channel_id=1, source_target_pairs={{0,16},{2,18},{4,20},{6,22},{8,24},{10,26},{12,28},{14,30},{16,0},... | collective-permute-start | bytes 196616 | tf_op jit(solution)/shard_map/ppermute | solution.py:551
  17.1 1.3 %collective-permute-start.8 = (bf16[2,128,128]{2,1,0:T(8,128)(2,1)S(1)}, bf16[2,128,128]{2,1,0:T(8,128)(2,1)S(1)}, u32[]{:S(2)}, u32[]{:S(2)}) collective-permute-start(bf16[2,128,128]{2,1,0:T(8,128)(2,1)S(1)} %get-tuple-element.78), channel_id=1, source_target_pairs={{0,24},{2,26},{4,28},{6,30},{8,0},{10,2},{12,4},{14,6},{16,8},{18,... | collective-permute-start | bytes 196616 | tf_op jit(solution)/shard_map/ppermute | solution.py:551
  18.4 0.7 %collective-permute-start.12 = (bf16[4,128,128]{2,1,0:T(8,128)(2,1)S(1)}, bf16[4,128,128]{2,1,0:T(8,128)(2,1)S(1)}, u32[]{:S(2)}, u32[]{:S(2)}) collective-permute-start(bf16[4,128,128]{2,1,0:T(8,128)(2,1)S(1)} %get-tuple-element.83), channel_id=1, source_target_pairs={{0,2},{2,0},{4,6},{6,4},{8,10},{10,8},{12,14},{14,12},{16,18},{18,... | collective-permute-start | bytes 393224 | tf_op jit(solution)/shard_map/ppermute | solution.py:464
  19.6 1.6 %collective-permute-done.7.refs_1_ = bf16[2,128,128]{2,1,0:T(8,128)(2,1)S(1)} collective-permute-done((bf16[2,128,128]{2,1,0:T(8,128)(2,1)S(1)}, bf16[2,128,128]{2,1,0:T(8,128)(2,1)S(1)}, u32[]{:S(2)}, u32[]{:S(2)}) %collective-permute-start.7) | collective-permute-done | bytes 65568 | tf_op jit(solution)/shard_map/ppermute | solution.py:551
  21.2 0.5 %collective-permute-done.8.refs_2_ = bf16[2,128,128]{2,1,0:T(8,128)(2,1)S(1)} collective-permute-done((bf16[2,128,128]{2,1,0:T(8,128)(2,1)S(1)}, bf16[2,128,128]{2,1,0:T(8,128)(2,1)S(1)}, u32[]{:S(2)}, u32[]{:S(2)}) %collective-permute-start.8) | collective-permute-done | bytes 65568 | tf_op jit(solution)/shard_map/ppermute | solution.py:551
  21.7 0.9 %collective-permute-start.13 = (bf16[4,128,128]{2,1,0:T(8,128)(2,1)S(1)}, bf16[4,128,128]{2,1,0:T(8,128)(2,1)S(1)}, u32[]{:S(2)}, u32[]{:S(2)}) collective-permute-start(bf16[4,128,128]{2,1,0:T(8,128)(2,1)S(1)} %high_buckets.1.refs_2_), channel_id=1, source_target_pairs={{0,2},{2,0},{4,6},{6,4},{8,10},{10,8},{12,14},{14,12},{16,18},{18,... | collective-permute-start | bytes 393224 | tf_op jit(solution)/shard_map/ppermute | solution.py:464
  22.7 1.5 %collective-permute-start.4 = (bf16[4,128,128]{2,1,0:T(8,128)(2,1)S(1)}, bf16[4,128,128]{2,1,0:T(8,128)(2,1)S(1)}, u32[]{:S(2)}, u32[]{:S(2)}) collective-permute-start(bf16[4,128,128]{2,1,0:T(8,128)(2,1)S(1)} %get-tuple-element.76), channel_id=1, source_target_pairs={{0,4},{2,6},{4,0},{6,2},{8,12},{10,14},{12,8},{14,10},{16,20},{18,... | collective-permute-start | bytes 393224 | tf_op jit(solution)/shard_map/ppermute | solution.py:464
  24.2 1.1 %collective-permute-start.5 = (bf16[4,128,128]{2,1,0:T(8,128)(2,1)S(1)}, bf16[4,128,128]{2,1,0:T(8,128)(2,1)S(1)}, u32[]{:S(2)}, u32[]{:S(2)}) collective-permute-start(bf16[4,128,128]{2,1,0:T(8,128)(2,1)S(1)} %get-tuple-element.77), channel_id=1, source_target_pairs={{0,6},{2,4},{4,2},{6,0},{8,14},{10,12},{12,10},{14,8},{16,22},{18,... | collective-permute-start | bytes 393224 | tf_op jit(solution)/shard_map/ppermute | solution.py:464
  25.3 0.9 %collective-permute-start.9 = (bf16[4,128,128]{2,1,0:T(8,128)(2,1)S(1)}, bf16[4,128,128]{2,1,0:T(8,128)(2,1)S(1)}, u32[]{:S(2)}, u32[]{:S(2)}) collective-permute-start(bf16[4,128,128]{2,1,0:T(8,128)(2,1)S(1)} %high_buckets.1.refs_2_), channel_id=1, source_target_pairs={{0,4},{2,6},{4,0},{6,2},{8,12},{10,14},{12,8},{14,10},{16,20},{18,... | collective-permute-start | bytes 393224 | tf_op jit(solution)/shard_map/ppermute | solution.py:464
  26.2 1.4 %local_levels_second.1 = (bf16[1024,1024]{1,0:T(8,128)(2,1)S(1)}, bf16[512,512]{1,0:T(8,128)(2,1)S(1)}, f32[512,512]{1,0:T(8,128)S(1)}) custom-call(bf16[1024,2048]{1,0:T(8,128)(2,1)S(1)} %collective-permute-done.out_weight_hbm, bf16[512,1024]{1,0:T(8,128)(2,1)S(1)} %get-tuple-element.61.query_ref, bf16[512,1024]{1,0:T(8,128)(2,1)S(1)} %get-tuple-element.62.key_ref, ...), custom_call_target="tpu_custom_call" | custom-call | flops 201326592 | bytes 2097152 | tf_op jit(solution)/shard_map/local_levels_second/pallas_call | solution.py:428
  27.6 1.5 %collective-permute-start.10 = (bf16[4,128,128]{2,1,0:T(8,128)(2,1)S(1)}, bf16[4,128,128]{2,1,0:T(8,128)(2,1)S(1)}, u32[]{:S(2)}, u32[]{:S(2)}) collective-permute-start(bf16[4,128,128]{2,1,0:T(8,128)(2,1)S(1)} %high_buckets.1.refs_2_), channel_id=1, source_target_pairs={{0,6},{2,4},{4,2},{6,0},{8,14},{10,12},{12,10},{14,8},{16,22},{18,... | collective-permute-start | bytes 393224 | tf_op jit(solution)/shard_map/ppermute | solution.py:464
  29.1 1.7 %cross_levels.3.own_first = bf16[512,512]{1,0:T(8,128)(2,1)S(1)} custom-call(f32[512,512]{1,0:T(8,128)S(1)} %get-tuple-element.80.combined_ref, bf16[512,512]{1,0:T(8,128)(2,1)S(1)} %get-tuple-element.81.query_ref, f32[512,64]{1,0:T(8,128)S(1)} %get-tuple-element.67.weight_ref, f32[8,128]{1,0:T(8,128)S(1)} %bitcast.4, ...), custom_call_target="tpu_custom_call" | custom-call | flops 268435456 | bytes 1048576 | tf_op jit(solution)/shard_map/cross_levels/pallas_call | solution.py:428
  30.9 0.8 %collective-permute-done.4.refs_0_ = bf16[4,128,128]{2,1,0:T(8,128)(2,1)S(1)} collective-permute-done((bf16[4,128,128]{2,1,0:T(8,128)(2,1)S(1)}, bf16[4,128,128]{2,1,0:T(8,128)(2,1)S(1)}, u32[]{:S(2)}, u32[]{:S(2)}) %collective-permute-start.4) | collective-permute-done | bytes 131104 | tf_op jit(solution)/shard_map/ppermute | solution.py:464
  31.7 2.8 %collective-permute-done.9.refs_2_ = bf16[4,128,128]{2,1,0:T(8,128)(2,1)S(1)} collective-permute-done((bf16[4,128,128]{2,1,0:T(8,128)(2,1)S(1)}, bf16[4,128,128]{2,1,0:T(8,128)(2,1)S(1)}, u32[]{:S(2)}, u32[]{:S(2)}) %collective-permute-start.9) | collective-permute-done | bytes 131104 | tf_op jit(solution)/shard_map/ppermute | solution.py:464
  34.5 1.7 %cross_levels.2.own_second = bf16[512,512]{1,0:T(8,128)(2,1)S(1)} custom-call(f32[512,512]{1,0:T(8,128)S(1)} %get-tuple-element.69.combined_ref, bf16[512,512]{1,0:T(8,128)(2,1)S(1)} %get-tuple-element.70.query_ref, f32[512,64]{1,0:T(8,128)S(1)} %get-tuple-element.67.weight_ref, f32[8,128]{1,0:T(8,128)S(1)} %bitcast.5, ...), custom_call_target="tpu_custom_call" | custom-call | flops 268435456 | bytes 1048576 | tf_op jit(solution)/shard_map/cross_levels/pallas_call | solution.py:428
  36.3 1.8 %early_projection.1.part_ref = f32[512,1024]{1,0:T(8,128)S(1)} custom-call(bf16[512,512]{1,0:T(8,128)(2,1)S(1)} %cross_levels.3.own_first, bf16[512,512]{1,0:T(8,128)(2,1)S(1)} %cross_levels.2.own_second, bf16[512,512]{1,0:T(8,128)(2,1)S(1)} %collective-permute-done.14.other_first, bf16[1024,1024]{1,0:T(8,128)(2,1)S(1)} %get-tuple-element.84.own_weight, ...), custom_call_target="tpu_custom_call" | custom-call | flops 1610612736 | bytes 2097152 | tf_op jit(solution)/shard_map/early_projection/pallas_call | solution.py:428
  38.2 1.6 %late_projection.1 = bf16[512,1024]{1,0:T(8,128)(2,1)} custom-call(bf16[512,512]{1,0:T(8,128)(2,1)S(1)} %collective-permute-done.11.other_second, bf16[1024,1024]{1,0:T(8,128)(2,1)S(1)} %get-tuple-element.79.other_weight, f32[512,1024]{1,0:T(8,128)S(1)} %early_projection.1.part_ref), custom_call_target="tpu_custom_call" | custom-call | flops 536870912 | bytes 2097152 | tf_op jit(solution)/shard_map/late_projection/pallas_call | solution.py:428
  (23 shorter events, 1.5 us)
Async XLA Ops:
  0.0 7.6 %copy-start.3 = (s32[512]{0:T(512)S(1)}, s32[512]{0:T(512)}, u32[]{:S(2)}) copy-start(s32[512]{0:T(512)} %param.12) | copy-start | bytes 6148
  0.0 7.6 %copy-start.1 = (f32[64,8,7]{0,1,2:T(8,128)S(1)}, f32[64,8,7]{0,1,2:T(8,128)}, u32[]{:S(2)}) copy-start(f32[64,8,7]{0,1,2:T(8,128)} %param.11) | copy-start | bytes 43012
  3.0 22.3 %collective-permute-start = (bf16[1024,2048]{1,0:T(8,128)(2,1)}, bf16[1024,2048]{1,0:T(8,128)(2,1)S(1)}, u32[]{:S(2)}, u32[]{:S(2)}) collective-permute-start(bf16[1024,2048]{1,0:T(8,128)(2,1)} %out_weight_hbm), channel_id=1, source_target_pairs={{0,1},{1,0},{2,3},{3,2},{4,5},{5,4},{6,7},{7,6},{8,9},{9,8},{10,11... | collective-permute-start | bytes 12582920 | tf_op jit(solution)/shard_map/ppermute | solution.py:461
  3.5 7.9 %collective-permute-start.1 = (bf16[2,128,128]{2,1,0:T(8,128)(2,1)S(1)}, bf16[2,128,128]{2,1,0:T(8,128)(2,1)S(1)}, u32[]{:S(2)}, u32[]{:S(2)}) collective-permute-start(bf16[2,128,128]{2,1,0:T(8,128)(2,1)S(1)} %get-tuple-element.51), channel_id=1, source_target_pairs={{0,2},{2,0},{4,6},{6,4},{8,10},{10,8},{12,14},{14,12},{16,18},{18,... | collective-permute-start | bytes 196616 | tf_op jit(solution)/shard_map/ppermute | solution.py:464
  6.1 5.4 %collective-permute-start.2 = (bf16[2,128,128]{2,1,0:T(8,128)(2,1)S(1)}, bf16[2,128,128]{2,1,0:T(8,128)(2,1)S(1)}, u32[]{:S(2)}, u32[]{:S(2)}) collective-permute-start(bf16[2,128,128]{2,1,0:T(8,128)(2,1)S(1)} %get-tuple-element.52), channel_id=1, source_target_pairs={{0,4},{2,6},{4,0},{6,2},{8,12},{10,14},{12,8},{14,10},{16,20},{18,... | collective-permute-start | bytes 196616 | tf_op jit(solution)/shard_map/ppermute | solution.py:464
  7.6 5.2 %collective-permute-start.3 = (bf16[2,128,128]{2,1,0:T(8,128)(2,1)S(1)}, bf16[2,128,128]{2,1,0:T(8,128)(2,1)S(1)}, u32[]{:S(2)}, u32[]{:S(2)}) collective-permute-start(bf16[2,128,128]{2,1,0:T(8,128)(2,1)S(1)} %get-tuple-element.53), channel_id=1, source_target_pairs={{0,6},{2,4},{4,2},{6,0},{8,14},{10,12},{12,10},{14,8},{16,22},{18,... | collective-permute-start | bytes 196616 | tf_op jit(solution)/shard_map/ppermute | solution.py:464
  7.6 2.2 %copy-start = (bf16[1024,2048]{1,0:T(8,128)(2,1)S(1)}, bf16[1024,2048]{1,0:T(8,128)(2,1)}, u32[]{:S(2)}) copy-start(bf16[1024,2048]{1,0:T(8,128)(2,1)} %out_weight_hbm) | copy-start | bytes 12582916
  12.9 6.7 %collective-permute-start.6 = (bf16[2,128,128]{2,1,0:T(8,128)(2,1)S(1)}, bf16[2,128,128]{2,1,0:T(8,128)(2,1)S(1)}, u32[]{:S(2)}, u32[]{:S(2)}) collective-permute-start(bf16[2,128,128]{2,1,0:T(8,128)(2,1)S(1)} %get-tuple-element.78), channel_id=1, source_target_pairs={{0,8},{2,10},{4,12},{6,14},{8,16},{10,18},{12,20},{14,22},{16,24},... | collective-permute-start | bytes 196616 | tf_op jit(solution)/shard_map/ppermute | solution.py:551
  14.5 6.7 %collective-permute-start.7 = (bf16[2,128,128]{2,1,0:T(8,128)(2,1)S(1)}, bf16[2,128,128]{2,1,0:T(8,128)(2,1)S(1)}, u32[]{:S(2)}, u32[]{:S(2)}) collective-permute-start(bf16[2,128,128]{2,1,0:T(8,128)(2,1)S(1)} %get-tuple-element.78), channel_id=1, source_target_pairs={{0,16},{2,18},{4,20},{6,22},{8,24},{10,26},{12,28},{14,30},{16,0},... | collective-permute-start | bytes 196616 | tf_op jit(solution)/shard_map/ppermute | solution.py:551
  17.1 4.6 %collective-permute-start.8 = (bf16[2,128,128]{2,1,0:T(8,128)(2,1)S(1)}, bf16[2,128,128]{2,1,0:T(8,128)(2,1)S(1)}, u32[]{:S(2)}, u32[]{:S(2)}) collective-permute-start(bf16[2,128,128]{2,1,0:T(8,128)(2,1)S(1)} %get-tuple-element.78), channel_id=1, source_target_pairs={{0,24},{2,26},{4,28},{6,30},{8,0},{10,2},{12,4},{14,6},{16,8},{18,... | collective-permute-start | bytes 196616 | tf_op jit(solution)/shard_map/ppermute | solution.py:551
  18.4 9.2 %collective-permute-start.12 = (bf16[4,128,128]{2,1,0:T(8,128)(2,1)S(1)}, bf16[4,128,128]{2,1,0:T(8,128)(2,1)S(1)}, u32[]{:S(2)}, u32[]{:S(2)}) collective-permute-start(bf16[4,128,128]{2,1,0:T(8,128)(2,1)S(1)} %get-tuple-element.83), channel_id=1, source_target_pairs={{0,2},{2,0},{4,6},{6,4},{8,10},{10,8},{12,14},{14,12},{16,18},{18,... | collective-permute-start | bytes 393224 | tf_op jit(solution)/shard_map/ppermute | solution.py:464
  21.7 7.4 %collective-permute-start.13 = (bf16[4,128,128]{2,1,0:T(8,128)(2,1)S(1)}, bf16[4,128,128]{2,1,0:T(8,128)(2,1)S(1)}, u32[]{:S(2)}, u32[]{:S(2)}) collective-permute-start(bf16[4,128,128]{2,1,0:T(8,128)(2,1)S(1)} %high_buckets.1.refs_2_), channel_id=1, source_target_pairs={{0,2},{2,0},{4,6},{6,4},{8,10},{10,8},{12,14},{14,12},{16,18},{18,... | collective-permute-start | bytes 393224 | tf_op jit(solution)/shard_map/ppermute | solution.py:464
  22.7 9.0 %collective-permute-start.4 = (bf16[4,128,128]{2,1,0:T(8,128)(2,1)S(1)}, bf16[4,128,128]{2,1,0:T(8,128)(2,1)S(1)}, u32[]{:S(2)}, u32[]{:S(2)}) collective-permute-start(bf16[4,128,128]{2,1,0:T(8,128)(2,1)S(1)} %get-tuple-element.76), channel_id=1, source_target_pairs={{0,4},{2,6},{4,0},{6,2},{8,12},{10,14},{12,8},{14,10},{16,20},{18,... | collective-permute-start | bytes 393224 | tf_op jit(solution)/shard_map/ppermute | solution.py:464
  24.2 4.9 %copy-start.2 = (f32[1024]{0:T(1024)S(1)}, f32[1024]{0:T(1024)}, u32[]{:S(2)}) copy-start(f32[1024]{0:T(1024)} %param.13) | copy-start | bytes 12292
  24.2 7.5 %collective-permute-start.5 = (bf16[4,128,128]{2,1,0:T(8,128)(2,1)S(1)}, bf16[4,128,128]{2,1,0:T(8,128)(2,1)S(1)}, u32[]{:S(2)}, u32[]{:S(2)}) collective-permute-start(bf16[4,128,128]{2,1,0:T(8,128)(2,1)S(1)} %get-tuple-element.77), channel_id=1, source_target_pairs={{0,6},{2,4},{4,2},{6,0},{8,14},{10,12},{12,10},{14,8},{16,22},{18,... | collective-permute-start | bytes 393224 | tf_op jit(solution)/shard_map/ppermute | solution.py:464
  25.3 9.2 %collective-permute-start.9 = (bf16[4,128,128]{2,1,0:T(8,128)(2,1)S(1)}, bf16[4,128,128]{2,1,0:T(8,128)(2,1)S(1)}, u32[]{:S(2)}, u32[]{:S(2)}) collective-permute-start(bf16[4,128,128]{2,1,0:T(8,128)(2,1)S(1)} %high_buckets.1.refs_2_), channel_id=1, source_target_pairs={{0,4},{2,6},{4,0},{6,2},{8,12},{10,14},{12,8},{14,10},{16,20},{18,... | collective-permute-start | bytes 393224 | tf_op jit(solution)/shard_map/ppermute | solution.py:464
  27.6 6.9 %collective-permute-start.10 = (bf16[4,128,128]{2,1,0:T(8,128)(2,1)S(1)}, bf16[4,128,128]{2,1,0:T(8,128)(2,1)S(1)}, u32[]{:S(2)}, u32[]{:S(2)}) collective-permute-start(bf16[4,128,128]{2,1,0:T(8,128)(2,1)S(1)} %high_buckets.1.refs_2_), channel_id=1, source_target_pairs={{0,6},{2,4},{4,2},{6,0},{8,14},{10,12},{12,10},{14,8},{16,22},{18,... | collective-permute-start | bytes 393224 | tf_op jit(solution)/shard_map/ppermute | solution.py:464
  30.8 5.5 %collective-permute-start.14 = (bf16[512,512]{1,0:T(8,128)(2,1)S(1)}, bf16[512,512]{1,0:T(8,128)(2,1)S(1)}, u32[]{:S(2)}, u32[]{:S(2)}) collective-permute-start(bf16[512,512]{1,0:T(8,128)(2,1)S(1)} %cross_levels.3.own_first), channel_id=1, source_target_pairs={{0,1},{1,0},{2,3},{3,2},{4,5},{5,4},{6,7},{7,6},{8,9},{9,8},{10,11... | collective-permute-start | bytes 1572872 | tf_op jit(solution)/shard_map/ppermute | solution.py:461
  36.2 2.0 %collective-permute-start.11 = (bf16[512,512]{1,0:T(8,128)(2,1)S(1)}, bf16[512,512]{1,0:T(8,128)(2,1)S(1)}, u32[]{:S(2)}, u32[]{:S(2)}) collective-permute-start(bf16[512,512]{1,0:T(8,128)(2,1)S(1)} %cross_levels.2.own_second), channel_id=1, source_target_pairs={{0,1},{1,0},{2,3},{3,2},{4,5},{5,4},{6,7},{7,6},{8,9},{9,8},{10,11... | collective-permute-start | bytes 1572872 | tf_op jit(solution)/shard_map/ppermute | solution.py:461

commit v4 on v3

--- a/solution.py
+++ b/solution.py
@@ -13,7 +13,7 @@
 ROPE_BASE = 500000.0
 NORM_EPS = 1e-06
 FETCH_LIMIT = 59 << 20
-LOCAL_LIMIT = 40 << 20
+LOCAL_LIMIT = 42 << 20
 SMALL_LIMIT = 20 << 20
 FINE = 16
 
@@ -191,10 +191,10 @@
     return jnp.concatenate([high, middle, low], axis=1)
 
 
-def fetch_weight(slots, weight_hbm, weight_out, sems):
+def fetch_weight(slots, head_index, weight_hbm, weight_out, sems):
     rows = weight_out.shape[0] // slots
     out_cols = weight_out.shape[1]
-    column = pl.multiple_of(lax.axis_index("head") * out_cols, out_cols)
+    column = pl.multiple_of(head_index * out_cols, out_cols)
     copies = []
     for slot in range(slots):
         start = pl.multiple_of(quarter_of(slot, slots) * rows, rows)
@@ -211,7 +211,7 @@
 
 def local_levels(
     head_dim, first_head, query_ref, key_ref, value_ref, cos_ref, sin_ref, bucket_ref,
-    weight_ref, query_out, combined_out
+    weight_ref, query_out, combined_out, low_refs=()
 ):
     tok_rows, width = query_out.shape
     stretch_len = tok_rows // STRETCHES_DEV
@@ -246,6 +246,11 @@
             totals[i] = weights[rows, 0:1] * totals[i]
             for bit, read in reads[i]:
                 totals[i] = totals[i] + weights[rows, bit + 1 : bit + 2] * read
+        if low_refs:
+            added = low_levels(
+                jnp.concatenate(turned, axis=0), head, weight_ref, bucket_ref.shape[0], low_refs
+            )
+            totals = [totals[i] + added[rows] for i, rows in enumerate(spans)]
         for i, rows in enumerate(spans):
             query_out[rows, outs] = turned[i]
             combined_out[rows, outs] = totals[i]
@@ -265,13 +270,16 @@
     sin_ref,
     bucket_ref,
     weight_out,
-    out_weight_out,
+    own_weight_out,
+    sent_weight_out,
     query_out,
     combined_out,
     one_hot_ref,
     sems,
 ):
-    copies = fetch_weight(slots, out_weight_hbm, out_weight_out, sems)
+    head_index = lax.axis_index("head")
+    copies = fetch_weight(slots, head_index, out_weight_hbm, own_weight_out, sems.at[0])
+    copies += fetch_weight(slots, head_index ^ 1, out_weight_hbm, sent_weight_out, sems.at[1])
     fill_one_hot(index_ref, one_hot_ref)
     quarter_heads = table_ref.shape[1] // slots
     table_rows = table_ref.shape[2]
@@ -298,10 +306,25 @@
         copy.wait()
 
 
+def low_levels(queries, head, weight_ref, heads, low_refs):
+    slots = len(low_refs)
+    quarter_heads = heads // slots
+    stride = weight_ref.shape[1] // heads
+    low_bits = low_refs[0].shape[0] // quarter_heads
+    first = len(local_plan(STRETCHES_DEV)[-1]) + 1
+    shard_index = lax.axis_index("ctx")
+    total = None
+    for bit in range(low_bits):
+        bucket = low_refs[head // quarter_heads][bit * quarter_heads + head % quarter_heads]
+        column = head * stride + first + bit
+        present = (shard_index >> bit & 1).astype(F32)
+        part = weight_ref[:, column : column + 1] * present * dot_nn(queries, bucket)
+        total = part if total is None else total + part
+    return total
+
+
 def second_local_kernel(
-    slots,
     head_dim,
-    out_weight_hbm,
     query_ref,
     key_ref,
     value_ref,
@@ -309,18 +332,21 @@
     sin_ref,
     bucket_ref,
     weight_ref,
-    out_weight_out,
-    query_out,
-    combined_out,
-    sems,
+    first_query_ref,
+    first_combined_ref,
+    *refs,
 ):
-    copies = fetch_weight(slots, out_weight_hbm, out_weight_out, sems)
+    *low_refs, first_combined_out, query_out, combined_out = refs
+    heads = bucket_ref.shape[0]
+    for head in range(heads // 2):
+        cols = slice(head * head_dim, (head + 1) * head_dim)
+        first_combined_out[:, cols] = first_combined_ref[:, cols] + low_levels(
+            first_query_ref[:, cols], head, weight_ref, heads, low_refs
+        )
     local_levels(
-        head_dim, bucket_ref.shape[0] // 2, query_ref, key_ref, value_ref, cos_ref,
-        sin_ref, bucket_ref, weight_ref, query_out, combined_out
-    )
-    for copy in copies:
-        copy.wait()
+        head_dim, heads // 2, query_ref, key_ref, value_ref, cos_ref, sin_ref, bucket_ref,
+        weight_ref, query_out, combined_out, low_refs
+    )
 
 
 def low_kernel(slots, low_bits, *refs):
@@ -360,7 +386,6 @@
     all_slots,
     head_dim,
     levels,
-    low_levels,
     high_levels,
     combined_ref,
     query_ref,
@@ -368,14 +393,14 @@
     gain_ref,
     *refs,
 ):
-    low_refs = refs[:slots]
-    high_refs = refs[slots : 2 * slots]
-    hidden_out = refs[2 * slots]
+    *high_refs, hidden_out = refs
     quarter_heads = hidden_out.shape[1] // head_dim // slots
     stride = weight_ref.shape[1] // (all_slots * quarter_heads)
     shard_index = lax.axis_index("ctx")
-    cross_levels = low_levels + high_levels
-    present = [(shard_index >> bit & 1).astype(F32) for bit in range(cross_levels)]
+    first_bit = all_slots.bit_length() - 1
+    present = [
+        (shard_index >> (first_bit + bit) & 1).astype(F32) for bit in range(high_levels)
+    ]
     for slot in range(slots):
         for spot in range(quarter_heads):
             here = slot * quarter_heads + spot
@@ -383,12 +408,9 @@
             cols = slice(here * head_dim, (here + 1) * head_dim)
             total = combined_ref[:, cols]
             queries = query_ref[:, cols]
-            for level in range(cross_levels):
-                if level < low_levels:
-                    bucket = low_refs[slot][level * quarter_heads + spot]
-                else:
-                    bucket = high_refs[slot][(level - low_levels) * quarter_heads + spot]
-                column = head * stride + levels - cross_levels + level
+            for level in range(high_levels):
+                bucket = high_refs[slot][level * quarter_heads + spot]
+                column = head * stride + levels - high_levels + level
                 weight = weight_ref[:, column : column + 1] * present[level]
                 total = total + weight * dot_nn(queries, bucket)
             mean_square = jnp.mean(total * total, axis=-1, keepdims=True)
@@ -498,29 +520,29 @@
         4 * block_bytes,
     )
 
-    out_weight, shares = lax.optimization_barrier((out_weight, shares))
     parts = [shares[0]] + [swap_low(shares[by], by) for by in range(1, slots)]
-    other_weight = swap_heads(out_weight)
-
     half = VMEM((tok_rows, half_width), BF16)
     half_wide = VMEM((tok_rows, half_width), F32)
     weight_block = VMEM((model_width, out_cols), BF16)
     stride = -(-levels // 8) * 8
     level_block = VMEM((tok_rows, heads_here * stride), F32)
     inputs = (moved, keys, moved_values, cosine, sine, local_states)
-    level_weights, own_weight, first_queries, first_combined = call(
+    level_weights, own_weight, sent_weight, first_queries, first_combined = call(
         functools.partial(first_local_kernel, slots, head_dim, levels),
         "local_levels_first",
         (weight_index.reshape(1, tok_rows), level_table.transpose(2, 1, 0), out_weight) + inputs,
         [VMEM, VMEM, ANY] + [VMEM] * len(inputs),
-        [level_block, weight_block, half, half_wide],
-        [VMEM] * 4,
-        [VMEM((3 * table_rows, tok_rows), BF16), pltpu.SemaphoreType.DMA((slots,))],
+        [level_block, weight_block, weight_block, half, half_wide],
+        [VMEM] * 5,
+        [VMEM((3 * table_rows, tok_rows), BF16), pltpu.SemaphoreType.DMA((2, slots))],
         LOCAL_LIMIT,
         3 * head_macs * heads_here,
         2 * block_bytes,
     )
-    parts, inputs, level_weights = lax.optimization_barrier((parts, inputs, level_weights))
+    parts, inputs, level_weights, sent_weight = lax.optimization_barrier(
+        (parts, inputs, level_weights, sent_weight)
+    )
+    other_block = swap_heads(sent_weight)
 
     low_count = low_bits * quarter_heads
     high_count = high_bits * quarter_heads
@@ -571,16 +593,17 @@
     )
     high_slots = [high] + [swap_low(high, by) for by in range(1, slots)]
 
-    other_block, second_queries, second_combined = call(
-        functools.partial(second_local_kernel, slots, head_dim),
+    operands = inputs + (level_weights, first_queries, first_combined, *low_slots)
+    first_combined, second_queries, second_combined = call(
+        functools.partial(second_local_kernel, head_dim),
         "local_levels_second",
-        (other_weight,) + inputs + (level_weights,),
-        [ANY] + [VMEM] * (len(inputs) + 1),
-        [weight_block, half, half_wide],
+        operands,
+        [VMEM] * len(operands),
+        [half_wide, half, half_wide],
         [VMEM] * 3,
-        [pltpu.SemaphoreType.DMA((slots,))],
-        LOCAL_LIMIT,
-        3 * head_macs * heads_here,
+        [],
+        SMALL_LIMIT,
+        5 * head_macs * heads_here,
         2 * block_bytes,
     )
 
@@ -596,12 +619,11 @@
             rotated_queries,
             level_weights,
             gain,
-            *low_slots[first : first + chunk],
             *high_slots[first : first + chunk],
         )
         (piece,) = call(
             functools.partial(
-                cross_kernel, first, chunk, slots, head_dim, levels, low_bits, high_bits
+                cross_kernel, first, chunk, slots, head_dim, levels, high_bits
             ),
             "cross_levels",
             operands,

time: 39.9 us -> 38.8 us (0.972)
  local copies, waits for them, and re-layouts: 2.2 us -> 0.01 us
  Pallas kernels: 12.9 us -> 14.7 us
    unnamed x8 -> x6, local copies, waits for them, and re-layouts: 2.2 us -> 0.01 us
    pallas_call x9, Pallas kernels: 12.9 us -> 14.7 us  [call(): pl.pallas_call(kernel, in_specs=[pl.BlockSpec(memory_space=space) for spa...]
    ppermute x3, starting transfers between devices: 0.66 us -> 0.14 us  [swap_heads(): return lax.ppermute(block, 'head', [(i, i ^ 1) for i in range(n_head)])]
  transfers between devices with their start and end apart: 15 -> 15, of which waited for: 7 -> 6; matrix products, arithmetic and copies ran while one was open for 0% -> 0% of each run, Pallas kernels for 21% -> 26%
where the time goes in v4:
time: 38.8 us; the launch traced here: 38.7 us
  starting transfers between devices  16.6 us (43%)
  Pallas kernels  14.7 us (38%)
  waiting for transfers between devices  7.22 us (19%)
    pallas_call x9, Pallas kernels, call(): pl.pallas_call(kernel, in_specs=[pl.BlockSpec(memory_space=space) for spa...  14.7 us
    ppermute x9, starting transfers between devices, swap_low(): return lax.ppermute(block, 'ctx', [(i, i ^ by) for i in range(n_ctx)])  10.9 us
    ppermute x3, starting transfers between devices, local(): lax.ppermute(running, 'ctx', [(i, turned(i, by)) for i in range(n_ctx)])  5.57 us
    ppermute x9, waiting for transfers between devices, swap_low(): return lax.ppermute(block, 'ctx', [(i, i ^ by) for i in range(n_ctx)])  4.82 us
    ppermute x3, waiting for transfers between devices, local(): lax.ppermute(running, 'ctx', [(i, turned(i, by)) for i in range(n_ctx)])  2.31 us
  transfers between devices with their start and end apart: 15, of which 6 were waited for; matrix products, arithmetic and copies ran while one was open for 0% of the time, Pallas kernels for 26%

profile of v4, /device:TPU:0, one launch (start us, length us, event | category | flops | bytes accessed | tf_op | source)
XLA Modules:
  0.0 38.7 jit_solution(12937152015680532151)
XLA Ops:
  0.0 3.0 %states.1 = (bf16[512,1024]{1,0:T(8,128)(2,1)S(1)}, bf16[512,1024]{1,0:T(8,128)(2,1)S(1)}, bf16[512,1024]{1,0:T(8,128)(2,1)S(1)}, f32[512,128]{1,0:T(8,128)S(1)}...) custom-call(f32[128,128]{1,0:T(8,128)} %constant.2.clone.angle_hbm, ...), custom_call_target="tpu_custom_call" | custom-call | flops 268435456 | bytes 4194304 | tf_op jit(solution)/shard_map/states/pallas_call | solution.py:450
  3.0 3.0 %collective-permute-start = (bf16[2,128,128]{2,1,0:T(8,128)(2,1)S(1)}, bf16[2,128,128]{2,1,0:T(8,128)(2,1)S(1)}, u32[]{:S(2)}, u32[]{:S(2)}) collective-permute-start(bf16[2,128,128]{2,1,0:T(8,128)(2,1)S(1)} %get-tuple-element.43), channel_id=1, source_target_pairs={{0,2},{2,0},{4,6},{6,4},{8,10},{10,8},{12,14},{14,12},{16,18},{18,... | collective-permute-start | bytes 196616 | tf_op jit(solution)/shard_map/ppermute | solution.py:486
  6.0 1.5 %collective-permute-start.1 = (bf16[2,128,128]{2,1,0:T(8,128)(2,1)S(1)}, bf16[2,128,128]{2,1,0:T(8,128)(2,1)S(1)}, u32[]{:S(2)}, u32[]{:S(2)}) collective-permute-start(bf16[2,128,128]{2,1,0:T(8,128)(2,1)S(1)} %get-tuple-element.44), channel_id=1, source_target_pairs={{0,4},{2,6},{4,0},{6,2},{8,12},{10,14},{12,8},{14,10},{16,20},{18,... | collective-permute-start | bytes 196616 | tf_op jit(solution)/shard_map/ppermute | solution.py:486
  7.5 3.5 %local_levels_first.1 = (f32[512,64]{1,0:T(8,128)S(1)}, bf16[1024,1024]{1,0:T(8,128)(2,1)S(1)}, bf16[1024,1024]{1,0:T(8,128)(2,1)S(1)}, bf16[512,512]{1,0:T(8,128)(2,1)S(1)}, f32[512,512]{1,0:T(8,128)S(1)}) custom-call(s32[1,512]{1,0:T(1,128)S(1)} %bitcast.6, f32[7,8,64]{2,1,0:T(8,128)S(1)} %bitcast.3, bf16[1024,2048]{1,0:T(8,128)(2,1)} %out_weight_hbm.1, ...), custom_call_target="tpu_custom_call" | custom-call | flops 201326592 | bytes 2097152 | tf_op jit(solution)/shard_map/local_levels_first/pallas_call | solution.py:450
  11.1 1.6 %collective-permute-done.2.refs_3_ = bf16[2,128,128]{2,1,0:T(8,128)(2,1)S(1)} collective-permute-done((bf16[2,128,128]{2,1,0:T(8,128)(2,1)S(1)}, bf16[2,128,128]{2,1,0:T(8,128)(2,1)S(1)}, u32[]{:S(2)}, u32[]{:S(2)}) %collective-permute-start.2) | collective-permute-done | bytes 65568 | tf_op jit(solution)/shard_map/ppermute | solution.py:486
  12.7 0.1 low_buckets.1
  12.8 1.6 %collective-permute-start.6 = (bf16[2,128,128]{2,1,0:T(8,128)(2,1)S(1)}, bf16[2,128,128]{2,1,0:T(8,128)(2,1)S(1)}, u32[]{:S(2)}, u32[]{:S(2)}) collective-permute-start(bf16[2,128,128]{2,1,0:T(8,128)(2,1)S(1)} %get-tuple-element.75), channel_id=1, source_target_pairs={{0,8},{2,10},{4,12},{6,14},{8,16},{10,18},{12,20},{14,22},{16,24},... | collective-permute-start | bytes 196616 | tf_op jit(solution)/shard_map/ppermute | solution.py:573
  14.4 2.6 %collective-permute-start.7 = (bf16[2,128,128]{2,1,0:T(8,128)(2,1)S(1)}, bf16[2,128,128]{2,1,0:T(8,128)(2,1)S(1)}, u32[]{:S(2)}, u32[]{:S(2)}) collective-permute-start(bf16[2,128,128]{2,1,0:T(8,128)(2,1)S(1)} %get-tuple-element.75), channel_id=1, source_target_pairs={{0,16},{2,18},{4,20},{6,22},{8,24},{10,26},{12,28},{14,30},{16,0},... | collective-permute-start | bytes 196616 | tf_op jit(solution)/shard_map/ppermute | solution.py:573
  17.0 1.3 %collective-permute-start.8 = (bf16[2,128,128]{2,1,0:T(8,128)(2,1)S(1)}, bf16[2,128,128]{2,1,0:T(8,128)(2,1)S(1)}, u32[]{:S(2)}, u32[]{:S(2)}) collective-permute-start(bf16[2,128,128]{2,1,0:T(8,128)(2,1)S(1)} %get-tuple-element.75), channel_id=1, source_target_pairs={{0,24},{2,26},{4,28},{6,30},{8,0},{10,2},{12,4},{14,6},{16,8},{18,... | collective-permute-start | bytes 196616 | tf_op jit(solution)/shard_map/ppermute | solution.py:573
  18.3 0.5 %collective-permute-start.3 = (bf16[4,128,128]{2,1,0:T(8,128)(2,1)S(1)}, bf16[4,128,128]{2,1,0:T(8,128)(2,1)S(1)}, u32[]{:S(2)}, u32[]{:S(2)}) collective-permute-start(bf16[4,128,128]{2,1,0:T(8,128)(2,1)S(1)} %get-tuple-element.68), channel_id=1, source_target_pairs={{0,2},{2,0},{4,6},{6,4},{8,10},{10,8},{12,14},{14,12},{16,18},{18,... | collective-permute-start | bytes 393224 | tf_op jit(solution)/shard_map/ppermute | solution.py:486
  18.9 0.5 %collective-permute-done.6.refs_0_ = bf16[2,128,128]{2,1,0:T(8,128)(2,1)S(1)} collective-permute-done((bf16[2,128,128]{2,1,0:T(8,128)(2,1)S(1)}, bf16[2,128,128]{2,1,0:T(8,128)(2,1)S(1)}, u32[]{:S(2)}, u32[]{:S(2)}) %collective-permute-start.6) | collective-permute-done | bytes 65568 | tf_op jit(solution)/shard_map/ppermute | solution.py:573
  19.4 0.9 %collective-permute-start.4 = (bf16[4,128,128]{2,1,0:T(8,128)(2,1)S(1)}, bf16[4,128,128]{2,1,0:T(8,128)(2,1)S(1)}, u32[]{:S(2)}, u32[]{:S(2)}) collective-permute-start(bf16[4,128,128]{2,1,0:T(8,128)(2,1)S(1)} %get-tuple-element.69), channel_id=1, source_target_pairs={{0,4},{2,6},{4,0},{6,2},{8,12},{10,14},{12,8},{14,10},{16,20},{18,... | collective-permute-start | bytes 393224 | tf_op jit(solution)/shard_map/ppermute | solution.py:486
  20.3 1.8 %collective-permute-done.7.refs_1_ = bf16[2,128,128]{2,1,0:T(8,128)(2,1)S(1)} collective-permute-done((bf16[2,128,128]{2,1,0:T(8,128)(2,1)S(1)}, bf16[2,128,128]{2,1,0:T(8,128)(2,1)S(1)}, u32[]{:S(2)}, u32[]{:S(2)}) %collective-permute-start.7) | collective-permute-done | bytes 65568 | tf_op jit(solution)/shard_map/ppermute | solution.py:573
  22.1 1.4 %collective-permute-start.5 = (bf16[4,128,128]{2,1,0:T(8,128)(2,1)S(1)}, bf16[4,128,128]{2,1,0:T(8,128)(2,1)S(1)}, u32[]{:S(2)}, u32[]{:S(2)}) collective-permute-start(bf16[4,128,128]{2,1,0:T(8,128)(2,1)S(1)} %get-tuple-element.70), channel_id=1, source_target_pairs={{0,6},{2,4},{4,2},{6,0},{8,14},{10,12},{12,10},{14,8},{16,22},{18,... | collective-permute-start | bytes 393224 | tf_op jit(solution)/shard_map/ppermute | solution.py:486
  23.5 0.7 %collective-permute-start.13 = (bf16[4,128,128]{2,1,0:T(8,128)(2,1)S(1)}, bf16[4,128,128]{2,1,0:T(8,128)(2,1)S(1)}, u32[]{:S(2)}, u32[]{:S(2)}) collective-permute-start(bf16[4,128,128]{2,1,0:T(8,128)(2,1)S(1)} %high_buckets.1.refs_0_), channel_id=1, source_target_pairs={{0,2},{2,0},{4,6},{6,4},{8,10},{10,8},{12,14},{14,12},{16,18},{18,... | collective-permute-start | bytes 393224 | tf_op jit(solution)/shard_map/ppermute | solution.py:486
  24.2 1.5 %collective-permute-start.9 = (bf16[4,128,128]{2,1,0:T(8,128)(2,1)S(1)}, bf16[4,128,128]{2,1,0:T(8,128)(2,1)S(1)}, u32[]{:S(2)}, u32[]{:S(2)}) collective-permute-start(bf16[4,128,128]{2,1,0:T(8,128)(2,1)S(1)} %high_buckets.1.refs_0_), channel_id=1, source_target_pairs={{0,4},{2,6},{4,0},{6,2},{8,12},{10,14},{12,8},{14,10},{16,20},{18,... | collective-permute-start | bytes 393224 | tf_op jit(solution)/shard_map/ppermute | solution.py:486
  25.7 1.4 %collective-permute-start.10 = (bf16[4,128,128]{2,1,0:T(8,128)(2,1)S(1)}, bf16[4,128,128]{2,1,0:T(8,128)(2,1)S(1)}, u32[]{:S(2)}, u32[]{:S(2)}) collective-permute-start(bf16[4,128,128]{2,1,0:T(8,128)(2,1)S(1)} %high_buckets.1.refs_0_), channel_id=1, source_target_pairs={{0,6},{2,4},{4,2},{6,0},{8,14},{10,12},{12,10},{14,8},{16,22},{18,... | collective-permute-start | bytes 393224 | tf_op jit(solution)/shard_map/ppermute | solution.py:486
  27.1 2.3 %collective-permute-done.5.refs_3_ = bf16[4,128,128]{2,1,0:T(8,128)(2,1)S(1)} collective-permute-done((bf16[4,128,128]{2,1,0:T(8,128)(2,1)S(1)}, bf16[4,128,128]{2,1,0:T(8,128)(2,1)S(1)}, u32[]{:S(2)}, u32[]{:S(2)}) %collective-permute-start.5) | collective-permute-done | bytes 131104 | tf_op jit(solution)/shard_map/ppermute | solution.py:486
  29.4 2.4 %local_levels_second.1 = (f32[512,512]{1,0:T(8,128)S(1)}, bf16[512,512]{1,0:T(8,128)(2,1)S(1)}, f32[512,512]{1,0:T(8,128)S(1)}) custom-call(bf16[512,1024]{1,0:T(8,128)(2,1)S(1)} %get-tuple-element.54.query_ref, bf16[512,1024]{1,0:T(8,128)(2,1)S(1)} %get-tuple-element.55.key_ref, bf16[512,1024]{1,0:T(8,128)(2,1)S(1)} %get-tuple-element.56.value_ref, ...), custom_call_target="tpu_custom_call" | custom-call | flops 335544320 | bytes 2097152 | tf_op jit(solution)/shard_map/local_levels_second/pallas_call | solution.py:450
  31.8 1.2 %cross_levels.3.own_first = bf16[512,512]{1,0:T(8,128)(2,1)S(1)} custom-call(f32[512,512]{1,0:T(8,128)S(1)} %get-tuple-element.77.combined_ref, bf16[512,512]{1,0:T(8,128)(2,1)S(1)} %get-tuple-element.61.first_query_ref.query_ref, f32[512,64]{1,0:T(8,128)S(1)} %get-tuple-element.60.weight_ref, f32[8,128]{1,0:T(8,128)S(1)} %bitcast.4, ...), custom_call_target="tpu_custom_call" | custom-call | flops 268435456 | bytes 1048576 | tf_op jit(solution)/shard_map/cross_levels/pallas_call | solution.py:450
  33.1 0.9 %collective-permute-done.10.refs_1_ = bf16[4,128,128]{2,1,0:T(8,128)(2,1)S(1)} collective-permute-done((bf16[4,128,128]{2,1,0:T(8,128)(2,1)S(1)}, bf16[4,128,128]{2,1,0:T(8,128)(2,1)S(1)}, u32[]{:S(2)}, u32[]{:S(2)}) %collective-permute-start.10) | collective-permute-done | bytes 131104 | tf_op jit(solution)/shard_map/ppermute | solution.py:486
  34.0 1.2 %cross_levels.2.own_second = bf16[512,512]{1,0:T(8,128)(2,1)S(1)} custom-call(f32[512,512]{1,0:T(8,128)S(1)} %get-tuple-element.72.combined_ref, bf16[512,512]{1,0:T(8,128)(2,1)S(1)} %get-tuple-element.73.query_ref, f32[512,64]{1,0:T(8,128)S(1)} %get-tuple-element.60.weight_ref, f32[8,128]{1,0:T(8,128)S(1)} %bitcast.5, ...), custom_call_target="tpu_custom_call" | custom-call | flops 268435456 | bytes 1048576 | tf_op jit(solution)/shard_map/cross_levels/pallas_call | solution.py:450
  35.2 1.8 %early_projection.1.part_ref = f32[512,1024]{1,0:T(8,128)S(1)} custom-call(bf16[512,512]{1,0:T(8,128)(2,1)S(1)} %cross_levels.3.own_first, bf16[512,512]{1,0:T(8,128)(2,1)S(1)} %cross_levels.2.own_second, bf16[512,512]{1,0:T(8,128)(2,1)S(1)} %collective-permute-done.14.other_first, bf16[1024,1024]{1,0:T(8,128)(2,1)S(1)} %get-tuple-element.78.own_weight, ...), custom_call_target="tpu_custom_call" | custom-call | flops 1610612736 | bytes 2097152 | tf_op jit(solution)/shard_map/early_projection/pallas_call | solution.py:450
  37.1 1.6 %late_projection.1 = bf16[512,1024]{1,0:T(8,128)(2,1)} custom-call(bf16[512,512]{1,0:T(8,128)(2,1)S(1)} %collective-permute-done.11.other_second, bf16[1024,1024]{1,0:T(8,128)(2,1)S(1)} %collective-permute-done.12.other_weight, f32[512,1024]{1,0:T(8,128)S(1)} %early_projection.1.part_ref), custom_call_target="tpu_custom_call" | custom-call | flops 536870912 | bytes 2097152 | tf_op jit(solution)/shard_map/late_projection/pallas_call | solution.py:450
  (21 shorter events, 0.3 us)
Async XLA Ops:
  0.0 7.5 %copy-start.2 = (s32[512]{0:T(512)S(1)}, s32[512]{0:T(512)}, u32[]{:S(2)}) copy-start(s32[512]{0:T(512)} %param.12) | copy-start | bytes 6148
  0.0 7.5 %copy-start = (f32[64,8,7]{0,1,2:T(8,128)S(1)}, f32[64,8,7]{0,1,2:T(8,128)}, u32[]{:S(2)}) copy-start(f32[64,8,7]{0,1,2:T(8,128)} %param.11) | copy-start | bytes 43012
  3.0 8.1 %collective-permute-start = (bf16[2,128,128]{2,1,0:T(8,128)(2,1)S(1)}, bf16[2,128,128]{2,1,0:T(8,128)(2,1)S(1)}, u32[]{:S(2)}, u32[]{:S(2)}) collective-permute-start(bf16[2,128,128]{2,1,0:T(8,128)(2,1)S(1)} %get-tuple-element.43), channel_id=1, source_target_pairs={{0,2},{2,0},{4,6},{6,4},{8,10},{10,8},{12,14},{14,12},{16,18},{18,... | collective-permute-start | bytes 196616 | tf_op jit(solution)/shard_map/ppermute | solution.py:486
  6.0 5.1 %collective-permute-start.1 = (bf16[2,128,128]{2,1,0:T(8,128)(2,1)S(1)}, bf16[2,128,128]{2,1,0:T(8,128)(2,1)S(1)}, u32[]{:S(2)}, u32[]{:S(2)}) collective-permute-start(bf16[2,128,128]{2,1,0:T(8,128)(2,1)S(1)} %get-tuple-element.44), channel_id=1, source_target_pairs={{0,4},{2,6},{4,0},{6,2},{8,12},{10,14},{12,8},{14,10},{16,20},{18,... | collective-permute-start | bytes 196616 | tf_op jit(solution)/shard_map/ppermute | solution.py:486
  7.5 5.2 %collective-permute-start.2 = (bf16[2,128,128]{2,1,0:T(8,128)(2,1)S(1)}, bf16[2,128,128]{2,1,0:T(8,128)(2,1)S(1)}, u32[]{:S(2)}, u32[]{:S(2)}) collective-permute-start(bf16[2,128,128]{2,1,0:T(8,128)(2,1)S(1)} %get-tuple-element.45), channel_id=1, source_target_pairs={{0,6},{2,4},{4,2},{6,0},{8,14},{10,12},{12,10},{14,8},{16,22},{18,... | collective-permute-start | bytes 196616 | tf_op jit(solution)/shard_map/ppermute | solution.py:486
  12.7 22.5 %collective-permute-start.12 = (bf16[1024,1024]{1,0:T(8,128)(2,1)S(1)}, bf16[1024,1024]{1,0:T(8,128)(2,1)S(1)}, u32[]{:S(2)}, u32[]{:S(2)}) collective-permute-start(bf16[1024,1024]{1,0:T(8,128)(2,1)S(1)} %get-tuple-element.76), channel_id=1, source_target_pairs={{0,1},{1,0},{2,3},{3,2},{4,5},{5,4},{6,7},{7,6},{8,9},{9,8},{10,11... | collective-permute-start | bytes 6291464 | tf_op jit(solution)/shard_map/ppermute | solution.py:483
  12.8 6.6 %collective-permute-start.6 = (bf16[2,128,128]{2,1,0:T(8,128)(2,1)S(1)}, bf16[2,128,128]{2,1,0:T(8,128)(2,1)S(1)}, u32[]{:S(2)}, u32[]{:S(2)}) collective-permute-start(bf16[2,128,128]{2,1,0:T(8,128)(2,1)S(1)} %get-tuple-element.75), channel_id=1, source_target_pairs={{0,8},{2,10},{4,12},{6,14},{8,16},{10,18},{12,20},{14,22},{16,24},... | collective-permute-start | bytes 196616 | tf_op jit(solution)/shard_map/ppermute | solution.py:573
  14.4 7.7 %collective-permute-start.7 = (bf16[2,128,128]{2,1,0:T(8,128)(2,1)S(1)}, bf16[2,128,128]{2,1,0:T(8,128)(2,1)S(1)}, u32[]{:S(2)}, u32[]{:S(2)}) collective-permute-start(bf16[2,128,128]{2,1,0:T(8,128)(2,1)S(1)} %get-tuple-element.75), channel_id=1, source_target_pairs={{0,16},{2,18},{4,20},{6,22},{8,24},{10,26},{12,28},{14,30},{16,0},... | collective-permute-start | bytes 196616 | tf_op jit(solution)/shard_map/ppermute | solution.py:573
  17.0 6.5 %collective-permute-start.8 = (bf16[2,128,128]{2,1,0:T(8,128)(2,1)S(1)}, bf16[2,128,128]{2,1,0:T(8,128)(2,1)S(1)}, u32[]{:S(2)}, u32[]{:S(2)}) collective-permute-start(bf16[2,128,128]{2,1,0:T(8,128)(2,1)S(1)} %get-tuple-element.75), channel_id=1, source_target_pairs={{0,24},{2,26},{4,28},{6,30},{8,0},{10,2},{12,4},{14,6},{16,8},{18,... | collective-permute-start | bytes 196616 | tf_op jit(solution)/shard_map/ppermute | solution.py:573
  18.3 5.9 %collective-permute-start.3 = (bf16[4,128,128]{2,1,0:T(8,128)(2,1)S(1)}, bf16[4,128,128]{2,1,0:T(8,128)(2,1)S(1)}, u32[]{:S(2)}, u32[]{:S(2)}) collective-permute-start(bf16[4,128,128]{2,1,0:T(8,128)(2,1)S(1)} %get-tuple-element.68), channel_id=1, source_target_pairs={{0,2},{2,0},{4,6},{6,4},{8,10},{10,8},{12,14},{14,12},{16,18},{18,... | collective-permute-start | bytes 393224 | tf_op jit(solution)/shard_map/ppermute | solution.py:486
  19.4 6.4 %collective-permute-start.4 = (bf16[4,128,128]{2,1,0:T(8,128)(2,1)S(1)}, bf16[4,128,128]{2,1,0:T(8,128)(2,1)S(1)}, u32[]{:S(2)}, u32[]{:S(2)}) collective-permute-start(bf16[4,128,128]{2,1,0:T(8,128)(2,1)S(1)} %get-tuple-element.69), channel_id=1, source_target_pairs={{0,4},{2,6},{4,0},{6,2},{8,12},{10,14},{12,8},{14,10},{16,20},{18,... | collective-permute-start | bytes 393224 | tf_op jit(solution)/shard_map/ppermute | solution.py:486
  22.1 7.3 %collective-permute-start.5 = (bf16[4,128,128]{2,1,0:T(8,128)(2,1)S(1)}, bf16[4,128,128]{2,1,0:T(8,128)(2,1)S(1)}, u32[]{:S(2)}, u32[]{:S(2)}) collective-permute-start(bf16[4,128,128]{2,1,0:T(8,128)(2,1)S(1)} %get-tuple-element.70), channel_id=1, source_target_pairs={{0,6},{2,4},{4,2},{6,0},{8,14},{10,12},{12,10},{14,8},{16,22},{18,... | collective-permute-start | bytes 393224 | tf_op jit(solution)/shard_map/ppermute | solution.py:486
  23.5 8.3 %collective-permute-start.13 = (bf16[4,128,128]{2,1,0:T(8,128)(2,1)S(1)}, bf16[4,128,128]{2,1,0:T(8,128)(2,1)S(1)}, u32[]{:S(2)}, u32[]{:S(2)}) collective-permute-start(bf16[4,128,128]{2,1,0:T(8,128)(2,1)S(1)} %high_buckets.1.refs_0_), channel_id=1, source_target_pairs={{0,2},{2,0},{4,6},{6,4},{8,10},{10,8},{12,14},{14,12},{16,18},{18,... | collective-permute-start | bytes 393224 | tf_op jit(solution)/shard_map/ppermute | solution.py:486
  24.2 8.9 %collective-permute-start.9 = (bf16[4,128,128]{2,1,0:T(8,128)(2,1)S(1)}, bf16[4,128,128]{2,1,0:T(8,128)(2,1)S(1)}, u32[]{:S(2)}, u32[]{:S(2)}) collective-permute-start(bf16[4,128,128]{2,1,0:T(8,128)(2,1)S(1)} %high_buckets.1.refs_0_), channel_id=1, source_target_pairs={{0,4},{2,6},{4,0},{6,2},{8,12},{10,14},{12,8},{14,10},{16,20},{18,... | collective-permute-start | bytes 393224 | tf_op jit(solution)/shard_map/ppermute | solution.py:486
  25.7 8.2 %collective-permute-start.10 = (bf16[4,128,128]{2,1,0:T(8,128)(2,1)S(1)}, bf16[4,128,128]{2,1,0:T(8,128)(2,1)S(1)}, u32[]{:S(2)}, u32[]{:S(2)}) collective-permute-start(bf16[4,128,128]{2,1,0:T(8,128)(2,1)S(1)} %high_buckets.1.refs_0_), channel_id=1, source_target_pairs={{0,6},{2,4},{4,2},{6,0},{8,14},{10,12},{12,10},{14,8},{16,22},{18,... | collective-permute-start | bytes 393224 | tf_op jit(solution)/shard_map/ppermute | solution.py:486
  29.4 2.4 %copy-start.1 = (f32[1024]{0:T(1024)S(1)}, f32[1024]{0:T(1024)}, u32[]{:S(2)}) copy-start(f32[1024]{0:T(1024)} %param.13) | copy-start | bytes 12292
  33.0 2.2 %collective-permute-start.14 = (bf16[512,512]{1,0:T(8,128)(2,1)S(1)}, bf16[512,512]{1,0:T(8,128)(2,1)S(1)}, u32[]{:S(2)}, u32[]{:S(2)}) collective-permute-start(bf16[512,512]{1,0:T(8,128)(2,1)S(1)} %cross_levels.3.own_first), channel_id=1, source_target_pairs={{0,1},{1,0},{2,3},{3,2},{4,5},{5,4},{6,7},{7,6},{8,9},{9,8},{10,11... | collective-permute-start | bytes 1572872 | tf_op jit(solution)/shard_map/ppermute | solution.py:483
  35.1 2.0 %collective-permute-start.11 = (bf16[512,512]{1,0:T(8,128)(2,1)S(1)}, bf16[512,512]{1,0:T(8,128)(2,1)S(1)}, u32[]{:S(2)}, u32[]{:S(2)}) collective-permute-start(bf16[512,512]{1,0:T(8,128)(2,1)S(1)} %cross_levels.2.own_second), channel_id=1, source_target_pairs={{0,1},{1,0},{2,3},{3,2},{4,5},{5,4},{6,7},{7,6},{8,9},{9,8},{10,11... | collective-permute-start | bytes 1572872 | tf_op jit(solution)/shard_map/ppermute | solution.py:483

commit v5 on v4

--- a/solution.py
+++ b/solution.py
@@ -91,6 +91,12 @@
                 row.append((bit, tuple(range(end - (1 << bit), end))))
         plan.append(row)
     return plan
+
+
+def head_columns(head, slots, heads, head_dim):
+    slot, spot = divmod(head, heads // slots)
+    source = quarter_of(slot, slots) * (heads // slots) + spot
+    return pl.ds(pl.multiple_of(source * head_dim, head_dim), head_dim)
 
 
 def state_kernel(
@@ -112,59 +118,50 @@
     total_outs = refs[:slots]
     key_raw, angle_ref, sems = refs[slots:]
     tok_rows, model_width = key_raw.shape
-    width = model_width // slots
-
-    def fetch(source, target, slot, sem):
-        start = pl.multiple_of(quarter_of(slot, slots) * width, width)
-        return pltpu.make_async_copy(
-            source.at[:, pl.ds(start, width)], target.at[:, pl.ds(slot * width, width)], sem
-        )
+    stretch_len = tok_rows // STRETCHES_DEV
+    heads = range(model_width // head_dim)
+    groups = bucket_groups()
+    spans = [slice(i * stretch_len, (i + 1) * stretch_len) for i in range(STRETCHES_DEV)]
 
     angles_in = pltpu.make_async_copy(angle_hbm, angle_ref, sems.at[3, 0])
     angles_in.start()
-    order = list(range(slots - 1, -1, -1))
-    copies = {}
-    for kind, (source, target) in enumerate(
-        ((key_hbm, key_raw), (value_hbm, value_out), (query_hbm, query_out))
-    ):
-        for slot in order:
-            copies[kind, slot] = fetch(source, target, slot, sems.at[kind, slot])
-    for slot in order:
-        copies[0, slot].start()
-        copies[1, slot].start()
-    for slot in range(slots):
-        copies[2, slot].start()
+    copies = [
+        [
+            pltpu.make_async_copy(source.at[rows, :], target.at[rows, :], sems.at[kind, index])
+            for index, rows in enumerate(spans)
+        ]
+        for kind, (source, target) in enumerate(
+            ((key_hbm, key_raw), (value_hbm, value_out), (query_hbm, query_out))
+        )
+    ]
+    for index in range(STRETCHES_DEV):
+        copies[0][index].start()
+        copies[1][index].start()
+    for copy in copies[2]:
+        copy.start()
     angles_in.wait()
     fill_angles(angle_ref, lax.axis_index("ctx"), n_ctx, cos_out, sin_out)
 
-    stretch_len = tok_rows // STRETCHES_DEV
-    groups = bucket_groups()
-    quarter_heads = width // head_dim
-    for slot in order:
-        copies[0, slot].wait()
-        copies[1, slot].wait()
-        heads = range(slot * quarter_heads, (slot + 1) * quarter_heads)
-        turned, states = {}, {}
+    quarter_heads = len(heads) // slots
+    states = {}
+    for index, rows in enumerate(spans):
+        copies[0][index].wait()
+        copies[1][index].wait()
+        blocks = []
         for head in heads:
-            cols = slice(head * head_dim, (head + 1) * head_dim)
-            for stretch in range(STRETCHES_DEV):
-                rows = slice(stretch * stretch_len, (stretch + 1) * stretch_len)
-                block = rotated(key_raw[rows, cols], cos_out[rows, :], sin_out[rows, :])
-                turned[head, stretch] = block
-                states[head, stretch] = dot_tn(block, value_out[rows, cols])
+            source = head_columns(head, slots, len(heads), head_dim)
+            block = rotated(key_raw[rows, source], cos_out[rows, :], sin_out[rows, :])
+            blocks.append(block)
+            states[head, index] = dot_tn(block, value_out[rows, source])
         for head in heads:
-            cols = slice(head * head_dim, (head + 1) * head_dim)
-            for stretch in range(STRETCHES_DEV):
-                rows = slice(stretch * stretch_len, (stretch + 1) * stretch_len)
-                key_out[rows, cols] = turned[head, stretch]
-            sums = {}
-            for group, members in enumerate(groups):
-                sums[members] = sum(states[head, m] for m in members)
-                bucket_out[head, group] = sums[members].astype(BF16)
-            total = sum(states[head, m] for m in range(STRETCHES_DEV))
-            total_outs[slot][head - heads[0]] = total.astype(BF16)
-    for slot in range(slots):
-        copies[2, slot].wait()
+            key_out[rows, head * head_dim : (head + 1) * head_dim] = blocks[head]
+    for head in heads:
+        for group, members in enumerate(groups):
+            bucket_out[head, group] = sum(states[head, m] for m in members).astype(BF16)
+        total = sum(states[head, m] for m in range(STRETCHES_DEV))
+        total_outs[head // quarter_heads][head % quarter_heads] = total.astype(BF16)
+    for copy in copies[2]:
+        copy.wait()
 
 
 def bucket_groups():
@@ -210,7 +207,7 @@
 
 
 def local_levels(
-    head_dim, first_head, query_ref, key_ref, value_ref, cos_ref, sin_ref, bucket_ref,
+    slots, head_dim, first_head, query_ref, key_ref, value_ref, cos_ref, sin_ref, bucket_ref,
     weight_ref, query_out, combined_out, low_refs=()
 ):
     tok_rows, width = query_out.shape
@@ -228,9 +225,10 @@
         head = first_head + spot
         cols = slice(head * head_dim, (head + 1) * head_dim)
         outs = slice(spot * head_dim, (spot + 1) * head_dim)
+        source = head_columns(head, slots, bucket_ref.shape[0], head_dim)
         weights = weight_ref[:, head * stride : head * stride + len(plan)]
         turned = [
-            rotated(query_ref[rows, cols], cos_ref[rows, :], sin_ref[rows, :]) for rows in spans
+            rotated(query_ref[rows, source], cos_ref[rows, :], sin_ref[rows, :]) for rows in spans
         ]
         scores = [dot_nt(turned[i], key_ref[rows, cols]) for i, rows in enumerate(spans)]
         reads = [
@@ -241,7 +239,7 @@
             for i in range(STRETCHES_DEV)
         ]
         scores = [jnp.where(causal, block, 0.0).astype(BF16) for block in scores]
-        totals = [dot_nn(scores[i], value_ref[rows, cols]) for i, rows in enumerate(spans)]
+        totals = [dot_nn(scores[i], value_ref[rows, source]) for i, rows in enumerate(spans)]
         for i, rows in enumerate(spans):
             totals[i] = weights[rows, 0:1] * totals[i]
             for bit, read in reads[i]:
@@ -299,7 +297,7 @@
     parts = exact_parts(jnp.concatenate(tables, axis=0))
     weight_out[...] = dot_nn(parts, one_hot_ref[...]).T
     local_levels(
-        head_dim, 0, query_ref, key_ref, value_ref, cos_ref, sin_ref, bucket_ref,
+        slots, head_dim, 0, query_ref, key_ref, value_ref, cos_ref, sin_ref, bucket_ref,
         weight_out, query_out, combined_out
     )
     for copy in copies:
@@ -344,7 +342,7 @@
             first_query_ref[:, cols], head, weight_ref, heads, low_refs
         )
     local_levels(
-        head_dim, heads // 2, query_ref, key_ref, value_ref, cos_ref, sin_ref, bucket_ref,
+        len(low_refs), head_dim, heads // 2, query_ref, key_ref, value_ref, cos_ref, sin_ref, bucket_ref,
         weight_ref, query_out, combined_out, low_refs
     )
 
@@ -434,12 +432,12 @@
 def late_kernel(tile, other_second, other_weight, part_ref, out_hbm, out_ref, sems):
     depth = other_second.shape[1]
     copies = []
-    for index, start in enumerate(range(0, out_ref.shape[1], tile)):
-        cols = slice(start, start + tile)
-        total = part_ref[:, cols] + dot_nn(other_second[...], other_weight[depth:, cols])
-        out_ref[:, cols] = total.astype(BF16)
+    for index, start in enumerate(range(0, out_ref.shape[0], tile)):
+        rows = slice(start, start + tile)
+        total = part_ref[rows, :] + dot_nn(other_second[rows, :], other_weight[depth:, :])
+        out_ref[rows, :] = total.astype(BF16)
         copies.append(
-            pltpu.make_async_copy(out_ref.at[:, cols], out_hbm.at[:, cols], sems.at[index])
+            pltpu.make_async_copy(out_ref.at[rows, :], out_hbm.at[rows, :], sems.at[index])
         )
         copies[-1].start()
     for copy in copies:
@@ -514,7 +512,7 @@
         ]
         + [share()] * slots,
         [VMEM] * (6 + slots),
-        [block, VMEM(angles.shape, F32), pltpu.SemaphoreType.DMA((4, slots))],
+        [block, VMEM(angles.shape, F32), pltpu.SemaphoreType.DMA((4, STRETCHES_DEV))],
         FETCH_LIMIT,
         4 * head_macs * heads_here,
         4 * block_bytes,
@@ -591,7 +589,8 @@
         0,
         block_bytes,
     )
-    high_slots = [high] + [swap_low(high, by) for by in range(1, slots)]
+    high_slots = [swap_low(high, by) for by in range(slots - 1, 0, -1)]
+    high_slots = [high] + high_slots[::-1]
 
     operands = inputs + (level_weights, first_queries, first_combined, *low_slots)
     first_combined, second_queries, second_combined = call(
@@ -652,13 +651,13 @@
         2 * block_bytes,
     )
     (mixed_out,) = call(
-        functools.partial(late_kernel, tile),
+        functools.partial(late_kernel, tok_rows // STRETCHES_DEV),
         "late_projection",
         (other_hidden[1], other_block, part),
         [VMEM] * 3,
         [jax.ShapeDtypeStruct((tok_rows, out_cols), BF16)],
         [ANY],
-        [VMEM((tok_rows, out_cols), BF16), pltpu.SemaphoreType.DMA((out_cols // tile,))],
+        [VMEM((tok_rows, out_cols), BF16), pltpu.SemaphoreType.DMA((STRETCHES_DEV,))],
         SMALL_LIMIT,
         tok_rows * model_width * out_cols,
         2 * block_bytes,

time: 38.8 us -> 38.6 us (level)
  transfers between devices with their start and end apart: 15 -> 15, of which waited for: 6 -> 6; matrix products, arithmetic and copies ran while one was open for 0% -> 0% of each run, Pallas kernels for 26% -> 27%
where the time goes in v5:
time: 38.6 us; the launch traced here: 38.5 us
  starting transfers between devices  16.7 us (43%)
  Pallas kernels  14.6 us (38%)
  waiting for transfers between devices  7.06 us (18%)
    pallas_call x9, Pallas kernels, call(): pl.pallas_call(kernel, in_specs=[pl.BlockSpec(memory_space=space) for spa...  14.6 us
    ppermute x9, starting transfers between devices, swap_low(): return lax.ppermute(block, 'ctx', [(i, i ^ by) for i in range(n_ctx)])  11 us
    ppermute x3, starting transfers between devices, local(): lax.ppermute(running, 'ctx', [(i, turned(i, by)) for i in range(n_ctx)])  5.57 us
    ppermute x9, waiting for transfers between devices, swap_low(): return lax.ppermute(block, 'ctx', [(i, i ^ by) for i in range(n_ctx)])  4.7 us
    ppermute x3, waiting for transfers between devices, local(): lax.ppermute(running, 'ctx', [(i, turned(i, by)) for i in range(n_ctx)])  2.27 us
  transfers between devices with their start and end apart: 15, of which 6 were waited for; matrix products, arithmetic and copies ran while one was open for 0% of the time, Pallas kernels for 27%

profile of v5, /device:TPU:0, one launch (start us, length us, event | category | flops | bytes accessed | tf_op | source)
XLA Modules:
  0.0 38.5 jit_solution(18412666231400962446)
XLA Ops:
  0.0 2.9 %states.1 = (bf16[512,1024]{1,0:T(8,128)(2,1)S(1)}, bf16[512,1024]{1,0:T(8,128)(2,1)S(1)}, bf16[512,1024]{1,0:T(8,128)(2,1)S(1)}, f32[512,128]{1,0:T(8,128)S(1)}...) custom-call(f32[128,128]{1,0:T(8,128)} %constant.2.clone.angle_hbm, ...), custom_call_target="tpu_custom_call" | custom-call | flops 268435456 | bytes 4194304 | tf_op jit(solution)/shard_map/states/pallas_call | solution.py:448
  2.9 3.0 %collective-permute-start = (bf16[2,128,128]{2,1,0:T(8,128)(2,1)S(1)}, bf16[2,128,128]{2,1,0:T(8,128)(2,1)S(1)}, u32[]{:S(2)}, u32[]{:S(2)}) collective-permute-start(bf16[2,128,128]{2,1,0:T(8,128)(2,1)S(1)} %get-tuple-element.43), channel_id=1, source_target_pairs={{0,2},{2,0},{4,6},{6,4},{8,10},{10,8},{12,14},{14,12},{16,18},{18,... | collective-permute-start | bytes 196616 | tf_op jit(solution)/shard_map/ppermute | solution.py:484
  5.9 1.5 %collective-permute-start.1 = (bf16[2,128,128]{2,1,0:T(8,128)(2,1)S(1)}, bf16[2,128,128]{2,1,0:T(8,128)(2,1)S(1)}, u32[]{:S(2)}, u32[]{:S(2)}) collective-permute-start(bf16[2,128,128]{2,1,0:T(8,128)(2,1)S(1)} %get-tuple-element.44), channel_id=1, source_target_pairs={{0,4},{2,6},{4,0},{6,2},{8,12},{10,14},{12,8},{14,10},{16,20},{18,... | collective-permute-start | bytes 196616 | tf_op jit(solution)/shard_map/ppermute | solution.py:484
  7.4 3.5 %local_levels_first.1 = (f32[512,64]{1,0:T(8,128)S(1)}, bf16[1024,1024]{1,0:T(8,128)(2,1)S(1)}, bf16[1024,1024]{1,0:T(8,128)(2,1)S(1)}, bf16[512,512]{1,0:T(8,128)(2,1)S(1)}, f32[512,512]{1,0:T(8,128)S(1)}) custom-call(s32[1,512]{1,0:T(1,128)S(1)} %bitcast.6, f32[7,8,64]{2,1,0:T(8,128)S(1)} %bitcast.3, bf16[1024,2048]{1,0:T(8,128)(2,1)} %out_weight_hbm.1, ...), custom_call_target="tpu_custom_call" | custom-call | flops 201326592 | bytes 2097152 | tf_op jit(solution)/shard_map/local_levels_first/pallas_call | solution.py:448
  11.0 1.6 %collective-permute-done.2.refs_3_ = bf16[2,128,128]{2,1,0:T(8,128)(2,1)S(1)} collective-permute-done((bf16[2,128,128]{2,1,0:T(8,128)(2,1)S(1)}, bf16[2,128,128]{2,1,0:T(8,128)(2,1)S(1)}, u32[]{:S(2)}, u32[]{:S(2)}) %collective-permute-start.2) | collective-permute-done | bytes 65568 | tf_op jit(solution)/shard_map/ppermute | solution.py:484
  12.6 0.1 low_buckets.1
  12.7 1.6 %collective-permute-start.6 = (bf16[2,128,128]{2,1,0:T(8,128)(2,1)S(1)}, bf16[2,128,128]{2,1,0:T(8,128)(2,1)S(1)}, u32[]{:S(2)}, u32[]{:S(2)}) collective-permute-start(bf16[2,128,128]{2,1,0:T(8,128)(2,1)S(1)} %get-tuple-element.75), channel_id=1, source_target_pairs={{0,8},{2,10},{4,12},{6,14},{8,16},{10,18},{12,20},{14,22},{16,24},... | collective-permute-start | bytes 196616 | tf_op jit(solution)/shard_map/ppermute | solution.py:571
  14.3 2.6 %collective-permute-start.7 = (bf16[2,128,128]{2,1,0:T(8,128)(2,1)S(1)}, bf16[2,128,128]{2,1,0:T(8,128)(2,1)S(1)}, u32[]{:S(2)}, u32[]{:S(2)}) collective-permute-start(bf16[2,128,128]{2,1,0:T(8,128)(2,1)S(1)} %get-tuple-element.75), channel_id=1, source_target_pairs={{0,16},{2,18},{4,20},{6,22},{8,24},{10,26},{12,28},{14,30},{16,0},... | collective-permute-start | bytes 196616 | tf_op jit(solution)/shard_map/ppermute | solution.py:571
  16.9 1.3 %collective-permute-start.8 = (bf16[2,128,128]{2,1,0:T(8,128)(2,1)S(1)}, bf16[2,128,128]{2,1,0:T(8,128)(2,1)S(1)}, u32[]{:S(2)}, u32[]{:S(2)}) collective-permute-start(bf16[2,128,128]{2,1,0:T(8,128)(2,1)S(1)} %get-tuple-element.75), channel_id=1, source_target_pairs={{0,24},{2,26},{4,28},{6,30},{8,0},{10,2},{12,4},{14,6},{16,8},{18,... | collective-permute-start | bytes 196616 | tf_op jit(solution)/shard_map/ppermute | solution.py:571
  18.2 0.5 %collective-permute-start.3 = (bf16[4,128,128]{2,1,0:T(8,128)(2,1)S(1)}, bf16[4,128,128]{2,1,0:T(8,128)(2,1)S(1)}, u32[]{:S(2)}, u32[]{:S(2)}) collective-permute-start(bf16[4,128,128]{2,1,0:T(8,128)(2,1)S(1)} %get-tuple-element.68), channel_id=1, source_target_pairs={{0,2},{2,0},{4,6},{6,4},{8,10},{10,8},{12,14},{14,12},{16,18},{18,... | collective-permute-start | bytes 393224 | tf_op jit(solution)/shard_map/ppermute | solution.py:484
  18.8 0.5 %collective-permute-done.6.refs_0_ = bf16[2,128,128]{2,1,0:T(8,128)(2,1)S(1)} collective-permute-done((bf16[2,128,128]{2,1,0:T(8,128)(2,1)S(1)}, bf16[2,128,128]{2,1,0:T(8,128)(2,1)S(1)}, u32[]{:S(2)}, u32[]{:S(2)}) %collective-permute-start.6) | collective-permute-done | bytes 65568 | tf_op jit(solution)/shard_map/ppermute | solution.py:571
  19.3 1.0 %collective-permute-start.4 = (bf16[4,128,128]{2,1,0:T(8,128)(2,1)S(1)}, bf16[4,128,128]{2,1,0:T(8,128)(2,1)S(1)}, u32[]{:S(2)}, u32[]{:S(2)}) collective-permute-start(bf16[4,128,128]{2,1,0:T(8,128)(2,1)S(1)} %get-tuple-element.69), channel_id=1, source_target_pairs={{0,4},{2,6},{4,0},{6,2},{8,12},{10,14},{12,8},{14,10},{16,20},{18,... | collective-permute-start | bytes 393224 | tf_op jit(solution)/shard_map/ppermute | solution.py:484
  20.2 1.8 %collective-permute-done.7.refs_1_ = bf16[2,128,128]{2,1,0:T(8,128)(2,1)S(1)} collective-permute-done((bf16[2,128,128]{2,1,0:T(8,128)(2,1)S(1)}, bf16[2,128,128]{2,1,0:T(8,128)(2,1)S(1)}, u32[]{:S(2)}, u32[]{:S(2)}) %collective-permute-start.7) | collective-permute-done | bytes 65568 | tf_op jit(solution)/shard_map/ppermute | solution.py:571
  22.0 1.4 %collective-permute-start.5 = (bf16[4,128,128]{2,1,0:T(8,128)(2,1)S(1)}, bf16[4,128,128]{2,1,0:T(8,128)(2,1)S(1)}, u32[]{:S(2)}, u32[]{:S(2)}) collective-permute-start(bf16[4,128,128]{2,1,0:T(8,128)(2,1)S(1)} %get-tuple-element.70), channel_id=1, source_target_pairs={{0,6},{2,4},{4,2},{6,0},{8,14},{10,12},{12,10},{14,8},{16,22},{18,... | collective-permute-start | bytes 393224 | tf_op jit(solution)/shard_map/ppermute | solution.py:484
  23.4 0.6 %collective-permute-start.13 = (bf16[4,128,128]{2,1,0:T(8,128)(2,1)S(1)}, bf16[4,128,128]{2,1,0:T(8,128)(2,1)S(1)}, u32[]{:S(2)}, u32[]{:S(2)}) collective-permute-start(bf16[4,128,128]{2,1,0:T(8,128)(2,1)S(1)} %high_buckets.1.refs_0_), channel_id=1, source_target_pairs={{0,2},{2,0},{4,6},{6,4},{8,10},{10,8},{12,14},{14,12},{16,18},{18,... | collective-permute-start | bytes 393224 | tf_op jit(solution)/shard_map/ppermute | solution.py:484
  24.1 1.5 %collective-permute-start.9 = (bf16[4,128,128]{2,1,0:T(8,128)(2,1)S(1)}, bf16[4,128,128]{2,1,0:T(8,128)(2,1)S(1)}, u32[]{:S(2)}, u32[]{:S(2)}) collective-permute-start(bf16[4,128,128]{2,1,0:T(8,128)(2,1)S(1)} %high_buckets.1.refs_0_), channel_id=1, source_target_pairs={{0,4},{2,6},{4,0},{6,2},{8,12},{10,14},{12,8},{14,10},{16,20},{18,... | collective-permute-start | bytes 393224 | tf_op jit(solution)/shard_map/ppermute | solution.py:484
  25.6 1.4 %collective-permute-start.10 = (bf16[4,128,128]{2,1,0:T(8,128)(2,1)S(1)}, bf16[4,128,128]{2,1,0:T(8,128)(2,1)S(1)}, u32[]{:S(2)}, u32[]{:S(2)}) collective-permute-start(bf16[4,128,128]{2,1,0:T(8,128)(2,1)S(1)} %high_buckets.1.refs_0_), channel_id=1, source_target_pairs={{0,6},{2,4},{4,2},{6,0},{8,14},{10,12},{12,10},{14,8},{16,22},{18,... | collective-permute-start | bytes 393224 | tf_op jit(solution)/shard_map/ppermute | solution.py:484
  27.0 2.3 %collective-permute-done.5.refs_3_ = bf16[4,128,128]{2,1,0:T(8,128)(2,1)S(1)} collective-permute-done((bf16[4,128,128]{2,1,0:T(8,128)(2,1)S(1)}, bf16[4,128,128]{2,1,0:T(8,128)(2,1)S(1)}, u32[]{:S(2)}, u32[]{:S(2)}) %collective-permute-start.5) | collective-permute-done | bytes 131104 | tf_op jit(solution)/shard_map/ppermute | solution.py:484
  29.3 2.5 %local_levels_second.1 = (f32[512,512]{1,0:T(8,128)S(1)}, bf16[512,512]{1,0:T(8,128)(2,1)S(1)}, f32[512,512]{1,0:T(8,128)S(1)}) custom-call(bf16[512,1024]{1,0:T(8,128)(2,1)S(1)} %get-tuple-element.54.query_ref, bf16[512,1024]{1,0:T(8,128)(2,1)S(1)} %get-tuple-element.55.key_ref, bf16[512,1024]{1,0:T(8,128)(2,1)S(1)} %get-tuple-element.56.value_ref, ...), custom_call_target="tpu_custom_call" | custom-call | flops 335544320 | bytes 2097152 | tf_op jit(solution)/shard_map/local_levels_second/pallas_call | solution.py:448
  31.8 1.2 %cross_levels.3.own_first = bf16[512,512]{1,0:T(8,128)(2,1)S(1)} custom-call(f32[512,512]{1,0:T(8,128)S(1)} %get-tuple-element.77.combined_ref, bf16[512,512]{1,0:T(8,128)(2,1)S(1)} %get-tuple-element.61.first_query_ref.query_ref, f32[512,64]{1,0:T(8,128)S(1)} %get-tuple-element.60.weight_ref, f32[8,128]{1,0:T(8,128)S(1)} %bitcast.4, ...), custom_call_target="tpu_custom_call" | custom-call | flops 268435456 | bytes 1048576 | tf_op jit(solution)/shard_map/cross_levels/pallas_call | solution.py:448
  33.0 0.8 %collective-permute-done.10.refs_1_ = bf16[4,128,128]{2,1,0:T(8,128)(2,1)S(1)} collective-permute-done((bf16[4,128,128]{2,1,0:T(8,128)(2,1)S(1)}, bf16[4,128,128]{2,1,0:T(8,128)(2,1)S(1)}, u32[]{:S(2)}, u32[]{:S(2)}) %collective-permute-start.10) | collective-permute-done | bytes 131104 | tf_op jit(solution)/shard_map/ppermute | solution.py:484
  33.9 1.2 %cross_levels.2.own_second = bf16[512,512]{1,0:T(8,128)(2,1)S(1)} custom-call(f32[512,512]{1,0:T(8,128)S(1)} %get-tuple-element.72.combined_ref, bf16[512,512]{1,0:T(8,128)(2,1)S(1)} %get-tuple-element.73.query_ref, f32[512,64]{1,0:T(8,128)S(1)} %get-tuple-element.60.weight_ref, f32[8,128]{1,0:T(8,128)S(1)} %bitcast.5, ...), custom_call_target="tpu_custom_call" | custom-call | flops 268435456 | bytes 1048576 | tf_op jit(solution)/shard_map/cross_levels/pallas_call | solution.py:448
  35.1 1.8 %early_projection.1.part_ref = f32[512,1024]{1,0:T(8,128)S(1)} custom-call(bf16[512,512]{1,0:T(8,128)(2,1)S(1)} %cross_levels.3.own_first, bf16[512,512]{1,0:T(8,128)(2,1)S(1)} %cross_levels.2.own_second, bf16[512,512]{1,0:T(8,128)(2,1)S(1)} %collective-permute-done.14.other_first, bf16[1024,1024]{1,0:T(8,128)(2,1)S(1)} %get-tuple-element.78.own_weight, ...), custom_call_target="tpu_custom_call" | custom-call | flops 1610612736 | bytes 2097152 | tf_op jit(solution)/shard_map/early_projection/pallas_call | solution.py:448
  37.0 1.5 %late_projection.1 = bf16[512,1024]{1,0:T(8,128)(2,1)} custom-call(bf16[512,512]{1,0:T(8,128)(2,1)S(1)} %collective-permute-done.11.other_second, bf16[1024,1024]{1,0:T(8,128)(2,1)S(1)} %collective-permute-done.12.other_weight, f32[512,1024]{1,0:T(8,128)S(1)} %early_projection.1.part_ref), custom_call_target="tpu_custom_call" | custom-call | flops 536870912 | bytes 2097152 | tf_op jit(solution)/shard_map/late_projection/pallas_call | solution.py:448
  (21 shorter events, 0.3 us)
Async XLA Ops:
  0.0 7.4 %copy-start.2 = (s32[512]{0:T(512)S(1)}, s32[512]{0:T(512)}, u32[]{:S(2)}) copy-start(s32[512]{0:T(512)} %param.12) | copy-start | bytes 6148
  0.0 7.4 %copy-start = (f32[64,8,7]{0,1,2:T(8,128)S(1)}, f32[64,8,7]{0,1,2:T(8,128)}, u32[]{:S(2)}) copy-start(f32[64,8,7]{0,1,2:T(8,128)} %param.11) | copy-start | bytes 43012
  2.9 8.1 %collective-permute-start = (bf16[2,128,128]{2,1,0:T(8,128)(2,1)S(1)}, bf16[2,128,128]{2,1,0:T(8,128)(2,1)S(1)}, u32[]{:S(2)}, u32[]{:S(2)}) collective-permute-start(bf16[2,128,128]{2,1,0:T(8,128)(2,1)S(1)} %get-tuple-element.43), channel_id=1, source_target_pairs={{0,2},{2,0},{4,6},{6,4},{8,10},{10,8},{12,14},{14,12},{16,18},{18,... | collective-permute-start | bytes 196616 | tf_op jit(solution)/shard_map/ppermute | solution.py:484
  5.9 5.1 %collective-permute-start.1 = (bf16[2,128,128]{2,1,0:T(8,128)(2,1)S(1)}, bf16[2,128,128]{2,1,0:T(8,128)(2,1)S(1)}, u32[]{:S(2)}, u32[]{:S(2)}) collective-permute-start(bf16[2,128,128]{2,1,0:T(8,128)(2,1)S(1)} %get-tuple-element.44), channel_id=1, source_target_pairs={{0,4},{2,6},{4,0},{6,2},{8,12},{10,14},{12,8},{14,10},{16,20},{18,... | collective-permute-start | bytes 196616 | tf_op jit(solution)/shard_map/ppermute | solution.py:484
  7.4 5.2 %collective-permute-start.2 = (bf16[2,128,128]{2,1,0:T(8,128)(2,1)S(1)}, bf16[2,128,128]{2,1,0:T(8,128)(2,1)S(1)}, u32[]{:S(2)}, u32[]{:S(2)}) collective-permute-start(bf16[2,128,128]{2,1,0:T(8,128)(2,1)S(1)} %get-tuple-element.45), channel_id=1, source_target_pairs={{0,6},{2,4},{4,2},{6,0},{8,14},{10,12},{12,10},{14,8},{16,22},{18,... | collective-permute-start | bytes 196616 | tf_op jit(solution)/shard_map/ppermute | solution.py:484
  12.6 22.5 %collective-permute-start.12 = (bf16[1024,1024]{1,0:T(8,128)(2,1)S(1)}, bf16[1024,1024]{1,0:T(8,128)(2,1)S(1)}, u32[]{:S(2)}, u32[]{:S(2)}) collective-permute-start(bf16[1024,1024]{1,0:T(8,128)(2,1)S(1)} %get-tuple-element.76), channel_id=1, source_target_pairs={{0,1},{1,0},{2,3},{3,2},{4,5},{5,4},{6,7},{7,6},{8,9},{9,8},{10,11... | collective-permute-start | bytes 6291464 | tf_op jit(solution)/shard_map/ppermute | solution.py:481
  12.7 6.6 %collective-permute-start.6 = (bf16[2,128,128]{2,1,0:T(8,128)(2,1)S(1)}, bf16[2,128,128]{2,1,0:T(8,128)(2,1)S(1)}, u32[]{:S(2)}, u32[]{:S(2)}) collective-permute-start(bf16[2,128,128]{2,1,0:T(8,128)(2,1)S(1)} %get-tuple-element.75), channel_id=1, source_target_pairs={{0,8},{2,10},{4,12},{6,14},{8,16},{10,18},{12,20},{14,22},{16,24},... | collective-permute-start | bytes 196616 | tf_op jit(solution)/shard_map/ppermute | solution.py:571
  14.3 7.7 %collective-permute-start.7 = (bf16[2,128,128]{2,1,0:T(8,128)(2,1)S(1)}, bf16[2,128,128]{2,1,0:T(8,128)(2,1)S(1)}, u32[]{:S(2)}, u32[]{:S(2)}) collective-permute-start(bf16[2,128,128]{2,1,0:T(8,128)(2,1)S(1)} %get-tuple-element.75), channel_id=1, source_target_pairs={{0,16},{2,18},{4,20},{6,22},{8,24},{10,26},{12,28},{14,30},{16,0},... | collective-permute-start | bytes 196616 | tf_op jit(solution)/shard_map/ppermute | solution.py:571
  16.9 6.5 %collective-permute-start.8 = (bf16[2,128,128]{2,1,0:T(8,128)(2,1)S(1)}, bf16[2,128,128]{2,1,0:T(8,128)(2,1)S(1)}, u32[]{:S(2)}, u32[]{:S(2)}) collective-permute-start(bf16[2,128,128]{2,1,0:T(8,128)(2,1)S(1)} %get-tuple-element.75), channel_id=1, source_target_pairs={{0,24},{2,26},{4,28},{6,30},{8,0},{10,2},{12,4},{14,6},{16,8},{18,... | collective-permute-start | bytes 196616 | tf_op jit(solution)/shard_map/ppermute | solution.py:571
  18.2 5.9 %collective-permute-start.3 = (bf16[4,128,128]{2,1,0:T(8,128)(2,1)S(1)}, bf16[4,128,128]{2,1,0:T(8,128)(2,1)S(1)}, u32[]{:S(2)}, u32[]{:S(2)}) collective-permute-start(bf16[4,128,128]{2,1,0:T(8,128)(2,1)S(1)} %get-tuple-element.68), channel_id=1, source_target_pairs={{0,2},{2,0},{4,6},{6,4},{8,10},{10,8},{12,14},{14,12},{16,18},{18,... | collective-permute-start | bytes 393224 | tf_op jit(solution)/shard_map/ppermute | solution.py:484
  19.3 6.4 %collective-permute-start.4 = (bf16[4,128,128]{2,1,0:T(8,128)(2,1)S(1)}, bf16[4,128,128]{2,1,0:T(8,128)(2,1)S(1)}, u32[]{:S(2)}, u32[]{:S(2)}) collective-permute-start(bf16[4,128,128]{2,1,0:T(8,128)(2,1)S(1)} %get-tuple-element.69), channel_id=1, source_target_pairs={{0,4},{2,6},{4,0},{6,2},{8,12},{10,14},{12,8},{14,10},{16,20},{18,... | collective-permute-start | bytes 393224 | tf_op jit(solution)/shard_map/ppermute | solution.py:484
  22.0 7.3 %collective-permute-start.5 = (bf16[4,128,128]{2,1,0:T(8,128)(2,1)S(1)}, bf16[4,128,128]{2,1,0:T(8,128)(2,1)S(1)}, u32[]{:S(2)}, u32[]{:S(2)}) collective-permute-start(bf16[4,128,128]{2,1,0:T(8,128)(2,1)S(1)} %get-tuple-element.70), channel_id=1, source_target_pairs={{0,6},{2,4},{4,2},{6,0},{8,14},{10,12},{12,10},{14,8},{16,22},{18,... | collective-permute-start | bytes 393224 | tf_op jit(solution)/shard_map/ppermute | solution.py:484
  23.4 8.3 %collective-permute-start.13 = (bf16[4,128,128]{2,1,0:T(8,128)(2,1)S(1)}, bf16[4,128,128]{2,1,0:T(8,128)(2,1)S(1)}, u32[]{:S(2)}, u32[]{:S(2)}) collective-permute-start(bf16[4,128,128]{2,1,0:T(8,128)(2,1)S(1)} %high_buckets.1.refs_0_), channel_id=1, source_target_pairs={{0,2},{2,0},{4,6},{6,4},{8,10},{10,8},{12,14},{14,12},{16,18},{18,... | collective-permute-start | bytes 393224 | tf_op jit(solution)/shard_map/ppermute | solution.py:484
  24.1 8.9 %collective-permute-start.9 = (bf16[4,128,128]{2,1,0:T(8,128)(2,1)S(1)}, bf16[4,128,128]{2,1,0:T(8,128)(2,1)S(1)}, u32[]{:S(2)}, u32[]{:S(2)}) collective-permute-start(bf16[4,128,128]{2,1,0:T(8,128)(2,1)S(1)} %high_buckets.1.refs_0_), channel_id=1, source_target_pairs={{0,4},{2,6},{4,0},{6,2},{8,12},{10,14},{12,8},{14,10},{16,20},{18,... | collective-permute-start | bytes 393224 | tf_op jit(solution)/shard_map/ppermute | solution.py:484
  25.6 8.2 %collective-permute-start.10 = (bf16[4,128,128]{2,1,0:T(8,128)(2,1)S(1)}, bf16[4,128,128]{2,1,0:T(8,128)(2,1)S(1)}, u32[]{:S(2)}, u32[]{:S(2)}) collective-permute-start(bf16[4,128,128]{2,1,0:T(8,128)(2,1)S(1)} %high_buckets.1.refs_0_), channel_id=1, source_target_pairs={{0,6},{2,4},{4,2},{6,0},{8,14},{10,12},{12,10},{14,8},{16,22},{18,... | collective-permute-start | bytes 393224 | tf_op jit(solution)/shard_map/ppermute | solution.py:484
  29.3 2.5 %copy-start.1 = (f32[1024]{0:T(1024)S(1)}, f32[1024]{0:T(1024)}, u32[]{:S(2)}) copy-start(f32[1024]{0:T(1024)} %param.13) | copy-start | bytes 12292
  32.9 2.2 %collective-permute-start.14 = (bf16[512,512]{1,0:T(8,128)(2,1)S(1)}, bf16[512,512]{1,0:T(8,128)(2,1)S(1)}, u32[]{:S(2)}, u32[]{:S(2)}) collective-permute-start(bf16[512,512]{1,0:T(8,128)(2,1)S(1)} %cross_levels.3.own_first), channel_id=1, source_target_pairs={{0,1},{1,0},{2,3},{3,2},{4,5},{5,4},{6,7},{7,6},{8,9},{9,8},{10,11... | collective-permute-start | bytes 1572872 | tf_op jit(solution)/shard_map/ppermute | solution.py:481
  35.0 2.0 %collective-permute-start.11 = (bf16[512,512]{1,0:T(8,128)(2,1)S(1)}, bf16[512,512]{1,0:T(8,128)(2,1)S(1)}, u32[]{:S(2)}, u32[]{:S(2)}) collective-permute-start(bf16[512,512]{1,0:T(8,128)(2,1)S(1)} %cross_levels.2.own_second), channel_id=1, source_target_pairs={{0,1},{1,0},{2,3},{3,2},{4,5},{5,4},{6,7},{7,6},{8,9},{9,8},{10,11... | collective-permute-start | bytes 1572872 | tf_op jit(solution)/shard_map/ppermute | solution.py:481
